TPU v7x, 128 devices: a whole 4x4x4 slice. The times are simulated.
128 devices in a mesh: ctx: 16 (over y, z), tp: 4 (over x), dp: 2 (over core).
Axes of the slice: x: 4, y: 4, z: 4, core: 2. Of those that a mesh axis runs over, the one named last changes fastest.
Arguments:
- queries: bfloat16 [2, 2048, 2048], P('dp', 'ctx', 'tp'), may hold values from -96 to 96
- key_rows: bfloat16 [2, 2048, 2048], P('dp', 'ctx', 'tp'), may hold values from -32 to 32
- value_rows: bfloat16 [2, 2048, 4096], P('dp', 'ctx', 'tp'), may hold values from -6 to 6
- log_decay: float32 [2, 32, 2048], P('dp', 'tp', 'ctx'), may hold values from -0.77 to 0
- write_rate: float32 [2, 32, 2048], P('dp', 'tp', 'ctx'), may hold values from 0.05 to 0.95
- initial_state: float32 [2, 32, 128, 128], P('dp', 'tp'), may hold values from -6 to 6
- final_state_grad: float32 [2, 32, 128, 128], P('dp', 'tp'), may hold values from -6 to 6
- output_matrix: bfloat16 [2048, 4096], P('dp', 'tp'), may hold values from -0.09375 to 0.09375
- output_grad: bfloat16 [2, 2048, 2048], P('dp', 'ctx', 'tp'), may hold values from -6 to 6
Outputs:
- query_grad: bfloat16 [2, 2048, 2048], P('dp', 'ctx', 'tp')
- key_grad: bfloat16 [2, 2048, 2048], P('dp', 'ctx', 'tp')
- value_grad: bfloat16 [2, 2048, 4096], P('dp', 'ctx', 'tp')
- decay_grad: float32 [2, 32, 2048], P('dp', 'tp', 'ctx')
- rate_grad: float32 [2, 32, 2048], P('dp', 'tp', 'ctx')
- weight_grad: float32 [2048, 4096], P('dp', 'tp')
All inputs are finite; a program needn't handle non-finite values.
Results may differ from a plain program's by a relative error of at most 0.02.
Values may be sent and summed in bfloat16 or wider, within the bound.
No kernel may reach another device: no remote copies, remote signals or barrier semaphores. Data moves between devices by JAX's collectives and lax.ppermute only.
A program may use at most 128 MiB of HBM per device.

v0:
```python
import functools

import jax
import jax.numpy as jnp
from jax import lax
from jax.experimental import pallas as pl
from jax.experimental.pallas import tpu as pltpu
from jax.sharding import PartitionSpec as P

DK = 128
DV = 128
BLOCK = 128
HALF = DV // 2
F32 = jnp.float32
BF16 = jnp.bfloat16
QSCALE = DK ** (-0.5)

NN = (((1,), (0,)), ((), ()))
NT = (((1,), (1,)), ((), ()))
TN = (((0,), (0,)), ((), ()))


def mm(a, b, dims=NN):
    return lax.dot_general(a.astype(BF16), b.astype(BF16), dims, preferred_element_type=F32)


def split(a):
    high = a.astype(BF16)
    return high, (a - high.astype(F32)).astype(BF16)


def mm3(a, b, dims=NN):
    (ah, al), (bh, bl) = a, b
    dot = functools.partial(lax.dot_general, dimension_numbers=dims, preferred_element_type=F32)
    return dot(ah, bh) + (dot(ah, bl) + dot(al, bh))


def exact(a, b):
    return lax.dot_general(
        a, b, NN, precision=lax.Precision.HIGHEST, preferred_element_type=F32
    )


def iotas():
    row = lax.broadcasted_iota(jnp.int32, (BLOCK, BLOCK), 0)
    col = lax.broadcasted_iota(jnp.int32, (BLOCK, BLOCK), 1)
    return row, col


def unit_rows(rows):
    scale = lax.rsqrt(jnp.sum(rows * rows, axis=-1, keepdims=True) + 1e-06)
    return rows * scale, scale


def gate_columns(gates, row, col):
    cumul = exact(gates, (row <= col).astype(F32))
    columns = cumul.T
    last = columns[BLOCK - 1 : BLOCK, :]
    return cumul, columns, jnp.exp(columns), jnp.exp(last - columns), jnp.exp(last)


def decays(cumul, columns, h, strict):
    gap = columns[:, h : h + 1] - cumul[h : h + 1, :]
    return jnp.where(strict, jnp.exp(jnp.where(strict, gap, 0.0)), 0.0)


def unit_lower_inverses(parts, row, col):
    ident = (row == col).astype(F32)
    found = None
    size = 1
    while size < BLOCK:
        off = (row // (2 * size) == col // (2 * size)) & (row // size != col // size)
        offs = [jnp.where(off, a, 0.0) for a in parts]
        if size == 1:
            found = [ident - a for a in offs]
        else:
            halves = [split(t) for t in found]
            inner = [mm3(t, split(a)) for t, a in zip(halves, offs)]
            found = [t - mm3(split(x), s) for t, x, s in zip(found, inner, halves)]
        size *= 2
    return found


def local_maps(q_ref, k_ref, v_ref, g_ref, b_ref, pay_ref, t_ref, wm_ref, u0_ref, qe_ref, o0_ref):
    heads = g_ref.shape[1]
    copies = heads * DK // q_ref.shape[2]
    row, col = iotas()
    strict = row > col
    ident = (row == col).astype(F32)
    cumul, columns, growth, weight, ends = gate_columns(g_ref[0], row, col)
    betas = b_ref[0].T
    qhat, khat, pair_k, pair_q = [], [], [], []
    for j in range(heads // copies):
        cut = slice(j * DK, (j + 1) * DK)
        qn = unit_rows(q_ref[0, :, cut].astype(F32))[0] * QSCALE
        kn = unit_rows(k_ref[0, :, cut].astype(F32))[0]
        qhat.append(qn)
        khat.append(kn)
        pair_k.append(mm(kn, kn, NT))
        pair_q.append(mm(qn, kn, NT))
    decay = [decays(cumul, columns, h, strict) for h in range(heads)]
    beta = [betas[:, h : h + 1] for h in range(heads)]
    parts = [beta[h] * pair_k[h // copies] * decay[h] for h in range(heads)]
    inverse = unit_lower_inverses(parts, row, col)
    for h in range(heads):
        j = h // copies
        grow = growth[:, h : h + 1]
        value = v_ref[0, :, h * DV : (h + 1) * DV].astype(F32)
        t = split(inverse[h])
        wm = mm3(t, split((beta[h] * grow) * khat[j]))
        u0 = mm3(t, split(beta[h] * value))
        kw = split(weight[:, h : h + 1] * khat[j])
        step = ends[:, h : h + 1] * ident - mm3(split(wm), kw, TN)
        write = mm3(split(u0), kw, TN).astype(BF16)
        scores = pair_q[j] * (decay[h] + ident)
        t_ref[h] = t[0]
        wm_ref[h] = wm.astype(BF16)
        u0_ref[h] = u0.astype(BF16)
        qe_ref[h] = (grow * qhat[j] - mm(scores, wm)).astype(BF16)
        o0_ref[h] = mm(scores, u0).astype(BF16)
        step = step.astype(BF16)
        for half in range(2):
            pay_ref[2 * h + half, 0:DK] = step
            pay_ref[2 * h + half, DK : DK + HALF] = write[half * HALF : (half + 1) * HALF]


def head_grads(d_ref, grad_ref, own_ref, other_ref, qe_ref, pay_ref, hg_ref):
    d = d_ref[0]
    parts = grad_ref.shape[0] // 2
    wide = grad_ref.shape[2]
    total = jnp.zeros((BLOCK, own_ref.shape[1]), F32)
    for i in range(parts):
        cut = slice(i * wide, (i + 1) * wide)
        total += mm(grad_ref[parts * d + i], own_ref[cut, :])
        total += mm(grad_ref[parts * (1 - d) + i], other_ref[cut, :])
    total = total.astype(BF16)
    hg_ref[...] = total
    for h in range(qe_ref.shape[0]):
        back = mm(total[:, h * DV : (h + 1) * DV], qe_ref[h], TN).astype(BF16)
        for half in range(2):
            pay_ref[2 * h + half] = back[half * HALF : (half + 1) * HALF]


def chain(x_ref, l_ref, s0_ref, g1_ref, y_ref):
    blocks = x_ref.shape[0]

    def times(state, step, dims):
        out = mm(jnp.concatenate(split(state), axis=0), step, dims)
        return out[:HALF] + out[HALF:]

    state, back = s0_ref[...], g1_ref[...]
    for c in range(blocks):
        e = blocks - 1 - c
        y_ref[c, 0:HALF] = state.astype(BF16)
        y_ref[e, HALF:] = back.astype(BF16)
        if c < blocks - 1:
            state = times(state, x_ref[c, 0:DK], NN) + x_ref[c, DK : DK + HALF].astype(F32)
            back = times(back, x_ref[e, 0:DK], NT) + l_ref[e].astype(F32)


def state_of(y_ref, h, low):
    return jnp.concatenate(
        [y_ref[2 * h, low : low + HALF], y_ref[2 * h + 1, low : low + HALF]], axis=0
    )


def outputs(qe_ref, o0_ref, y_ref, o_ref):
    for h in range(qe_ref.shape[0]):
        out = o0_ref[h].astype(F32) + mm(qe_ref[h], state_of(y_ref, h, 0), NT)
        o_ref[:, h * DV : (h + 1) * DV] = out.astype(BF16)


def gradients(
    q_ref, k_ref, v_ref, g_ref, b_ref, t_ref, wm_ref, u0_ref, hg_ref, y_ref,
    dq_ref, dk_ref, dv_ref, dg_ref, db_ref,
):
    heads = g_ref.shape[1]
    copies = heads * DK // q_ref.shape[2]
    row, col = iotas()
    strict = row > col
    incl = row >= col
    ident = (row == col).astype(F32)
    cumul, columns, growth, weight, ends = gate_columns(g_ref[0], row, col)
    betas = b_ref[0].T
    lane = lax.broadcasted_iota(jnp.int32, (BLOCK, heads), 1)
    level = lax.broadcasted_iota(jnp.int32, (heads, BLOCK), 0)
    cumul_g = jnp.zeros((BLOCK, heads), F32)
    beta_g = jnp.zeros((BLOCK, heads), F32)
    across = jnp.zeros((heads, BLOCK), F32)
    for j in range(heads // copies):
        cut = slice(j * DK, (j + 1) * DK)
        qn, q_scale = unit_rows(q_ref[0, :, cut].astype(F32))
        khat, k_scale = unit_rows(k_ref[0, :, cut].astype(F32))
        qhat = qn * QSCALE
        qlow, klow = qhat.astype(BF16), khat.astype(BF16)
        pair_k = mm(klow, klow, NT)
        pair_q = mm(qlow, klow, NT)
        qhat_g = jnp.zeros((BLOCK, DK), F32)
        khat_g = jnp.zeros((BLOCK, DK), F32)
        for h in range(j * copies, (j + 1) * copies):
            cut_v = slice(h * DV, (h + 1) * DV)
            decay = decays(cumul, columns, h, strict)
            grow, keep, beta = growth[:, h : h + 1], weight[:, h : h + 1], betas[:, h : h + 1]
            value = v_ref[0, :, cut_v].astype(F32)
            state, back = state_of(y_ref, h, 0), state_of(y_ref, h, HALF)
            out_g = hg_ref[:, cut_v]
            decay_in = decay + ident
            scores = pair_q * decay_in
            fresh = (u0_ref[h].astype(F32) - mm(wm_ref[h], state, NT)).astype(BF16)
            fresh_g = mm(scores, out_g, TN) + mm(keep * khat, back, NT)
            rhs_g = mm(t_ref[h], fresh_g, TN)
            rhs_low = rhs_g.astype(BF16)
            read_q = mm(out_g, state)
            read_k = mm(rhs_low, state)
            scores_g = mm(out_g, fresh, NT)
            part_g = jnp.where(strict, -mm(rhs_low, fresh, NT), 0.0) * decay
            pair_qg = (scores_g * decay_in).astype(BF16)
            pair_kg = (part_g * beta).astype(BF16)
            kept_g = mm(fresh, back)
            part_k = part_g * pair_k
            gaps = scores_g * scores + part_k * beta
            low_q = mm(pair_qg, klow).astype(BF16).astype(F32)
            low_k = mm(pair_qg, qlow, TN) + mm(pair_kg, klow) + mm(pair_kg, klow, TN)
            qhat_g += grow * read_q + low_q
            khat_g += keep * kept_g - (beta * grow) * read_k + low_k.astype(BF16).astype(F32)
            dv_ref[0, :, cut_v] = (beta * rhs_g).astype(BF16)
            read_sum = jnp.sum(read_k * khat, axis=1, keepdims=True)
            beta_col = jnp.sum(rhs_g * value + part_k, axis=1, keepdims=True) - grow * read_sum
            kept_sum = jnp.sum(kept_g * khat, axis=1, keepdims=True) * keep
            grow_g = jnp.sum(read_q * qhat, axis=1, keepdims=True) - beta * read_sum
            cumul_col = grow_g * grow + jnp.sum(gaps, axis=1, keepdims=True) - kept_sum
            whole = jnp.sum(back.astype(F32) * state.astype(F32)) * ends[:, h : h + 1]
            at_end = jnp.sum(kept_sum, axis=0, keepdims=True) + whole
            cumul_col += jnp.where(row[:, 0:1] == BLOCK - 1, at_end, 0.0)
            cumul_g = jnp.where(lane == h, cumul_col, cumul_g)
            beta_g = jnp.where(lane == h, beta_col, beta_g)
            across = jnp.where(level == h, jnp.sum(gaps, axis=0, keepdims=True), across)
        q_along = jnp.sum(qn * qhat_g, axis=1, keepdims=True)
        k_along = jnp.sum(khat * khat_g, axis=1, keepdims=True)
        dq_ref[0, :, cut] = ((q_scale * QSCALE) * (qhat_g - qn * q_along)).astype(BF16)
        dk_ref[0, :, cut] = (k_scale * (khat_g - khat * k_along)).astype(BF16)
    db_ref[0] = beta_g.T
    dg_ref[0] = exact(cumul_g.T - across, (row >= col).astype(F32))


def call(kernel, outs, *args, flops=0, scalars=0):
    size = sum(a.size * a.dtype.itemsize for a in args)
    size += sum(o.size * o.dtype.itemsize for o in outs)
    smem = [pl.BlockSpec(memory_space=pltpu.SMEM)] * scalars
    vmem = [pl.BlockSpec(memory_space=pltpu.VMEM)] * (len(args) - scalars)
    return pl.pallas_call(
        kernel,
        out_shape=outs,
        in_specs=smem + vmem,
        out_specs=[pl.BlockSpec(memory_space=pltpu.VMEM)] * len(outs),
        compiler_params=pltpu.CompilerParams(vmem_limit_bytes=48 * 2**20),
        cost_estimate=pl.CostEstimate(flops=flops, bytes_accessed=size, transcendentals=0),
    )(*args)


def shape(dims, dtype):
    return jax.ShapeDtypeStruct(dims, dtype)


def body(
    queries, key_rows, value_rows, log_decay, write_rate,
    initial_state, final_state_grad, output_matrix, output_grad,
):
    heads = log_decay.shape[1]
    blocks = lax.axis_size("ctx")
    feats = lax.axis_size("tp")
    here, core = lax.axis_index("ctx"), lax.axis_index("dp")
    rows = output_matrix.shape[0]
    swap = [(0, 1), (1, 0)]
    square = (heads, BLOCK, DK)
    unit = 2 * BLOCK**3 * heads

    with jax.named_scope("other_rows"):
        other_matrix = lax.ppermute(output_matrix, "dp", swap)
    with jax.named_scope("gather_grad"):
        gathered = lax.all_to_all(
            jnp.broadcast_to(output_grad, (feats,) + output_grad.shape[1:]), "tp", 0, 0, tiled=True
        )
    with jax.named_scope("local_maps"):
        maps, t, wm, u0, qe, o0 = call(
            local_maps,
            [shape((blocks, DK + HALF, DK), BF16)] + [shape(square, BF16)] * 5,
            queries, key_rows, value_rows, log_decay, write_rate,
            flops=50 * unit,
        )
    with jax.named_scope("head_grads"):
        backs, head_grad = call(
            head_grads,
            [shape((blocks, HALF, DK), BF16), shape((BLOCK, heads * DV), BF16)],
            core.reshape(1), gathered, output_matrix, other_matrix, qe,
            flops=18 * unit, scalars=1,
        )
    with jax.named_scope("send_maps"):
        maps_in = lax.all_to_all(maps, "ctx", 0, 0, tiled=True)
        backs_in = lax.all_to_all(backs, "ctx", 0, 0, tiled=True)
    with jax.named_scope("chain"):
        first = lax.dynamic_index_in_dim(
            initial_state.reshape(blocks, HALF, DK), here, 0, keepdims=False
        )
        last = lax.dynamic_index_in_dim(
            final_state_grad.reshape(blocks, HALF, DK), here, 0, keepdims=False
        )
        states, = call(
            chain, [shape((blocks, 2 * HALF, DK), BF16)], maps_in, backs_in, first, last,
            flops=4 * unit,
        )
    with jax.named_scope("return_states"):
        states = lax.all_to_all(states, "ctx", 0, 0, tiled=True)
    with jax.named_scope("outputs"):
        heads_low, = call(
            outputs, [shape((BLOCK, heads * DV), BF16)], qe, o0, states, flops=unit
        )
    with jax.named_scope("projection"):
        half = feats // 2
        mine = lax.dynamic_slice_in_dim(gathered, half * core, half, 0)
        theirs = lax.dynamic_slice_in_dim(gathered, half * (1 - core), half, 0)
        theirs = lax.ppermute(theirs, "dp", swap)
        other_low = lax.ppermute(heads_low, "dp", swap)

        def wide(parts):
            return jnp.moveaxis(parts, 0, 1).reshape(BLOCK, rows)

        grads = jnp.concatenate([wide(mine), wide(theirs)], axis=0)
        lows = jnp.concatenate([heads_low, other_low], axis=0)
        partial = lax.dot_general(grads, lows, TN, preferred_element_type=F32).astype(BF16)
        pieces = lax.all_to_all(
            partial.reshape(blocks, rows // blocks, heads * DV), "ctx", 0, 0, tiled=True
        )
        piece = jnp.sum(pieces.astype(F32), axis=0)
        piece = piece * float(BLOCK * blocks * lax.axis_size("dp")) ** (-0.5)
        spread = jnp.broadcast_to(piece.astype(BF16), (blocks,) + piece.shape)
        total = lax.all_to_all(spread, "ctx", 0, 0, tiled=True)
        weight_grad = total.reshape(rows, heads * DV).astype(F32)
    with jax.named_scope("gradients"):
        query_g, key_g, value_g, decay_g, rate_g = call(
            gradients,
            [
                shape(queries.shape, BF16),
                shape(key_rows.shape, BF16),
                shape(value_rows.shape, BF16),
                shape(log_decay.shape, F32),
                shape(write_rate.shape, F32),
            ],
            queries, key_rows, value_rows, log_decay, write_rate,
            t, wm, u0, head_grad, states,
            flops=17 * unit,
        )
    return (query_g, key_g, value_g, decay_g, rate_g, weight_grad)


def solution(mesh):
    rows = P("dp", "ctx", "tp")
    gates = P("dp", "tp", "ctx")
    state = P("dp", "tp", None, None)
    return jax.shard_map(
        body,
        mesh=mesh,
        in_specs=(rows, rows, rows, gates, gates, state, state, P("dp", "tp"), rows),
        out_specs=(rows, rows, rows, gates, gates, P("dp", "tp")),
        check_vma=False,
    )
```

profile of v0, /device:TPU:2, one launch (start us, length us, event | category | flops | bytes accessed | tf_op | source)
XLA Modules:
  0.0 146.8 jit_solution(2429068083830599483)
XLA Ops:
  0.6 0.1 collective-permute-start
  0.7 1.7 %broadcast_in_dim.11 = bf16[4,128,512]{2,1,0:T(8,128)(2,1)} broadcast(bf16[128,512]{1,0:T(8,128)(2,1)} %bitcast.21), dimensions={1,2} | broadcast | bytes 655360 | tf_op jit(solution)/shard_map/gather_grad/broadcast_in_dim | solution.py:282
  2.5 4.8 %all-to-all-start = ((bf16[4,128,512]{2,1,0:T(8,128)(2,1)}), bf16[4,128,512]{2,1,0:T(8,128)(2,1)S(1)}, u32[]{:S(2)}, u32[]{:S(2)}) async-start(bf16[4,128,512]{2,1,0:T(8,128)(2,1)} %broadcast_in_dim.11), calls=%async_computation | async-start | bytes 1048576 | tf_op jit(solution)/shard_map/gather_grad/all_to_all | solution.py:281
  7.3 0.9 copy-done.8
  8.3 0.9 copy-done.12
  9.2 0.9 copy-done.14
  10.1 0.7 copy-done.16
  10.7 0.7 copy-done.18
  11.4 5.9 %local_maps.1 = (bf16[16,192,128]{2,1,0:T(8,128)(2,1)S(1)}, bf16[8,128,128]{2,1,0:T(8,128)(2,1)S(1)}, bf16[8,128,128]{2,1,0:T(8,128)(2,1)S(1)}, bf16[8,128,128]{...) custom-call(bf16[1,128,512]{2,1,0:T(8,128)(2,1)S(1)} %copy-done.12, ...), custom_call_target="tpu_custom_call" | custom-call | flops 1677721600 | bytes 2629632 | tf_op jit(solution)/shard_map/local_maps/pallas_call | solution.py:251
  17.4 0.0 copy-start.1
  17.4 0.7 copy-done.1
  18.1 0.9 copy-done.4
  18.9 0.7 copy-done.5
  19.6 0.7 copy-done.20
  20.3 0.7 copy-done.22
  21.0 0.7 copy-done.24
  21.7 0.0 all-to-all-done.grad_ref
  21.7 8.0 %all-to-all-start.1 = ((bf16[16,192,128]{2,1,0:T(8,128)(2,1)}), bf16[16,192,128]{2,1,0:T(8,128)(2,1)S(1)}, u32[]{:S(2)}, u32[]{:S(2)}) async-start(bf16[16,192,128]{2,1,0:T(8,128)(2,1)} %copy-done.4), calls=%async_computation.1 | async-start | bytes 1572864 | tf_op jit(solution)/shard_map/send_maps/all_to_all | solution.py:299
  29.8 0.0 collective-permute-done.other_ref
  29.8 0.0 copy-done
  29.8 0.0 copy-start.2
  29.8 0.9 copy-done.2
  30.8 2.5 %head_grads.1 = (bf16[16,64,128]{2,1,0:T(8,128)(2,1)S(1)}, bf16[128,1024]{1,0:T(8,128)(2,1)S(1)}) custom-call(s32[1]{0:T(128)} %bitcast.d_ref, bf16[4,128,512]{2,1,0:T(8,128)(2,1)S(1)} %all-to-all-done.grad_ref, bf16[1024,1024]{1,0:T(8,128)(2,1)S(1)} %copy-done, bf16[1024,1024]{1,0:T(8,128)(2,1)} %collective-permute-done.other_ref, ...), custom_call_target="tpu_custom_call" | custom-call | flops 603979776 | bytes 5505028 | tf_op jit(solution)/shard_map/head_grads/pallas_call | solution.py:251
  33.3 0.0 copy-start.7
  33.3 0.7 copy-done.7
  34.0 0.7 copy-done.10
  34.7 9.6 %all-to-all-done.1.x_ref = bf16[16,192,128]{2,1,0:T(8,128)(2,1)S(1)} async-done(((bf16[16,192,128]{2,1,0:T(8,128)(2,1)}), bf16[16,192,128]{2,1,0:T(8,128)(2,1)S(1)}, u32[]{:S(2)}, u32[]{:S(2)}) %all-to-all-start.1) | async-done | bytes 786464 | tf_op jit(solution)/shard_map/send_maps/all_to_all | solution.py:299
  44.3 3.7 %all-to-all-start.2 = ((bf16[16,64,128]{2,1,0:T(8,128)(2,1)}), bf16[16,64,128]{2,1,0:T(8,128)(2,1)S(1)}, u32[]{:S(2)}, u32[]{:S(2)}) async-start(bf16[16,64,128]{2,1,0:T(8,128)(2,1)} %copy-done.7), calls=%async_computation.2 | async-start | bytes 524288 | tf_op jit(solution)/shard_map/send_maps/all_to_all | solution.py:300
  48.0 0.8 dynamic-slice_bitcast_fusion.1
  48.8 7.7 %all-to-all-done.2.l_ref = bf16[16,64,128]{2,1,0:T(8,128)(2,1)S(1)} async-done(((bf16[16,64,128]{2,1,0:T(8,128)(2,1)}), bf16[16,64,128]{2,1,0:T(8,128)(2,1)S(1)}, u32[]{:S(2)}, u32[]{:S(2)}) %all-to-all-start.2) | async-done | bytes 262176 | tf_op jit(solution)/shard_map/send_maps/all_to_all | solution.py:300
  56.4 2.8 %chain.1 = bf16[16,128,128]{2,1,0:T(8,128)(2,1)} custom-call(bf16[16,192,128]{2,1,0:T(8,128)(2,1)S(1)} %all-to-all-done.1.x_ref, bf16[16,64,128]{2,1,0:T(8,128)(2,1)S(1)} %all-to-all-done.2.l_ref, f32[64,128]{1,0:T(8,128)S(1)} %get-tuple-element.35.s0_ref, f32[64,128]{1,0:T(8,128)S(1)} %get-tuple-element.34.g1_ref), custom_call_target="tpu_custom_call" | custom-call | flops 134217728 | bytes 1638400 | tf_op jit(solution)/shard_map/chain/pallas_call | solution.py:251
  59.2 3.7 %all-to-all-start.3 = ((bf16[16,128,128]{2,1,0:T(8,128)(2,1)}), bf16[16,128,128]{2,1,0:T(8,128)(2,1)S(1)}, u32[]{:S(2)}, u32[]{:S(2)}) async-start(bf16[16,128,128]{2,1,0:T(8,128)(2,1)} %chain.1), calls=%async_computation.3 | async-start | bytes 1048576 | tf_op jit(solution)/shard_map/return_states/all_to_all | solution.py:313
  62.9 0.1 collective-permute-start.1
  63.0 9.9 %all-to-all-done.3.y_ref = bf16[16,128,128]{2,1,0:T(8,128)(2,1)S(1)} async-done(((bf16[16,128,128]{2,1,0:T(8,128)(2,1)}), bf16[16,128,128]{2,1,0:T(8,128)(2,1)S(1)}, u32[]{:S(2)}, u32[]{:S(2)}) %all-to-all-start.3) | async-done | bytes 524320 | tf_op jit(solution)/shard_map/return_states/all_to_all | solution.py:313
  73.0 0.0 copy-done.3
  73.0 0.0 copy-done.6
  73.0 0.3 outputs.1
  73.3 0.1 collective-permute-start.2
  73.4 0.2 copy.15
  73.5 0.0 collective-permute-done.1
  73.5 0.2 copy.16
  73.7 1.2 collective-permute-done.2
  74.9 0.7 convolution_convert_fusion
  75.6 31.9 %all_to_all.30 = bf16[16,64,1024]{2,1,0:T(8,128)(2,1)S(1)} all-to-all(bf16[16,64,1024]{2,1,0:T(8,128)(2,1)S(1)} %bitcast.17), channel_id=1, replica_groups=mesh['ctx'=16,'tp'=4,'dp'=2] {'ctx'}, dimensions={0} | all-to-all | bytes 4194304 | tf_op jit(solution)/shard_map/projection/all_to_all | solution.py:331
  107.5 0.4 convert_reduce_fusion
  107.9 1.6 %broadcast_in_dim.12 = bf16[16,64,1024]{2,1,0:T(8,128)(2,1)} broadcast(bf16[64,1024]{1,0:T(8,128)(2,1)S(1)} %multiply_convert_fusion), dimensions={1,2} | broadcast | bytes 2228224 | tf_op jit(solution)/shard_map/projection/broadcast_in_dim | solution.py:336
  109.5 0.0 copy-start.17
  109.5 0.0 copy-start.19
  109.5 0.0 copy-start.21
  109.5 0.0 copy-start.23
  109.6 0.0 copy-start.25
  109.6 4.8 %all-to-all-start.5 = ((bf16[16,64,1024]{2,1,0:T(8,128)(2,1)}), bf16[16,64,1024]{2,1,0:T(8,128)(2,1)}, u32[]{:S(2)}, u32[]{:S(2)}) async-start(bf16[16,64,1024]{2,1,0:T(8,128)(2,1)} %broadcast_in_dim.12), calls=%async_computation.5 | async-start | bytes 4194304 | tf_op jit(solution)/shard_map/projection/all_to_all | solution.py:337
  114.3 0.0 copy-done.9
  114.3 0.0 copy-done.11
  114.4 0.0 copy-done.13
  114.4 0.0 copy-done.15
  114.4 0.0 copy-done.17
  114.4 0.0 copy-done.19
  114.4 0.0 copy-done.21
  114.4 0.0 copy-done.23
  114.4 0.0 copy-done.25
  114.4 6.1 %gradients.1 = (bf16[1,128,512]{2,1,0:T(8,128)(2,1)}, bf16[1,128,512]{2,1,0:T(8,128)(2,1)}, bf16[1,128,1024]{2,1,0:T(8,128)(2,1)}, f32[1,8,128]{2,1,0:T(8,128)}, f32[1,8,128]{2,1,0:T(8,128)}) custom-call(bf16[1,128,512]{2,1,0:T(8,128)(2,1)S(1)} %copy-done.13, bf16[1,128,512]{2,1,0:T(8,128)(2,1)S(1)} %copy-done.15, bf16[1,128,1024]{2,1,0:T(8,128)(2,1)S(1)} %copy-done.9, ...), custom_call_target="tpu_custom_call" | custom-call | flops 570425344 | bytes 2637824 | tf_op jit(solution)/shard_map/gradients/pallas_call | solution.py:251
  120.5 22.3 %all-to-all-done.5 = bf16[16,64,1024]{2,1,0:T(8,128)(2,1)} async-done(((bf16[16,64,1024]{2,1,0:T(8,128)(2,1)}), bf16[16,64,1024]{2,1,0:T(8,128)(2,1)}, u32[]{:S(2)}, u32[]{:S(2)}) %all-to-all-start.5) | async-done | bytes 2097184 | tf_op jit(solution)/shard_map/projection/all_to_all | solution.py:337
  142.8 4.1 %bitcast_convert_fusion = f32[1024,1024]{1,0:T(8,128)} fusion(bf16[16,64,1024]{2,1,0:T(8,128)(2,1)} %all-to-all-done.5), kind=kLoop, calls=%fused_computation.1 | loop fusion | flops 1048576 | bytes 6291456 | tf_op jit(solution)/shard_map/projection/convert_element_type | solution.py:338
  (20 shorter events, 0.1 us)
Async XLA Ops:
  0.6 29.2 %collective-permute-start = (bf16[1024,1024]{1,0:T(8,128)(2,1)}, bf16[1024,1024]{1,0:T(8,128)(2,1)}, u32[]{:S(2)}, u32[]{:S(2)}) collective-permute-start(bf16[1024,1024]{1,0:T(8,128)(2,1)} %own_ref.1), channel_id=1, source_target_pairs={{0,1},{1,0},{2,3},{3,2},{4,5},{5,4},{6,7},{7,6},{8,9},{9,8},{10,11... | collective-permute-start | bytes 6291464 | tf_op jit(solution)/shard_map/other_rows/ppermute | solution.py:279
  2.5 19.3 %all-to-all-start = ((bf16[4,128,512]{2,1,0:T(8,128)(2,1)}), bf16[4,128,512]{2,1,0:T(8,128)(2,1)S(1)}, u32[]{:S(2)}, u32[]{:S(2)}) async-start(bf16[4,128,512]{2,1,0:T(8,128)(2,1)} %broadcast_in_dim.11), calls=%async_computation | async-start | bytes 1048576 | tf_op jit(solution)/shard_map/gather_grad/all_to_all | solution.py:281
  7.3 0.9 copy-start.8
  8.2 0.9 copy-start.12
  9.2 0.9 copy-start.14
  10.1 0.7 copy-start.16
  10.7 0.7 copy-start.18
  11.4 18.4 %copy-start = (bf16[1024,1024]{1,0:T(8,128)(2,1)S(1)}, bf16[1024,1024]{1,0:T(8,128)(2,1)}, u32[]{:S(2)}) copy-start(bf16[1024,1024]{1,0:T(8,128)(2,1)} %own_ref.1) | copy-start | bytes 6291460
  17.4 0.7 copy-start.1
  18.1 0.9 copy-start.4
  18.9 0.7 copy-start.5
  19.6 0.7 copy-start.20
  20.3 0.7 copy-start.22
  21.0 0.7 copy-start.24
  21.7 22.6 %all-to-all-start.1 = ((bf16[16,192,128]{2,1,0:T(8,128)(2,1)}), bf16[16,192,128]{2,1,0:T(8,128)(2,1)S(1)}, u32[]{:S(2)}, u32[]{:S(2)}) async-start(bf16[16,192,128]{2,1,0:T(8,128)(2,1)} %copy-done.4), calls=%async_computation.1 | async-start | bytes 1572864 | tf_op jit(solution)/shard_map/send_maps/all_to_all | solution.py:299
  29.8 1.0 copy-start.2
  33.3 0.7 copy-start.7
  34.0 0.7 copy-start.10
  44.3 28.7 %copy-start.3 = (bf16[8,128,128]{2,1,0:T(8,128)(2,1)S(1)}, bf16[8,128,128]{2,1,0:T(8,128)(2,1)}, u32[]{:S(2)}) copy-start(bf16[8,128,128]{2,1,0:T(8,128)(2,1)} %copy-done.1) | copy-start | bytes 786436
  44.3 28.7 %copy-start.6 = (bf16[8,128,128]{2,1,0:T(8,128)(2,1)S(1)}, bf16[8,128,128]{2,1,0:T(8,128)(2,1)}, u32[]{:S(2)}) copy-start(bf16[8,128,128]{2,1,0:T(8,128)(2,1)} %copy-done.5) | copy-start | bytes 786436
  44.3 12.1 %all-to-all-start.2 = ((bf16[16,64,128]{2,1,0:T(8,128)(2,1)}), bf16[16,64,128]{2,1,0:T(8,128)(2,1)S(1)}, u32[]{:S(2)}, u32[]{:S(2)}) async-start(bf16[16,64,128]{2,1,0:T(8,128)(2,1)} %copy-done.7), calls=%async_computation.2 | async-start | bytes 524288 | tf_op jit(solution)/shard_map/send_maps/all_to_all | solution.py:300
  59.2 13.8 %all-to-all-start.3 = ((bf16[16,128,128]{2,1,0:T(8,128)(2,1)}), bf16[16,128,128]{2,1,0:T(8,128)(2,1)S(1)}, u32[]{:S(2)}, u32[]{:S(2)}) async-start(bf16[16,128,128]{2,1,0:T(8,128)(2,1)} %chain.1), calls=%async_computation.3 | async-start | bytes 1048576 | tf_op jit(solution)/shard_map/return_states/all_to_all | solution.py:313
  62.9 10.6 %collective-permute-start.1 = (bf16[2,128,512]{2,1,0:T(8,128)(2,1)S(1)}, bf16[2,128,512]{2,1,0:T(8,128)(2,1)S(1)}, u32[]{:S(2)}, u32[]{:S(2)}) collective-permute-start(bf16[2,128,512]{2,1,0:T(8,128)(2,1)S(1)} %get-tuple-element.33), channel_id=1, source_target_pairs={{0,1},{1,0},{2,3},{3,2},{4,5},{5,4},{6,7},{7,6},{8,9},{9,8},{10,11... | collective-permute-start | bytes 786440 | tf_op jit(solution)/shard_map/projection/ppermute | solution.py:322
  73.3 1.6 %collective-permute-start.2 = (bf16[128,1024]{1,0:T(8,128)(2,1)S(1)}, bf16[128,1024]{1,0:T(8,128)(2,1)S(1)}, u32[]{:S(2)}, u32[]{:S(2)}) collective-permute-start(bf16[128,1024]{1,0:T(8,128)(2,1)S(1)} %outputs.1), channel_id=1, source_target_pairs={{0,1},{1,0},{2,3},{3,2},{4,5},{5,4},{6,7},{7,6},{8,9},{9,8},{10,11... | collective-permute-start | bytes 786440 | tf_op jit(solution)/shard_map/projection/ppermute | solution.py:323
  109.5 4.8 %copy-start.9 = (bf16[1,128,1024]{2,1,0:T(8,128)(2,1)S(1)}, bf16[1,128,1024]{2,1,0:T(8,128)(2,1)}, u32[]{:S(2)}) copy-start(bf16[1,128,1024]{2,1,0:T(8,128)(2,1)} %v_ref.3) | copy-start | bytes 786436
  109.5 4.8 %copy-start.11 = (bf16[128,1024]{1,0:T(8,128)(2,1)S(1)}, bf16[128,1024]{1,0:T(8,128)(2,1)}, u32[]{:S(2)}) copy-start(bf16[128,1024]{1,0:T(8,128)(2,1)} %copy-done.10) | copy-start | bytes 786436
  109.5 4.8 %copy-start.13 = (bf16[1,128,512]{2,1,0:T(8,128)(2,1)S(1)}, bf16[1,128,512]{2,1,0:T(8,128)(2,1)}, u32[]{:S(2)}) copy-start(bf16[1,128,512]{2,1,0:T(8,128)(2,1)} %q_ref.3) | copy-start | bytes 393220
  109.5 4.9 %copy-start.15 = (bf16[1,128,512]{2,1,0:T(8,128)(2,1)S(1)}, bf16[1,128,512]{2,1,0:T(8,128)(2,1)}, u32[]{:S(2)}) copy-start(bf16[1,128,512]{2,1,0:T(8,128)(2,1)} %k_ref.3) | copy-start | bytes 393220
  109.5 4.9 %copy-start.17 = (f32[1,8,128]{2,1,0:T(8,128)S(1)}, f32[1,8,128]{2,1,0:T(8,128)}, u32[]{:S(2)}) copy-start(f32[1,8,128]{2,1,0:T(8,128)} %g_ref.3) | copy-start | bytes 12292
  109.5 4.9 %copy-start.19 = (f32[1,8,128]{2,1,0:T(8,128)S(1)}, f32[1,8,128]{2,1,0:T(8,128)}, u32[]{:S(2)}) copy-start(f32[1,8,128]{2,1,0:T(8,128)} %b_ref.3) | copy-start | bytes 12292
  109.5 4.9 %copy-start.21 = (bf16[8,128,128]{2,1,0:T(8,128)(2,1)S(1)}, bf16[8,128,128]{2,1,0:T(8,128)(2,1)}, u32[]{:S(2)}) copy-start(bf16[8,128,128]{2,1,0:T(8,128)(2,1)} %copy-done.20) | copy-start | bytes 786436
  109.5 4.9 %copy-start.23 = (bf16[8,128,128]{2,1,0:T(8,128)(2,1)S(1)}, bf16[8,128,128]{2,1,0:T(8,128)(2,1)}, u32[]{:S(2)}) copy-start(bf16[8,128,128]{2,1,0:T(8,128)(2,1)} %copy-done.22) | copy-start | bytes 786436
  109.6 4.9 %copy-start.25 = (bf16[8,128,128]{2,1,0:T(8,128)(2,1)S(1)}, bf16[8,128,128]{2,1,0:T(8,128)(2,1)}, u32[]{:S(2)}) copy-start(bf16[8,128,128]{2,1,0:T(8,128)(2,1)} %copy-done.24) | copy-start | bytes 786436
  109.6 33.2 %all-to-all-start.5 = ((bf16[16,64,1024]{2,1,0:T(8,128)(2,1)}), bf16[16,64,1024]{2,1,0:T(8,128)(2,1)}, u32[]{:S(2)}, u32[]{:S(2)}) async-start(bf16[16,64,1024]{2,1,0:T(8,128)(2,1)} %broadcast_in_dim.12), calls=%async_computation.5 | async-start | bytes 4194304 | tf_op jit(solution)/shard_map/projection/all_to_all | solution.py:337
where the time goes:
time: 148 us; the launch traced here: 147 us
  waiting for transfers between devices  50.7 us (34%)
  blocking collectives  31.9 us (22%)
  starting transfers between devices  25.2 us (17%)
  Pallas kernels  17.6 us (12%)
  local copies, waits for them, and re-layouts  15.4 us (10%)
  other arithmetic  4.48 us (3%)
    all_to_all x1, blocking collectives, body(): lax.all_to_all(partial.reshape(blocks, rows // blocks, heads * DV), 'ctx'...  31.9 us
    all_to_all x1, waiting for transfers between devices, body(): total = lax.all_to_all(spread, 'ctx', 0, 0, tiled=True)  22.3 us
    pallas_call x5, Pallas kernels, call(): pl.pallas_call(kernel, out_shape=outs, in_specs=smem + vmem, out_specs=[p...  17.6 us
    unnamed x52, local copies, waits for them, and re-layouts  10.9 us
    all_to_all x1, waiting for transfers between devices, body(): states = lax.all_to_all(states, 'ctx', 0, 0, tiled=True)  9.95 us
    all_to_all x1, waiting for transfers between devices, body(): maps_in = lax.all_to_all(maps, 'ctx', 0, 0, tiled=True)  9.59 us
    all_to_all x1, starting transfers between devices, body(): maps_in = lax.all_to_all(maps, 'ctx', 0, 0, tiled=True)  8.05 us
    all_to_all x1, waiting for transfers between devices, body(): backs_in = lax.all_to_all(backs, 'ctx', 0, 0, tiled=True)  7.65 us
  transfers between devices with their start and end apart: 8, of which 5 were waited for; matrix products, arithmetic and copies ran while one was open for 2% of the time, Pallas kernels for 10%

commit v1 on v0

--- a/solution.py
+++ b/solution.py
@@ -1,4 +1,5 @@
 import functools
+import math
 
 import jax
 import jax.numpy as jnp
@@ -124,49 +125,129 @@
             pay_ref[2 * h + half, DK : DK + HALF] = write[half * HALF : (half + 1) * HALF]
 
 
-def head_grads(d_ref, grad_ref, own_ref, other_ref, qe_ref, pay_ref, hg_ref):
-    d = d_ref[0]
-    parts = grad_ref.shape[0] // 2
-    wide = grad_ref.shape[2]
+def head_grads(
+    at_ref, g0_ref, g1_ref, g2_ref, g3_ref, own_hbm, other_ref, qe_hbm, pay_in,
+    pay_ref, hg_ref, mine_ref, theirs_ref, all_ref, own_ref, qe_ref, back_ref, in_sems, out_sem,
+):
+    fetch = pltpu.make_async_copy(own_hbm, own_ref, in_sems.at[0])
+    fetch_qe = pltpu.make_async_copy(qe_hbm, qe_ref, in_sems.at[1])
+    fetch.start()
+    fetch_qe.start()
+    core, here = at_ref[0], at_ref[1]
+    feats, wide = all_ref.shape[0], all_ref.shape[2]
+    parts = feats // 2
+    for k, ref in enumerate((g0_ref, g1_ref, g2_ref, g3_ref)):
+        all_ref[lax.rem(here + k, feats)] = ref[0]
     total = jnp.zeros((BLOCK, own_ref.shape[1]), F32)
     for i in range(parts):
         cut = slice(i * wide, (i + 1) * wide)
-        total += mm(grad_ref[parts * d + i], own_ref[cut, :])
-        total += mm(grad_ref[parts * (1 - d) + i], other_ref[cut, :])
+        theirs = all_ref[parts * (1 - core) + i]
+        total += mm(theirs, other_ref[cut, :])
+        theirs_ref[:, cut] = theirs
+    fetch.wait()
+    for i in range(parts):
+        cut = slice(i * wide, (i + 1) * wide)
+        mine = all_ref[parts * core + i]
+        total += mm(mine, own_ref[cut, :])
+        mine_ref[:, cut] = mine
     total = total.astype(BF16)
     hg_ref[...] = total
+    fetch_qe.wait()
     for h in range(qe_ref.shape[0]):
         back = mm(total[:, h * DV : (h + 1) * DV], qe_ref[h], TN).astype(BF16)
         for half in range(2):
-            pay_ref[2 * h + half] = back[half * HALF : (half + 1) * HALF]
-
-
-def chain(x_ref, l_ref, s0_ref, g1_ref, y_ref):
-    blocks = x_ref.shape[0]
+            back_ref[2 * h + half] = back[half * HALF : (half + 1) * HALF]
+    put = pltpu.make_async_copy(back_ref, pay_ref.at[:, pl.ds(DK + HALF, HALF)], out_sem)
+    put.start()
+    put.wait()
+
+
+def chain(maps_ref, first_ref, last_ref, out_ref, kept_ref, sems):
+    blocks = maps_ref.shape[0]
+    copies = []
 
     def times(state, step, dims):
         out = mm(jnp.concatenate(split(state), axis=0), step, dims)
         return out[:HALF] + out[HALF:]
 
-    state, back = s0_ref[...], g1_ref[...]
+    def send(value, c, side):
+        rows = pl.ds(side * HALF, HALF)
+        kept_ref[c, rows] = value.astype(BF16)
+        copy = pltpu.make_async_copy(kept_ref.at[c, rows], out_ref.at[c, rows], sems.at[c, side])
+        copy.start()
+        copies.append(copy)
+
+    state, back = first_ref[...], last_ref[...]
     for c in range(blocks):
         e = blocks - 1 - c
-        y_ref[c, 0:HALF] = state.astype(BF16)
-        y_ref[e, HALF:] = back.astype(BF16)
+        send(state, c, 0)
+        send(back, e, 1)
         if c < blocks - 1:
-            state = times(state, x_ref[c, 0:DK], NN) + x_ref[c, DK : DK + HALF].astype(F32)
-            back = times(back, x_ref[e, 0:DK], NT) + l_ref[e].astype(F32)
-
-
-def state_of(y_ref, h, low):
-    return jnp.concatenate(
-        [y_ref[2 * h, low : low + HALF], y_ref[2 * h + 1, low : low + HALF]], axis=0
-    )
+            write = maps_ref[c, DK : DK + HALF].astype(F32)
+            read = maps_ref[e, DK + HALF :].astype(F32)
+            state = times(state, maps_ref[c, 0:DK], NN) + write
+            back = times(back, maps_ref[e, 0:DK], NT) + read
+    for copy in copies:
+        copy.wait()
+
+
+def projection(mine_ref, theirs_ref, low_ref, other_ref, out_ref, kept_ref, sems):
+    blocks, piece = out_ref.shape[0], out_ref.shape[1]
+    parts = sems.shape[0]
+    some = blocks // parts
+    copies = []
+    for p in range(parts):
+        cut = slice(p * some * piece, (p + 1) * some * piece)
+        total = mm(mine_ref[:, cut], low_ref[...], TN) + mm(theirs_ref[:, cut], other_ref[...], TN)
+        total = total.astype(BF16)
+        for c in range(some):
+            kept_ref[p * some + c] = total[c * piece : (c + 1) * piece]
+        at = pl.ds(p * some, some)
+        copies.append(pltpu.make_async_copy(kept_ref.at[at], out_ref.at[at], sems.at[p]))
+        copies[-1].start()
+    for copy in copies:
+        copy.wait()
+
+
+def reduce_spread(scale, pieces_ref, out_ref, sum_ref, sems):
+    blocks, rows = out_ref.shape[:2]
+    parts = sems.shape[1]
+    copies = []
+    for p in range(parts):
+        at = pl.ds(p * (rows // parts), rows // parts)
+        total = pieces_ref[0, at].astype(F32)
+        for c in range(1, blocks):
+            total += pieces_ref[c, at].astype(F32)
+        sum_ref[at] = (total * scale).astype(BF16)
+        for c in range(blocks):
+            copy = pltpu.make_async_copy(sum_ref.at[at], out_ref.at[c, at], sems.at[c, p])
+            copy.start()
+            copies.append(copy)
+    for copy in copies:
+        copy.wait()
+
+
+def widen(in_ref, out_ref, kept_ref, sems):
+    parts = sems.shape[0]
+    step = in_ref.shape[0] // parts
+    copies = []
+    for p in range(parts):
+        at = pl.ds(p * step, step)
+        kept_ref[at, :] = in_ref[at, :].astype(F32)
+        copies.append(pltpu.make_async_copy(kept_ref.at[at], out_ref.at[at], sems.at[p]))
+        copies[-1].start()
+    for copy in copies:
+        copy.wait()
+
+
+def halves_of(ref, h, low):
+    rows = slice(low, low + HALF)
+    return jnp.concatenate([ref[2 * h, rows], ref[2 * h + 1, rows]], axis=0)
 
 
 def outputs(qe_ref, o0_ref, y_ref, o_ref):
     for h in range(qe_ref.shape[0]):
-        out = o0_ref[h].astype(F32) + mm(qe_ref[h], state_of(y_ref, h, 0), NT)
+        out = o0_ref[h].astype(F32) + mm(qe_ref[h], halves_of(y_ref, h, 0), NT)
         o_ref[:, h * DV : (h + 1) * DV] = out.astype(BF16)
 
 
@@ -202,7 +283,7 @@
             decay = decays(cumul, columns, h, strict)
             grow, keep, beta = growth[:, h : h + 1], weight[:, h : h + 1], betas[:, h : h + 1]
             value = v_ref[0, :, cut_v].astype(F32)
-            state, back = state_of(y_ref, h, 0), state_of(y_ref, h, HALF)
+            state, back = halves_of(y_ref, h, 0), halves_of(y_ref, h, HALF)
             out_g = hg_ref[:, cut_v]
             decay_in = decay + ident
             scores = pair_q * decay_in
@@ -243,23 +324,40 @@
     dg_ref[0] = exact(cumul_g.T - across, (row >= col).astype(F32))
 
 
-def call(kernel, outs, *args, flops=0, scalars=0):
-    size = sum(a.size * a.dtype.itemsize for a in args)
-    size += sum(o.size * o.dtype.itemsize for o in outs)
-    smem = [pl.BlockSpec(memory_space=pltpu.SMEM)] * scalars
-    vmem = [pl.BlockSpec(memory_space=pltpu.VMEM)] * (len(args) - scalars)
+def whole(x):
+    return pl.BlockSpec(x.shape, lambda *i: (0,) * len(x.shape))
+
+
+SCALAR = pl.BlockSpec(memory_space=pltpu.SMEM)
+HELD = pl.BlockSpec(memory_space=pltpu.VMEM)
+FAR = pl.BlockSpec(memory_space=pl.ANY)
+
+
+def call(kernel, outs, *args, ins=None, out_specs=None, flops=0, scratch=(), grid=(), limit=24, **more):
+    size = sum(math.prod(x.shape) * x.dtype.itemsize for x in (*args, *outs))
     return pl.pallas_call(
         kernel,
+        grid=grid,
         out_shape=outs,
-        in_specs=smem + vmem,
-        out_specs=[pl.BlockSpec(memory_space=pltpu.VMEM)] * len(outs),
-        compiler_params=pltpu.CompilerParams(vmem_limit_bytes=48 * 2**20),
+        in_specs=[HELD] * len(args) if ins is None else ins,
+        out_specs=[HELD] * len(outs) if out_specs is None else out_specs,
+        scratch_shapes=scratch,
+        compiler_params=pltpu.CompilerParams(vmem_limit_bytes=limit * 2**20),
         cost_estimate=pl.CostEstimate(flops=flops, bytes_accessed=size, transcendentals=0),
+        **more,
     )(*args)
 
 
 def shape(dims, dtype):
     return jax.ShapeDtypeStruct(dims, dtype)
+
+
+def far(dims, dtype):
+    return pltpu.HBM(dims, dtype)
+
+
+def fixed(x):
+    return pltpu.with_memory_space_constraint(x, pltpu.HBM)
 
 
 def body(
@@ -270,84 +368,93 @@
     blocks = lax.axis_size("ctx")
     feats = lax.axis_size("tp")
     here, core = lax.axis_index("ctx"), lax.axis_index("dp")
-    rows = output_matrix.shape[0]
+    rows, wide = output_matrix.shape
+    piece = rows // blocks
     swap = [(0, 1), (1, 0)]
     square = (heads, BLOCK, DK)
     unit = 2 * BLOCK**3 * heads
 
+    def own_half(states):
+        parts = states.reshape(blocks, HALF, DK)
+        return lax.dynamic_index_in_dim(parts, here, 0, keepdims=False)
+
+    with jax.named_scope("gather_grad"):
+        grads = [output_grad]
+        for k in range(1, feats):
+            pairs = [((i + k) % feats, i) for i in range(feats)]
+            grads.append(lax.ppermute(output_grad, "tp", pairs))
     with jax.named_scope("other_rows"):
         other_matrix = lax.ppermute(output_matrix, "dp", swap)
-    with jax.named_scope("gather_grad"):
-        gathered = lax.all_to_all(
-            jnp.broadcast_to(output_grad, (feats,) + output_grad.shape[1:]), "tp", 0, 0, tiled=True
-        )
+    dma = pltpu.SemaphoreType.DMA
     with jax.named_scope("local_maps"):
+        args = tuple(map(fixed, (queries, key_rows, value_rows, log_decay, write_rate)))
+        outs = [far((blocks, 2 * DK, DK), BF16)] + [far(square, BF16)] * 5
         maps, t, wm, u0, qe, o0 = call(
-            local_maps,
-            [shape((blocks, DK + HALF, DK), BF16)] + [shape(square, BF16)] * 5,
-            queries, key_rows, value_rows, log_decay, write_rate,
+            local_maps, outs, *args,
+            ins=[whole(a) for a in args], out_specs=[whole(o) for o in outs], grid=(1,),
             flops=50 * unit,
         )
     with jax.named_scope("head_grads"):
-        backs, head_grad = call(
+        maps, head_grad, mine, theirs = call(
             head_grads,
-            [shape((blocks, HALF, DK), BF16), shape((BLOCK, heads * DV), BF16)],
-            core.reshape(1), gathered, output_matrix, other_matrix, qe,
-            flops=18 * unit, scalars=1,
-        )
+            [far(maps.shape, BF16), shape((BLOCK, wide), BF16)]
+            + [shape((BLOCK, rows), BF16)] * 2,
+            jnp.stack([core, lax.axis_index("tp")]), *grads,
+            fixed(output_matrix), other_matrix, fixed(qe), fixed(maps),
+            ins=[SCALAR] + [HELD] * feats + [FAR, HELD, FAR, FAR],
+            out_specs=[FAR, HELD, HELD, HELD],
+            scratch=[
+                pltpu.VMEM((feats,) + output_grad.shape[1:], BF16),
+                pltpu.VMEM(output_matrix.shape, BF16),
+                pltpu.VMEM(square, BF16),
+                pltpu.VMEM((blocks, HALF, DK), BF16),
+                dma((2,)),
+                dma(()),
+            ],
+            flops=18 * unit,
+            input_output_aliases={feats + 4: 0},
+        )
+        theirs = lax.ppermute(theirs, "dp", swap)
     with jax.named_scope("send_maps"):
-        maps_in = lax.all_to_all(maps, "ctx", 0, 0, tiled=True)
-        backs_in = lax.all_to_all(backs, "ctx", 0, 0, tiled=True)
+        maps = lax.all_to_all(maps, "ctx", 0, 0, tiled=True)
     with jax.named_scope("chain"):
-        first = lax.dynamic_index_in_dim(
-            initial_state.reshape(blocks, HALF, DK), here, 0, keepdims=False
-        )
-        last = lax.dynamic_index_in_dim(
-            final_state_grad.reshape(blocks, HALF, DK), here, 0, keepdims=False
-        )
         states, = call(
-            chain, [shape((blocks, 2 * HALF, DK), BF16)], maps_in, backs_in, first, last,
+            chain, [far((blocks, 2 * HALF, DK), BF16)],
+            maps, own_half(initial_state), own_half(final_state_grad),
+            out_specs=[FAR],
+            scratch=[pltpu.VMEM((blocks, 2 * HALF, DK), BF16), dma((blocks, 2))],
             flops=4 * unit,
         )
     with jax.named_scope("return_states"):
         states = lax.all_to_all(states, "ctx", 0, 0, tiled=True)
     with jax.named_scope("outputs"):
         heads_low, = call(
-            outputs, [shape((BLOCK, heads * DV), BF16)], qe, o0, states, flops=unit
-        )
+            outputs, [shape((BLOCK, wide), BF16)], qe, o0, states, flops=unit
+        )
+        other_low = lax.ppermute(heads_low, "dp", swap)
     with jax.named_scope("projection"):
-        half = feats // 2
-        mine = lax.dynamic_slice_in_dim(gathered, half * core, half, 0)
-        theirs = lax.dynamic_slice_in_dim(gathered, half * (1 - core), half, 0)
-        theirs = lax.ppermute(theirs, "dp", swap)
-        other_low = lax.ppermute(heads_low, "dp", swap)
-
-        def wide(parts):
-            return jnp.moveaxis(parts, 0, 1).reshape(BLOCK, rows)
-
-        grads = jnp.concatenate([wide(mine), wide(theirs)], axis=0)
-        lows = jnp.concatenate([heads_low, other_low], axis=0)
-        partial = lax.dot_general(grads, lows, TN, preferred_element_type=F32).astype(BF16)
-        pieces = lax.all_to_all(
-            partial.reshape(blocks, rows // blocks, heads * DV), "ctx", 0, 0, tiled=True
-        )
-        piece = jnp.sum(pieces.astype(F32), axis=0)
-        piece = piece * float(BLOCK * blocks * lax.axis_size("dp")) ** (-0.5)
-        spread = jnp.broadcast_to(piece.astype(BF16), (blocks,) + piece.shape)
-        total = lax.all_to_all(spread, "ctx", 0, 0, tiled=True)
-        weight_grad = total.reshape(rows, heads * DV).astype(F32)
+        pieces = (blocks, piece, wide)
+        partial, = call(
+            projection, [far(pieces, BF16)], mine, theirs, heads_low, other_low,
+            out_specs=[FAR], scratch=[pltpu.VMEM(pieces, BF16), dma((4,))], flops=16 * unit,
+        )
+        partial = lax.all_to_all(partial, "ctx", 0, 0, tiled=True)
+        spread, = call(
+            functools.partial(reduce_spread, float(BLOCK * blocks * lax.axis_size("dp")) ** (-0.5)),
+            [far(pieces, BF16)], partial,
+            out_specs=[FAR], scratch=[pltpu.VMEM((piece, wide), BF16), dma((blocks, 2))],
+        )
+        total = lax.all_to_all(spread, "ctx", 0, 0, tiled=True).reshape(rows, wide)
+        weight_grad, = call(
+            widen, [far((rows, wide), F32)], total,
+            out_specs=[FAR], scratch=[pltpu.VMEM((rows, wide), F32), dma((8,))],
+        )
     with jax.named_scope("gradients"):
+        args += (fixed(t), fixed(wm), fixed(u0), head_grad, states)
+        outs = [far(x.shape, x.dtype) for x in args[:5]]
         query_g, key_g, value_g, decay_g, rate_g = call(
-            gradients,
-            [
-                shape(queries.shape, BF16),
-                shape(key_rows.shape, BF16),
-                shape(value_rows.shape, BF16),
-                shape(log_decay.shape, F32),
-                shape(write_rate.shape, F32),
-            ],
-            queries, key_rows, value_rows, log_decay, write_rate,
-            t, wm, u0, head_grad, states,
+            gradients, outs, *args,
+            ins=[whole(a) for a in args], out_specs=[whole(o) for o in outs], grid=(1,),
             flops=17 * unit,
         )
     return (query_g, key_g, value_g, decay_g, rate_g, weight_grad)

time: 148 us -> 134 us (0.905)
  the two profiles are of different devices: /device:TPU:2 before, /device:TPU:0 now
where the time goes in v1:
time: 134 us; the launch traced here: 133 us
  waiting for transfers between devices  49.4 us (37%)
  blocking collectives  32.6 us (24%)
  Pallas kernels  28.2 us (21%)
  starting transfers between devices  21.2 us (16%)
    all_to_all x1, blocking collectives, body(): partial = lax.all_to_all(partial, 'ctx', 0, 0, tiled=True)  32.6 us
    pallas_call x8, Pallas kernels, call(): pl.pallas_call(kernel, grid=grid, out_shape=outs, in_specs=[HELD] * len(a...  28.2 us
    all_to_all x1, waiting for transfers between devices, body(): total = lax.all_to_all(spread, 'ctx', 0, 0, tiled=True).reshape(rows, wide)  21.4 us
    all_to_all x1, waiting for transfers between devices, body(): maps = lax.all_to_all(maps, 'ctx', 0, 0, tiled=True)  16.5 us
    all_to_all x1, waiting for transfers between devices, body(): states = lax.all_to_all(states, 'ctx', 0, 0, tiled=True)  9.96 us
    all_to_all x1, starting transfers between devices, body(): maps = lax.all_to_all(maps, 'ctx', 0, 0, tiled=True)  8.19 us
    ppermute x3, starting transfers between devices, body(): grads.append(lax.ppermute(output_grad, 'tp', pairs))  5.21 us
    all_to_all x1, starting transfers between devices, body(): total = lax.all_to_all(spread, 'ctx', 0, 0, tiled=True).reshape(rows, wide)  3.91 us
  transfers between devices with their start and end apart: 9, of which 4 were waited for; matrix products, arithmetic and copies ran while one was open for 1% of the time, Pallas kernels for 12%

profile of v1, /device:TPU:0, one launch (start us, length us, event | category | flops | bytes accessed | tf_op | source)
XLA Modules:
  0.0 133.2 jit_solution(3806812353005540800)
XLA Ops:
  0.6 0.0 copy-start.2
  0.6 0.1 collective-permute-start.3
  0.7 3.2 %collective-permute-start.1 = (bf16[1,128,512]{2,1,0:T(8,128)(2,1)}, bf16[1,128,512]{2,1,0:T(8,128)(2,1)S(1)}, u32[]{:S(2)}, u32[]{:S(2)}) collective-permute-start(bf16[1,128,512]{2,1,0:T(8,128)(2,1)} %g0_ref.1), channel_id=1, source_target_pairs={{4,0},{6,2},{0,4},{2,6},{5,1},{7,3},{1,5},{3,7},{12,8},{14,10},{8,... | collective-permute-start | bytes 393224 | tf_op jit(solution)/shard_map/gather_grad/ppermute | solution.py:385
  3.9 1.1 collective-permute-start
  5.1 0.9 collective-permute-start.2
  6.0 8.1 %local_maps.1 = (bf16[16,256,128]{2,1,0:T(8,128)(2,1)}, bf16[8,128,128]{2,1,0:T(8,128)(2,1)}, bf16[8,128,128]{2,1,0:T(8,128)(2,1)}, bf16[8,128,128]{2,1,0:T(8,12...) custom-call(bf16[1,128,512]{2,1,0:T(8,128)(2,1)} %q_ref.3, bf16[1,128,512]{2,1,0:T(8,128)(2,1)} %k_ref.3, ...), custom_call_target="tpu_custom_call" | custom-call | flops 1677721600 | bytes 2891776 | tf_op jit(solution)/shard_map/local_maps/pallas_call | solution.py:338
  14.1 0.1 pad_add_fusion.at_ref
  14.1 0.0 collective-permute-done.1.g2_ref
  14.1 0.0 collective-permute-done.g1_ref
  14.1 0.0 collective-permute-done.2.g3_ref
  14.1 0.0 collective-permute-done.3.other_ref
  14.2 0.0 copy-done.2
  14.2 3.6 %head_grads.1 = (bf16[16,256,128]{2,1,0:T(8,128)(2,1)}, bf16[128,1024]{1,0:T(8,128)(2,1)S(1)}, bf16[128,1024]{1,0:T(8,128)(2,1)S(1)}, bf16[128,1024]{1,0:T(8,128)(2,1)S(1)}) custom-call(s32[2]{0:T(128)S(1)} %pad_add_fusion.at_ref, bf16[1,128,512]{2,1,0:T(8,128)(2,1)S(1)} %copy-done.2, ...), custom_call_target="tpu_custom_call", output_to_operand_aliasing={{0}: (8, {})} | custom-call | flops 603979776 | bytes 7864328 | tf_op jit(solution)/shard_map/head_grads/pallas_call | solution.py:338
  17.8 0.0 copy-start
  17.8 0.0 copy-start.1
  17.8 8.2 %all-to-all-start = ((bf16[16,256,128]{2,1,0:T(8,128)(2,1)}), bf16[16,256,128]{2,1,0:T(8,128)(2,1)S(1)}, u32[]{:S(2)}, u32[]{:S(2)}) async-start(bf16[16,256,128]{2,1,0:T(8,128)(2,1)} %get-tuple-element.27), calls=%async_computation | async-start | bytes 2097152 | tf_op jit(solution)/shard_map/send_maps/all_to_all | solution.py:419
  26.0 0.8 dynamic-slice_bitcast_fusion
  26.8 16.5 %all-to-all-done.maps_ref = bf16[16,256,128]{2,1,0:T(8,128)(2,1)S(1)} async-done(((bf16[16,256,128]{2,1,0:T(8,128)(2,1)}), bf16[16,256,128]{2,1,0:T(8,128)(2,1)S(1)}, u32[]{:S(2)}, u32[]{:S(2)}) %all-to-all-start) | async-done | bytes 1048608 | tf_op jit(solution)/shard_map/send_maps/all_to_all | solution.py:419
  43.3 2.9 %chain.1 = bf16[16,128,128]{2,1,0:T(8,128)(2,1)} custom-call(bf16[16,256,128]{2,1,0:T(8,128)(2,1)S(1)} %all-to-all-done.maps_ref, f32[64,128]{1,0:T(8,128)S(1)} %get-tuple-element.37.first_ref, f32[64,128]{1,0:T(8,128)S(1)} %get-tuple-element.36.last_ref), custom_call_target="tpu_custom_call" | custom-call | flops 134217728 | bytes 1638400 | tf_op jit(solution)/shard_map/chain/pallas_call | solution.py:338
  46.2 3.6 %all-to-all-start.1 = ((bf16[16,128,128]{2,1,0:T(8,128)(2,1)}), bf16[16,128,128]{2,1,0:T(8,128)(2,1)S(1)}, u32[]{:S(2)}, u32[]{:S(2)}) async-start(bf16[16,128,128]{2,1,0:T(8,128)(2,1)} %chain.1), calls=%async_computation.1 | async-start | bytes 1048576 | tf_op jit(solution)/shard_map/return_states/all_to_all | solution.py:429
  49.8 0.1 collective-permute-start.4
  49.9 10.0 %all-to-all-done.1.y_ref = bf16[16,128,128]{2,1,0:T(8,128)(2,1)S(1)} async-done(((bf16[16,128,128]{2,1,0:T(8,128)(2,1)}), bf16[16,128,128]{2,1,0:T(8,128)(2,1)S(1)}, u32[]{:S(2)}, u32[]{:S(2)}) %all-to-all-start.1) | async-done | bytes 524320 | tf_op jit(solution)/shard_map/return_states/all_to_all | solution.py:429
  59.9 0.0 copy-done
  59.9 0.0 copy-done.1
  59.9 0.3 outputs.1.low_ref
  60.2 0.1 collective-permute-start.5
  60.3 0.0 collective-permute-done.4.theirs_ref
  60.3 1.5 %collective-permute-done.5.other_ref = bf16[128,1024]{1,0:T(8,128)(2,1)S(1)} collective-permute-done((bf16[128,1024]{1,0:T(8,128)(2,1)S(1)}, bf16[128,1024]{1,0:T(8,128)(2,1)S(1)}, u32[]{:S(2)}, u32[]{:S(2)}) %collective-permute-start.5) | collective-permute-done | bytes 262176 | tf_op jit(solution)/shard_map/outputs/ppermute | solution.py:434
  61.8 2.1 %projection.3 = bf16[16,64,1024]{2,1,0:T(8,128)(2,1)} custom-call(bf16[128,1024]{1,0:T(8,128)(2,1)S(1)} %get-tuple-element.33.mine_ref, bf16[128,1024]{1,0:T(8,128)(2,1)S(1)} %collective-permute-done.4.theirs_ref, bf16[128,1024]{1,0:T(8,128)(2,1)S(1)} %outputs.1.low_ref, bf16[128,1024]{1,0:T(8,128)(2,1)S(1)} %collective-permute-done.5.other_ref), custom_call_target="tpu_custom_call" | custom-call | flops 536870912 | bytes 3145728 | tf_op jit(solution)/shard_map/projection/pallas_call | solution.py:338
  63.9 32.6 %all_to_all.20.pieces_ref = bf16[16,64,1024]{2,1,0:T(8,128)(2,1)S(1)} all-to-all(bf16[16,64,1024]{2,1,0:T(8,128)(2,1)} %projection.3), channel_id=1, replica_groups=mesh['ctx'=16,'tp'=4,'dp'=2] {'ctx'}, dimensions={0} | all-to-all | bytes 4194304 | tf_op jit(solution)/shard_map/projection/all_to_all | solution.py:441
  96.5 1.7 %projection.4 = bf16[16,64,1024]{2,1,0:T(8,128)(2,1)} custom-call(bf16[16,64,1024]{2,1,0:T(8,128)(2,1)S(1)} %all_to_all.20.pieces_ref), custom_call_target="tpu_custom_call" | custom-call | bytes 4194304 | tf_op jit(solution)/shard_map/projection/pallas_call | solution.py:338
  98.2 3.9 %all-to-all-start.3 = ((bf16[16,64,1024]{2,1,0:T(8,128)(2,1)}), bf16[16,64,1024]{2,1,0:T(8,128)(2,1)S(1)}, u32[]{:S(2)}, u32[]{:S(2)}) async-start(bf16[16,64,1024]{2,1,0:T(8,128)(2,1)} %projection.4), calls=%async_computation.3 | async-start | bytes 4194304 | tf_op jit(solution)/shard_map/projection/all_to_all | solution.py:447
  102.1 7.4 %gradients.1 = (bf16[1,128,512]{2,1,0:T(8,128)(2,1)}, bf16[1,128,512]{2,1,0:T(8,128)(2,1)}, bf16[1,128,1024]{2,1,0:T(8,128)(2,1)}, f32[1,8,128]{2,1,0:T(8,128)}, f32[1,8,128]{2,1,0:T(8,128)}) custom-call(bf16[1,128,512]{2,1,0:T(8,128)(2,1)} %q_ref.3, bf16[1,128,512]{2,1,0:T(8,128)(2,1)} %k_ref.3, bf16[1,128,1024]{2,1,0:T(8,128)(2,1)} %v_ref.3, ...), custom_call_target="tpu_custom_call" | custom-call | flops 570425344 | bytes 2637824 | tf_op jit(solution)/shard_map/gradients/pallas_call | solution.py:338
  109.5 21.4 %all-to-all-done.3 = bf16[16,64,1024]{2,1,0:T(8,128)(2,1)S(1)} async-done(((bf16[16,64,1024]{2,1,0:T(8,128)(2,1)}), bf16[16,64,1024]{2,1,0:T(8,128)(2,1)S(1)}, u32[]{:S(2)}, u32[]{:S(2)}) %all-to-all-start.3) | async-done | bytes 2097184 | tf_op jit(solution)/shard_map/projection/all_to_all | solution.py:447
  130.9 2.1 %projection.5 = f32[1024,1024]{1,0:T(8,128)} custom-call(bf16[1024,1024]{1,0:T(8,128)(2,1)S(1)} %bitcast.9), custom_call_target="tpu_custom_call" | custom-call | bytes 6291456 | tf_op jit(solution)/shard_map/projection/pallas_call | solution.py:338
Async XLA Ops:
  0.6 13.5 %copy-start.2 = (bf16[1,128,512]{2,1,0:T(8,128)(2,1)S(1)}, bf16[1,128,512]{2,1,0:T(8,128)(2,1)}, u32[]{:S(2)}) copy-start(bf16[1,128,512]{2,1,0:T(8,128)(2,1)} %g0_ref.1) | copy-start | bytes 393220
  0.6 13.5 %collective-permute-start.3 = (bf16[1024,1024]{1,0:T(8,128)(2,1)}, bf16[1024,1024]{1,0:T(8,128)(2,1)S(1)}, u32[]{:S(2)}, u32[]{:S(2)}) collective-permute-start(bf16[1024,1024]{1,0:T(8,128)(2,1)} %own_hbm.1), channel_id=1, source_target_pairs={{0,1},{1,0},{2,3},{3,2},{4,5},{5,4},{6,7},{7,6},{8,9},{9,8},{10,11... | collective-permute-start | bytes 6291464 | tf_op jit(solution)/shard_map/other_rows/ppermute | solution.py:387
  0.7 13.4 %collective-permute-start.1 = (bf16[1,128,512]{2,1,0:T(8,128)(2,1)}, bf16[1,128,512]{2,1,0:T(8,128)(2,1)S(1)}, u32[]{:S(2)}, u32[]{:S(2)}) collective-permute-start(bf16[1,128,512]{2,1,0:T(8,128)(2,1)} %g0_ref.1), channel_id=1, source_target_pairs={{4,0},{6,2},{0,4},{2,6},{5,1},{7,3},{1,5},{3,7},{12,8},{14,10},{8,... | collective-permute-start | bytes 393224 | tf_op jit(solution)/shard_map/gather_grad/ppermute | solution.py:385
  3.9 10.2 %collective-permute-start = (bf16[1,128,512]{2,1,0:T(8,128)(2,1)}, bf16[1,128,512]{2,1,0:T(8,128)(2,1)S(1)}, u32[]{:S(2)}, u32[]{:S(2)}) collective-permute-start(bf16[1,128,512]{2,1,0:T(8,128)(2,1)} %g0_ref.1), channel_id=1, source_target_pairs={{2,0},{4,2},{6,4},{0,6},{3,1},{5,3},{7,5},{1,7},{10,8},{12,10},{14... | collective-permute-start | bytes 393224 | tf_op jit(solution)/shard_map/gather_grad/ppermute | solution.py:385
  5.1 9.1 %collective-permute-start.2 = (bf16[1,128,512]{2,1,0:T(8,128)(2,1)}, bf16[1,128,512]{2,1,0:T(8,128)(2,1)S(1)}, u32[]{:S(2)}, u32[]{:S(2)}) collective-permute-start(bf16[1,128,512]{2,1,0:T(8,128)(2,1)} %g0_ref.1), channel_id=1, source_target_pairs={{6,0},{0,2},{2,4},{4,6},{7,1},{1,3},{3,5},{5,7},{14,8},{8,10},{10,... | collective-permute-start | bytes 393224 | tf_op jit(solution)/shard_map/gather_grad/ppermute | solution.py:385
  17.8 42.1 %copy-start = (bf16[8,128,128]{2,1,0:T(8,128)(2,1)S(1)}, bf16[8,128,128]{2,1,0:T(8,128)(2,1)}, u32[]{:S(2)}) copy-start(bf16[8,128,128]{2,1,0:T(8,128)(2,1)} %get-tuple-element.24.qe_hbm.qe_ref) | copy-start | bytes 786436
  17.8 42.1 %copy-start.1 = (bf16[8,128,128]{2,1,0:T(8,128)(2,1)S(1)}, bf16[8,128,128]{2,1,0:T(8,128)(2,1)}, u32[]{:S(2)}) copy-start(bf16[8,128,128]{2,1,0:T(8,128)(2,1)} %get-tuple-element.35.o0_ref) | copy-start | bytes 786436
  17.8 25.5 %all-to-all-start = ((bf16[16,256,128]{2,1,0:T(8,128)(2,1)}), bf16[16,256,128]{2,1,0:T(8,128)(2,1)S(1)}, u32[]{:S(2)}, u32[]{:S(2)}) async-start(bf16[16,256,128]{2,1,0:T(8,128)(2,1)} %get-tuple-element.27), calls=%async_computation | async-start | bytes 2097152 | tf_op jit(solution)/shard_map/send_maps/all_to_all | solution.py:419
  46.2 13.7 %all-to-all-start.1 = ((bf16[16,128,128]{2,1,0:T(8,128)(2,1)}), bf16[16,128,128]{2,1,0:T(8,128)(2,1)S(1)}, u32[]{:S(2)}, u32[]{:S(2)}) async-start(bf16[16,128,128]{2,1,0:T(8,128)(2,1)} %chain.1), calls=%async_computation.1 | async-start | bytes 1048576 | tf_op jit(solution)/shard_map/return_states/all_to_all | solution.py:429
  49.8 10.5 %collective-permute-start.4 = (bf16[128,1024]{1,0:T(8,128)(2,1)S(1)}, bf16[128,1024]{1,0:T(8,128)(2,1)S(1)}, u32[]{:S(2)}, u32[]{:S(2)}) collective-permute-start(bf16[128,1024]{1,0:T(8,128)(2,1)S(1)} %get-tuple-element.34), channel_id=1, source_target_pairs={{0,1},{1,0},{2,3},{3,2},{4,5},{5,4},{6,7},{7,6},{8,9},{9,8},{10,11... | collective-permute-start | bytes 786440 | tf_op jit(solution)/shard_map/head_grads/ppermute | solution.py:417
  60.2 1.6 %collective-permute-start.5 = (bf16[128,1024]{1,0:T(8,128)(2,1)S(1)}, bf16[128,1024]{1,0:T(8,128)(2,1)S(1)}, u32[]{:S(2)}, u32[]{:S(2)}) collective-permute-start(bf16[128,1024]{1,0:T(8,128)(2,1)S(1)} %outputs.1.low_ref), channel_id=1, source_target_pairs={{0,1},{1,0},{2,3},{3,2},{4,5},{5,4},{6,7},{7,6},{8,9},{9,8},{10,11... | collective-permute-start | bytes 786440 | tf_op jit(solution)/shard_map/outputs/ppermute | solution.py:434
  98.2 32.7 %all-to-all-start.3 = ((bf16[16,64,1024]{2,1,0:T(8,128)(2,1)}), bf16[16,64,1024]{2,1,0:T(8,128)(2,1)S(1)}, u32[]{:S(2)}, u32[]{:S(2)}) async-start(bf16[16,64,1024]{2,1,0:T(8,128)(2,1)} %projection.4), calls=%async_computation.3 | async-start | bytes 4194304 | tf_op jit(solution)/shard_map/projection/all_to_all | solution.py:447

commit v2 on v1

--- a/solution.py
+++ b/solution.py
@@ -30,10 +30,14 @@
     return high, (a - high.astype(F32)).astype(BF16)
 
 
-def mm3(a, b, dims=NN):
-    (ah, al), (bh, bl) = a, b
-    dot = functools.partial(lax.dot_general, dimension_numbers=dims, preferred_element_type=F32)
-    return dot(ah, bh) + (dot(ah, bl) + dot(al, bh))
+def mm_left(a, b, dims=NN):
+    low = b.astype(BF16)
+    return mm(a[0], low, dims) + mm(a[1], low, dims)
+
+
+def mm_right(a, b, dims=NN):
+    low = a.astype(BF16)
+    return mm(low, b[0], dims) + mm(low, b[1], dims)
 
 
 def exact(a, b):
@@ -75,51 +79,60 @@
         if size == 1:
             found = [ident - a for a in offs]
         else:
-            halves = [split(t) for t in found]
-            inner = [mm3(t, split(a)) for t, a in zip(halves, offs)]
-            found = [t - mm3(split(x), s) for t, x, s in zip(found, inner, halves)]
+            lows = [t.astype(BF16) for t in found]
+            inner = [mm(t, a) for t, a in zip(lows, offs)]
+            found = [t - mm(x, s) for t, x, s in zip(found, inner, lows)]
         size *= 2
-    return found
-
-
-def local_maps(q_ref, k_ref, v_ref, g_ref, b_ref, pay_ref, t_ref, wm_ref, u0_ref, qe_ref, o0_ref):
-    heads = g_ref.shape[1]
-    copies = heads * DK // q_ref.shape[2]
-    row, col = iotas()
-    strict = row > col
-    ident = (row == col).astype(F32)
-    cumul, columns, growth, weight, ends = gate_columns(g_ref[0], row, col)
-    betas = b_ref[0].T
-    qhat, khat, pair_k, pair_q = [], [], [], []
-    for j in range(heads // copies):
-        cut = slice(j * DK, (j + 1) * DK)
-        qn = unit_rows(q_ref[0, :, cut].astype(F32))[0] * QSCALE
-        kn = unit_rows(k_ref[0, :, cut].astype(F32))[0]
-        qhat.append(qn)
-        khat.append(kn)
-        pair_k.append(mm(kn, kn, NT))
-        pair_q.append(mm(qn, kn, NT))
-    decay = [decays(cumul, columns, h, strict) for h in range(heads)]
-    beta = [betas[:, h : h + 1] for h in range(heads)]
-    parts = [beta[h] * pair_k[h // copies] * decay[h] for h in range(heads)]
-    inverse = unit_lower_inverses(parts, row, col)
-    for h in range(heads):
-        j = h // copies
-        grow = growth[:, h : h + 1]
+    lows = [t.astype(BF16) for t in found]
+    rest = [ident - (t.astype(F32) + mm_left(split(a), t)) for t, a in zip(lows, parts)]
+    return [t.astype(F32) + mm(t, r) for t, r in zip(lows, rest)]
+
+
+class Heads:
+    def __init__(self, q_ref, k_ref, g_ref, b_ref):
+        self.count = g_ref.shape[1]
+        self.copies = self.count * DK // q_ref.shape[2]
+        self.row, self.col = iotas()
+        self.ident = (self.row == self.col).astype(F32)
+        strict = self.row > self.col
+        cumul, columns, growth, weight, ends = gate_columns(g_ref[0], self.row, self.col)
+        betas = b_ref[0].T
+        one = [slice(h, h + 1) for h in range(self.count)]
+        self.decay = [decays(cumul, columns, h, strict) for h in range(self.count)]
+        self.beta, self.grow, self.keep, self.end = (
+            [x[:, cut] for cut in one] for x in (betas, growth, weight, ends)
+        )
+        self.qn, self.q_scale, self.khat, self.k_scale = [], [], [], []
+        self.pair_k, self.pair_q = [], []
+        for j in range(self.count // self.copies):
+            cut = slice(j * DK, (j + 1) * DK)
+            qn, q_scale = unit_rows(q_ref[0, :, cut].astype(F32))
+            khat, k_scale = unit_rows(k_ref[0, :, cut].astype(F32))
+            self.qn.append(qn)
+            self.q_scale.append(q_scale)
+            self.khat.append(khat)
+            self.k_scale.append(k_scale)
+            self.pair_k.append(mm(khat, khat, NT))
+            self.pair_q.append(mm(qn * QSCALE, khat, NT))
+        parts = [
+            self.beta[h] * self.pair_k[h // self.copies] * self.decay[h] for h in range(self.count)
+        ]
+        self.inverse = [split(t) for t in unit_lower_inverses(parts, self.row, self.col)]
+
+
+def local_maps(q_ref, k_ref, v_ref, g_ref, b_ref, pay_ref, qe_ref, o0_ref):
+    x = Heads(q_ref, k_ref, g_ref, b_ref)
+    for h in range(x.count):
+        j = h // x.copies
         value = v_ref[0, :, h * DV : (h + 1) * DV].astype(F32)
-        t = split(inverse[h])
-        wm = mm3(t, split((beta[h] * grow) * khat[j]))
-        u0 = mm3(t, split(beta[h] * value))
-        kw = split(weight[:, h : h + 1] * khat[j])
-        step = ends[:, h : h + 1] * ident - mm3(split(wm), kw, TN)
-        write = mm3(split(u0), kw, TN).astype(BF16)
-        scores = pair_q[j] * (decay[h] + ident)
-        t_ref[h] = t[0]
-        wm_ref[h] = wm.astype(BF16)
-        u0_ref[h] = u0.astype(BF16)
-        qe_ref[h] = (grow * qhat[j] - mm(scores, wm)).astype(BF16)
+        wm = mm_left(x.inverse[h], (x.beta[h] * x.grow[h]) * x.khat[j])
+        u0 = mm_left(x.inverse[h], x.beta[h] * value)
+        kw = split(x.keep[h] * x.khat[j])
+        step = (x.end[h] * x.ident - mm_right(wm, kw, TN)).astype(BF16)
+        write = mm_right(u0, kw, TN).astype(BF16)
+        scores = x.pair_q[j] * (x.decay[h] + x.ident)
+        qe_ref[h] = (x.grow[h] * (x.qn[j] * QSCALE) - mm(scores, wm)).astype(BF16)
         o0_ref[h] = mm(scores, u0).astype(BF16)
-        step = step.astype(BF16)
         for half in range(2):
             pay_ref[2 * h + half, 0:DK] = step
             pay_ref[2 * h + half, DK : DK + HALF] = write[half * HALF : (half + 1) * HALF]
@@ -252,44 +265,36 @@
 
 
 def gradients(
-    q_ref, k_ref, v_ref, g_ref, b_ref, t_ref, wm_ref, u0_ref, hg_ref, y_ref,
+    q_ref, k_ref, v_ref, g_ref, b_ref, hg_ref, y_ref,
     dq_ref, dk_ref, dv_ref, dg_ref, db_ref,
 ):
-    heads = g_ref.shape[1]
-    copies = heads * DK // q_ref.shape[2]
-    row, col = iotas()
+    x = Heads(q_ref, k_ref, g_ref, b_ref)
+    row, col = x.row, x.col
     strict = row > col
-    incl = row >= col
-    ident = (row == col).astype(F32)
-    cumul, columns, growth, weight, ends = gate_columns(g_ref[0], row, col)
-    betas = b_ref[0].T
-    lane = lax.broadcasted_iota(jnp.int32, (BLOCK, heads), 1)
-    level = lax.broadcasted_iota(jnp.int32, (heads, BLOCK), 0)
-    cumul_g = jnp.zeros((BLOCK, heads), F32)
-    beta_g = jnp.zeros((BLOCK, heads), F32)
-    across = jnp.zeros((heads, BLOCK), F32)
-    for j in range(heads // copies):
+    lane = lax.broadcasted_iota(jnp.int32, (BLOCK, x.count), 1)
+    level = lax.broadcasted_iota(jnp.int32, (x.count, BLOCK), 0)
+    cumul_g = jnp.zeros((BLOCK, x.count), F32)
+    beta_g = jnp.zeros((BLOCK, x.count), F32)
+    across = jnp.zeros((x.count, BLOCK), F32)
+    for j in range(x.count // x.copies):
         cut = slice(j * DK, (j + 1) * DK)
-        qn, q_scale = unit_rows(q_ref[0, :, cut].astype(F32))
-        khat, k_scale = unit_rows(k_ref[0, :, cut].astype(F32))
+        qn, khat = x.qn[j], x.khat[j]
         qhat = qn * QSCALE
         qlow, klow = qhat.astype(BF16), khat.astype(BF16)
-        pair_k = mm(klow, klow, NT)
-        pair_q = mm(qlow, klow, NT)
+        pair_k, pair_q = x.pair_k[j], x.pair_q[j]
         qhat_g = jnp.zeros((BLOCK, DK), F32)
         khat_g = jnp.zeros((BLOCK, DK), F32)
-        for h in range(j * copies, (j + 1) * copies):
+        for h in range(j * x.copies, (j + 1) * x.copies):
             cut_v = slice(h * DV, (h + 1) * DV)
-            decay = decays(cumul, columns, h, strict)
-            grow, keep, beta = growth[:, h : h + 1], weight[:, h : h + 1], betas[:, h : h + 1]
+            decay, grow, keep, beta = x.decay[h], x.grow[h], x.keep[h], x.beta[h]
             value = v_ref[0, :, cut_v].astype(F32)
             state, back = halves_of(y_ref, h, 0), halves_of(y_ref, h, HALF)
             out_g = hg_ref[:, cut_v]
-            decay_in = decay + ident
+            decay_in = decay + x.ident
             scores = pair_q * decay_in
-            fresh = (u0_ref[h].astype(F32) - mm(wm_ref[h], state, NT)).astype(BF16)
+            fresh = mm_left(x.inverse[h], beta * (value - grow * mm(klow, state, NT))).astype(BF16)
             fresh_g = mm(scores, out_g, TN) + mm(keep * khat, back, NT)
-            rhs_g = mm(t_ref[h], fresh_g, TN)
+            rhs_g = mm(x.inverse[h][0], fresh_g, TN)
             rhs_low = rhs_g.astype(BF16)
             read_q = mm(out_g, state)
             read_k = mm(rhs_low, state)
@@ -310,7 +315,7 @@
             kept_sum = jnp.sum(kept_g * khat, axis=1, keepdims=True) * keep
             grow_g = jnp.sum(read_q * qhat, axis=1, keepdims=True) - beta * read_sum
             cumul_col = grow_g * grow + jnp.sum(gaps, axis=1, keepdims=True) - kept_sum
-            whole = jnp.sum(back.astype(F32) * state.astype(F32)) * ends[:, h : h + 1]
+            whole = jnp.sum(back.astype(F32) * state.astype(F32)) * x.end[h]
             at_end = jnp.sum(kept_sum, axis=0, keepdims=True) + whole
             cumul_col += jnp.where(row[:, 0:1] == BLOCK - 1, at_end, 0.0)
             cumul_g = jnp.where(lane == h, cumul_col, cumul_g)
@@ -318,10 +323,30 @@
             across = jnp.where(level == h, jnp.sum(gaps, axis=0, keepdims=True), across)
         q_along = jnp.sum(qn * qhat_g, axis=1, keepdims=True)
         k_along = jnp.sum(khat * khat_g, axis=1, keepdims=True)
-        dq_ref[0, :, cut] = ((q_scale * QSCALE) * (qhat_g - qn * q_along)).astype(BF16)
-        dk_ref[0, :, cut] = (k_scale * (khat_g - khat * k_along)).astype(BF16)
+        dq_ref[0, :, cut] = ((x.q_scale[j] * QSCALE) * (qhat_g - qn * q_along)).astype(BF16)
+        dk_ref[0, :, cut] = (x.k_scale[j] * (khat_g - khat * k_along)).astype(BF16)
     db_ref[0] = beta_g.T
     dg_ref[0] = exact(cumul_g.T - across, (row >= col).astype(F32))
+
+
+def gradients_on(turn, at_ref, *refs):
+    *held, sems = refs[-13:]
+    far_in = refs[:7]
+    far_out = refs[7 + (1 if turn else 6) :][:5]
+
+    @pl.when(at_ref[0] == turn)
+    def _():
+        fetches = [pltpu.make_async_copy(far_in[i], held[i], sems.at[i]) for i in range(7)]
+        for copy in fetches:
+            copy.start()
+        for copy in fetches:
+            copy.wait()
+        gradients(*held)
+        puts = [pltpu.make_async_copy(held[7 + i], far_out[i], sems.at[7 + i]) for i in range(5)]
+        for copy in puts:
+            copy.start()
+        for copy in puts:
+            copy.wait()
 
 
 def whole(x):
@@ -388,8 +413,8 @@
     dma = pltpu.SemaphoreType.DMA
     with jax.named_scope("local_maps"):
         args = tuple(map(fixed, (queries, key_rows, value_rows, log_decay, write_rate)))
-        outs = [far((blocks, 2 * DK, DK), BF16)] + [far(square, BF16)] * 5
-        maps, t, wm, u0, qe, o0 = call(
+        outs = [far((blocks, 2 * DK, DK), BF16)] + [far(square, BF16)] * 2
+        maps, qe, o0 = call(
             local_maps, outs, *args,
             ins=[whole(a) for a in args], out_specs=[whole(o) for o in outs], grid=(1,),
             flops=50 * unit,
@@ -438,6 +463,17 @@
             projection, [far(pieces, BF16)], mine, theirs, heads_low, other_low,
             out_specs=[FAR], scratch=[pltpu.VMEM(pieces, BF16), dma((4,))], flops=16 * unit,
         )
+    with jax.named_scope("gradients"):
+        args += (head_grad, states)
+        outs = [far(x.shape, x.dtype) for x in args[:5]]
+        held = [pltpu.VMEM(x.shape, x.dtype) for x in args + args[:5]] + [dma((12,))]
+        *found, partial = call(
+            functools.partial(gradients_on, 1), outs + [far(pieces, BF16)],
+            core.reshape(1), *args, fixed(partial),
+            ins=[SCALAR] + [FAR] * 8, out_specs=[FAR] * 6, scratch=held, flops=35 * unit,
+            input_output_aliases={8: 5},
+        )
+    with jax.named_scope("projection"):
         partial = lax.all_to_all(partial, "ctx", 0, 0, tiled=True)
         spread, = call(
             functools.partial(reduce_spread, float(BLOCK * blocks * lax.axis_size("dp")) ** (-0.5)),
@@ -450,12 +486,11 @@
             out_specs=[FAR], scratch=[pltpu.VMEM((rows, wide), F32), dma((8,))],
         )
     with jax.named_scope("gradients"):
-        args += (fixed(t), fixed(wm), fixed(u0), head_grad, states)
-        outs = [far(x.shape, x.dtype) for x in args[:5]]
         query_g, key_g, value_g, decay_g, rate_g = call(
-            gradients, outs, *args,
-            ins=[whole(a) for a in args], out_specs=[whole(o) for o in outs], grid=(1,),
-            flops=17 * unit,
+            functools.partial(gradients_on, 0), outs,
+            core.reshape(1), *args, fixed(spread), *map(fixed, found),
+            ins=[SCALAR] + [FAR] * 13, out_specs=[FAR] * 5, scratch=held, flops=35 * unit,
+            input_output_aliases={9 + i: i for i in range(5)},
         )
     return (query_g, key_g, value_g, decay_g, rate_g, weight_grad)
 

time: 134 us -> 128 us (0.955)
  the two profiles are of different devices: /device:TPU:0 before, /device:TPU:1 now
where the time goes in v2:
time: 128 us; the launch traced here: 127 us
  waiting for transfers between devices  43.4 us (34%)
  Pallas kernels  29.5 us (23%)
  starting transfers between devices  28.4 us (22%)
  blocking collectives  24.1 us (19%)
    pallas_call x9, Pallas kernels, call(): pl.pallas_call(kernel, grid=grid, out_shape=outs, in_specs=[HELD] * len(a...  29.5 us
    all_to_all x1, blocking collectives, body(): partial = lax.all_to_all(partial, 'ctx', 0, 0, tiled=True)  24.1 us
    all_to_all x1, waiting for transfers between devices, body(): total = lax.all_to_all(spread, 'ctx', 0, 0, tiled=True).reshape(rows, wide)  21.7 us
    all_to_all x1, waiting for transfers between devices, body(): maps = lax.all_to_all(maps, 'ctx', 0, 0, tiled=True)  14.5 us
    all_to_all x1, starting transfers between devices, body(): maps = lax.all_to_all(maps, 'ctx', 0, 0, tiled=True)  7.91 us
    all_to_all x1, waiting for transfers between devices, body(): states = lax.all_to_all(states, 'ctx', 0, 0, tiled=True)  6.05 us
    ppermute x3, starting transfers between devices, body(): grads.append(lax.ppermute(output_grad, 'tp', pairs))  4.31 us
    ppermute x1, starting transfers between devices, body(): other_low = lax.ppermute(heads_low, 'dp', swap)  4.01 us
  transfers between devices with their start and end apart: 9, of which 4 were waited for; matrix products, arithmetic and copies ran while one was open for 1% of the time, Pallas kernels for 6%

profile of v2, /device:TPU:1, one launch (start us, length us, event | category | flops | bytes accessed | tf_op | source)
XLA Modules:
  0.0 127.2 jit_solution(417291604097079682)
XLA Ops:
  0.6 0.0 copy-start.2
  0.6 1.5 %collective-permute-start.3 = (bf16[1024,1024]{1,0:T(8,128)(2,1)}, bf16[1024,1024]{1,0:T(8,128)(2,1)S(1)}, u32[]{:S(2)}, u32[]{:S(2)}) collective-permute-start(bf16[1024,1024]{1,0:T(8,128)(2,1)} %own_hbm.1), channel_id=1, source_target_pairs={{0,1},{1,0},{2,3},{3,2},{4,5},{5,4},{6,7},{7,6},{8,9},{9,8},{10,11... | collective-permute-start | bytes 6291464 | tf_op jit(solution)/shard_map/other_rows/ppermute | solution.py:412
  2.1 2.8 %collective-permute-start.1 = (bf16[1,128,512]{2,1,0:T(8,128)(2,1)}, bf16[1,128,512]{2,1,0:T(8,128)(2,1)S(1)}, u32[]{:S(2)}, u32[]{:S(2)}) collective-permute-start(bf16[1,128,512]{2,1,0:T(8,128)(2,1)} %g0_ref.1), channel_id=1, source_target_pairs={{4,0},{6,2},{0,4},{2,6},{5,1},{7,3},{1,5},{3,7},{12,8},{14,10},{8,... | collective-permute-start | bytes 393224 | tf_op jit(solution)/shard_map/gather_grad/ppermute | solution.py:410
  5.0 0.9 collective-permute-start
  5.8 0.6 collective-permute-start.2
  6.5 7.1 %local_maps.1 = (bf16[16,256,128]{2,1,0:T(8,128)(2,1)}, bf16[8,128,128]{2,1,0:T(8,128)(2,1)}, bf16[8,128,128]{2,1,0:T(8,128)(2,1)}) custom-call(bf16[1,128,512]{2,1,0:T(8,128)(2,1)} %refs_0_.3, bf16[1,128,512]{2,1,0:T(8,128)(2,1)} %refs_1_.3, bf16[1,128,1024]{2,1,0:T(8,128)(2,1)} %refs_2_.3, f32[1,8,128]{2,1,0:T(8,128)} %refs_3_.3, f32[1,8,128]{2,1,0:T(8,128)} %refs_4_.3), custom_call_target="tpu_custom_call" | custom-call | flops 1677721600 | bytes 2105344 | tf_op jit(solution)/shard_map/local_maps/pallas_call | solution.py:363
  13.5 0.1 pad_add_fusion.at_ref
  13.6 0.0 collective-permute-done.1.g2_ref
  13.6 0.0 collective-permute-done.g1_ref
  13.6 0.0 collective-permute-done.2.g3_ref
  13.6 0.0 collective-permute-done.3.other_ref
  13.6 0.0 copy-done.2
  13.6 3.6 %head_grads.1 = (bf16[16,256,128]{2,1,0:T(8,128)(2,1)}, bf16[128,1024]{1,0:T(8,128)(2,1)S(1)}, bf16[128,1024]{1,0:T(8,128)(2,1)S(1)}, bf16[128,1024]{1,0:T(8,128)(2,1)S(1)}) custom-call(s32[2]{0:T(128)S(1)} %pad_add_fusion.at_ref, bf16[1,128,512]{2,1,0:T(8,128)(2,1)S(1)} %copy-done.2, ...), custom_call_target="tpu_custom_call", output_to_operand_aliasing={{0}: (8, {})} | custom-call | flops 603979776 | bytes 7864328 | tf_op jit(solution)/shard_map/head_grads/pallas_call | solution.py:363
  17.3 0.0 copy-start
  17.3 0.0 copy-start.1
  17.3 7.9 %all-to-all-start = ((bf16[16,256,128]{2,1,0:T(8,128)(2,1)}), bf16[16,256,128]{2,1,0:T(8,128)(2,1)S(1)}, u32[]{:S(2)}, u32[]{:S(2)}) async-start(bf16[16,256,128]{2,1,0:T(8,128)(2,1)} %get-tuple-element.27), calls=%async_computation | async-start | bytes 2097152 | tf_op jit(solution)/shard_map/send_maps/all_to_all | solution.py:444
  25.2 0.8 dynamic-slice_bitcast_fusion
  26.0 14.5 %all-to-all-done.maps_ref = bf16[16,256,128]{2,1,0:T(8,128)(2,1)S(1)} async-done(((bf16[16,256,128]{2,1,0:T(8,128)(2,1)}), bf16[16,256,128]{2,1,0:T(8,128)(2,1)S(1)}, u32[]{:S(2)}, u32[]{:S(2)}) %all-to-all-start) | async-done | bytes 1048608 | tf_op jit(solution)/shard_map/send_maps/all_to_all | solution.py:444
  40.5 2.9 %chain.1 = bf16[16,128,128]{2,1,0:T(8,128)(2,1)} custom-call(bf16[16,256,128]{2,1,0:T(8,128)(2,1)S(1)} %all-to-all-done.maps_ref, f32[64,128]{1,0:T(8,128)S(1)} %get-tuple-element.43.first_ref, f32[64,128]{1,0:T(8,128)S(1)} %get-tuple-element.42.last_ref), custom_call_target="tpu_custom_call" | custom-call | flops 134217728 | bytes 1638400 | tf_op jit(solution)/shard_map/chain/pallas_call | solution.py:363
  43.4 3.9 %all-to-all-start.1 = ((bf16[16,128,128]{2,1,0:T(8,128)(2,1)}), bf16[16,128,128]{2,1,0:T(8,128)(2,1)S(1)}, u32[]{:S(2)}, u32[]{:S(2)}) async-start(bf16[16,128,128]{2,1,0:T(8,128)(2,1)} %chain.1), calls=%async_computation.1 | async-start | bytes 1048576 | tf_op jit(solution)/shard_map/return_states/all_to_all | solution.py:454
  47.3 3.0 %collective-permute-start.4 = (bf16[128,1024]{1,0:T(8,128)(2,1)S(1)}, bf16[128,1024]{1,0:T(8,128)(2,1)S(1)}, u32[]{:S(2)}, u32[]{:S(2)}) collective-permute-start(bf16[128,1024]{1,0:T(8,128)(2,1)S(1)} %get-tuple-element.29), channel_id=1, source_target_pairs={{0,1},{1,0},{2,3},{3,2},{4,5},{5,4},{6,7},{7,6},{8,9},{9,8},{10,11... | collective-permute-start | bytes 786440 | tf_op jit(solution)/shard_map/head_grads/ppermute | solution.py:442
  50.3 6.0 %all-to-all-done.1.y_ref.refs_6_ = bf16[16,128,128]{2,1,0:T(8,128)(2,1)S(1)} async-done(((bf16[16,128,128]{2,1,0:T(8,128)(2,1)}), bf16[16,128,128]{2,1,0:T(8,128)(2,1)S(1)}, u32[]{:S(2)}, u32[]{:S(2)}) %all-to-all-start.1) | async-done | bytes 524320 | tf_op jit(solution)/shard_map/return_states/all_to_all | solution.py:454
  56.3 0.0 copy-done
  56.3 0.0 copy-done.1
  56.3 0.3 outputs.1.low_ref
  56.6 4.0 %collective-permute-start.5 = (bf16[128,1024]{1,0:T(8,128)(2,1)S(1)}, bf16[128,1024]{1,0:T(8,128)(2,1)S(1)}, u32[]{:S(2)}, u32[]{:S(2)}) collective-permute-start(bf16[128,1024]{1,0:T(8,128)(2,1)S(1)} %outputs.1.low_ref), channel_id=1, source_target_pairs={{0,1},{1,0},{2,3},{3,2},{4,5},{5,4},{6,7},{7,6},{8,9},{9,8},{10,11... | collective-permute-start | bytes 786440 | tf_op jit(solution)/shard_map/outputs/ppermute | solution.py:459
  60.7 0.0 collective-permute-done.4.theirs_ref
  60.7 1.2 collective-permute-done.5.other_ref
  61.8 2.1 %projection.3.refs_7_ = bf16[16,64,1024]{2,1,0:T(8,128)(2,1)} custom-call(bf16[128,1024]{1,0:T(8,128)(2,1)S(1)} %get-tuple-element.28.mine_ref, bf16[128,1024]{1,0:T(8,128)(2,1)S(1)} %collective-permute-done.4.theirs_ref, bf16[128,1024]{1,0:T(8,128)(2,1)S(1)} %outputs.1.low_ref, bf16[128,1024]{1,0:T(8,128)(2,1)S(1)} %collective-permute-done.5.other_ref), custom_call_target="tpu_custom_call" | custom-call | flops 536870912 | bytes 3145728 | tf_op jit(solution)/shard_map/projection/pallas_call | solution.py:363
  63.9 9.4 %gradients.2 = (bf16[1,128,512]{2,1,0:T(8,128)(2,1)}, bf16[1,128,512]{2,1,0:T(8,128)(2,1)}, bf16[1,128,1024]{2,1,0:T(8,128)(2,1)}, f32[1,8,128]{2,1,0:T(8,128)},...) custom-call(s32[1]{0:T(128)} %bitcast.at_ref, ...), custom_call_target="tpu_custom_call", output_to_operand_aliasing={{5}: (8, {})} | custom-call | flops 1174405120 | bytes 6045700 | tf_op jit(solution)/shard_map/gradients/pallas_call | solution.py:363
  73.3 24.1 %all_to_all.20.pieces_ref = bf16[16,64,1024]{2,1,0:T(8,128)(2,1)S(1)} all-to-all(bf16[16,64,1024]{2,1,0:T(8,128)(2,1)} %get-tuple-element.31), channel_id=1, replica_groups=mesh['ctx'=16,'tp'=4,'dp'=2] {'ctx'}, dimensions={0} | all-to-all | bytes 4194304 | tf_op jit(solution)/shard_map/projection/all_to_all | solution.py:477
  97.4 1.7 %projection.4.refs_7_ = bf16[16,64,1024]{2,1,0:T(8,128)(2,1)} custom-call(bf16[16,64,1024]{2,1,0:T(8,128)(2,1)S(1)} %all_to_all.20.pieces_ref), custom_call_target="tpu_custom_call" | custom-call | bytes 4194304 | tf_op jit(solution)/shard_map/projection/pallas_call | solution.py:363
  99.1 3.7 %all-to-all-start.3 = ((bf16[16,64,1024]{2,1,0:T(8,128)(2,1)}), bf16[16,64,1024]{2,1,0:T(8,128)(2,1)S(1)}, u32[]{:S(2)}, u32[]{:S(2)}) async-start(bf16[16,64,1024]{2,1,0:T(8,128)(2,1)} %projection.4.refs_7_), calls=%async_computation.3 | async-start | bytes 4194304 | tf_op jit(solution)/shard_map/projection/all_to_all | solution.py:483
  102.8 0.3 gradients.3
  103.2 21.7 %all-to-all-done.3 = bf16[16,64,1024]{2,1,0:T(8,128)(2,1)S(1)} async-done(((bf16[16,64,1024]{2,1,0:T(8,128)(2,1)}), bf16[16,64,1024]{2,1,0:T(8,128)(2,1)S(1)}, u32[]{:S(2)}, u32[]{:S(2)}) %all-to-all-start.3) | async-done | bytes 2097184 | tf_op jit(solution)/shard_map/projection/all_to_all | solution.py:483
  124.9 2.1 %projection.5 = f32[1024,1024]{1,0:T(8,128)} custom-call(bf16[1024,1024]{1,0:T(8,128)(2,1)S(1)} %bitcast.9), custom_call_target="tpu_custom_call" | custom-call | bytes 6291456 | tf_op jit(solution)/shard_map/projection/pallas_call | solution.py:363
Async XLA Ops:
  0.6 13.0 %copy-start.2 = (bf16[1,128,512]{2,1,0:T(8,128)(2,1)S(1)}, bf16[1,128,512]{2,1,0:T(8,128)(2,1)}, u32[]{:S(2)}) copy-start(bf16[1,128,512]{2,1,0:T(8,128)(2,1)} %g0_ref.1) | copy-start | bytes 393220
  0.6 13.0 %collective-permute-start.3 = (bf16[1024,1024]{1,0:T(8,128)(2,1)}, bf16[1024,1024]{1,0:T(8,128)(2,1)S(1)}, u32[]{:S(2)}, u32[]{:S(2)}) collective-permute-start(bf16[1024,1024]{1,0:T(8,128)(2,1)} %own_hbm.1), channel_id=1, source_target_pairs={{0,1},{1,0},{2,3},{3,2},{4,5},{5,4},{6,7},{7,6},{8,9},{9,8},{10,11... | collective-permute-start | bytes 6291464 | tf_op jit(solution)/shard_map/other_rows/ppermute | solution.py:412
  2.1 11.5 %collective-permute-start.1 = (bf16[1,128,512]{2,1,0:T(8,128)(2,1)}, bf16[1,128,512]{2,1,0:T(8,128)(2,1)S(1)}, u32[]{:S(2)}, u32[]{:S(2)}) collective-permute-start(bf16[1,128,512]{2,1,0:T(8,128)(2,1)} %g0_ref.1), channel_id=1, source_target_pairs={{4,0},{6,2},{0,4},{2,6},{5,1},{7,3},{1,5},{3,7},{12,8},{14,10},{8,... | collective-permute-start | bytes 393224 | tf_op jit(solution)/shard_map/gather_grad/ppermute | solution.py:410
  5.0 8.6 %collective-permute-start = (bf16[1,128,512]{2,1,0:T(8,128)(2,1)}, bf16[1,128,512]{2,1,0:T(8,128)(2,1)S(1)}, u32[]{:S(2)}, u32[]{:S(2)}) collective-permute-start(bf16[1,128,512]{2,1,0:T(8,128)(2,1)} %g0_ref.1), channel_id=1, source_target_pairs={{2,0},{4,2},{6,4},{0,6},{3,1},{5,3},{7,5},{1,7},{10,8},{12,10},{14... | collective-permute-start | bytes 393224 | tf_op jit(solution)/shard_map/gather_grad/ppermute | solution.py:410
  5.8 7.8 %collective-permute-start.2 = (bf16[1,128,512]{2,1,0:T(8,128)(2,1)}, bf16[1,128,512]{2,1,0:T(8,128)(2,1)S(1)}, u32[]{:S(2)}, u32[]{:S(2)}) collective-permute-start(bf16[1,128,512]{2,1,0:T(8,128)(2,1)} %g0_ref.1), channel_id=1, source_target_pairs={{6,0},{0,2},{2,4},{4,6},{7,1},{1,3},{3,5},{5,7},{14,8},{8,10},{10,... | collective-permute-start | bytes 393224 | tf_op jit(solution)/shard_map/gather_grad/ppermute | solution.py:410
  17.3 39.1 %copy-start = (bf16[8,128,128]{2,1,0:T(8,128)(2,1)S(1)}, bf16[8,128,128]{2,1,0:T(8,128)(2,1)}, u32[]{:S(2)}) copy-start(bf16[8,128,128]{2,1,0:T(8,128)(2,1)} %get-tuple-element.24.qe_hbm.qe_ref) | copy-start | bytes 786436
  17.3 39.1 %copy-start.1 = (bf16[8,128,128]{2,1,0:T(8,128)(2,1)S(1)}, bf16[8,128,128]{2,1,0:T(8,128)(2,1)}, u32[]{:S(2)}) copy-start(bf16[8,128,128]{2,1,0:T(8,128)(2,1)} %get-tuple-element.30.o0_ref) | copy-start | bytes 786436
  17.3 23.2 %all-to-all-start = ((bf16[16,256,128]{2,1,0:T(8,128)(2,1)}), bf16[16,256,128]{2,1,0:T(8,128)(2,1)S(1)}, u32[]{:S(2)}, u32[]{:S(2)}) async-start(bf16[16,256,128]{2,1,0:T(8,128)(2,1)} %get-tuple-element.27), calls=%async_computation | async-start | bytes 2097152 | tf_op jit(solution)/shard_map/send_maps/all_to_all | solution.py:444
  43.4 13.0 %all-to-all-start.1 = ((bf16[16,128,128]{2,1,0:T(8,128)(2,1)}), bf16[16,128,128]{2,1,0:T(8,128)(2,1)S(1)}, u32[]{:S(2)}, u32[]{:S(2)}) async-start(bf16[16,128,128]{2,1,0:T(8,128)(2,1)} %chain.1), calls=%async_computation.1 | async-start | bytes 1048576 | tf_op jit(solution)/shard_map/return_states/all_to_all | solution.py:454
  47.3 13.3 %collective-permute-start.4 = (bf16[128,1024]{1,0:T(8,128)(2,1)S(1)}, bf16[128,1024]{1,0:T(8,128)(2,1)S(1)}, u32[]{:S(2)}, u32[]{:S(2)}) collective-permute-start(bf16[128,1024]{1,0:T(8,128)(2,1)S(1)} %get-tuple-element.29), channel_id=1, source_target_pairs={{0,1},{1,0},{2,3},{3,2},{4,5},{5,4},{6,7},{7,6},{8,9},{9,8},{10,11... | collective-permute-start | bytes 786440 | tf_op jit(solution)/shard_map/head_grads/ppermute | solution.py:442
  56.6 5.2 %collective-permute-start.5 = (bf16[128,1024]{1,0:T(8,128)(2,1)S(1)}, bf16[128,1024]{1,0:T(8,128)(2,1)S(1)}, u32[]{:S(2)}, u32[]{:S(2)}) collective-permute-start(bf16[128,1024]{1,0:T(8,128)(2,1)S(1)} %outputs.1.low_ref), channel_id=1, source_target_pairs={{0,1},{1,0},{2,3},{3,2},{4,5},{5,4},{6,7},{7,6},{8,9},{9,8},{10,11... | collective-permute-start | bytes 786440 | tf_op jit(solution)/shard_map/outputs/ppermute | solution.py:459
  99.1 25.8 %all-to-all-start.3 = ((bf16[16,64,1024]{2,1,0:T(8,128)(2,1)}), bf16[16,64,1024]{2,1,0:T(8,128)(2,1)S(1)}, u32[]{:S(2)}, u32[]{:S(2)}) async-start(bf16[16,64,1024]{2,1,0:T(8,128)(2,1)} %projection.4.refs_7_), calls=%async_computation.3 | async-start | bytes 4194304 | tf_op jit(solution)/shard_map/projection/all_to_all | solution.py:483

commit v3 on v2

--- a/solution.py
+++ b/solution.py
@@ -28,6 +28,10 @@
 def split(a):
     high = a.astype(BF16)
     return high, (a - high.astype(F32)).astype(BF16)
+
+
+def mm3(a, b, dims=NN):
+    return mm(a[0], b[0], dims) + (mm(a[0], b[1], dims) + mm(a[1], b[0], dims))
 
 
 def mm_left(a, b, dims=NN):
@@ -140,7 +144,7 @@
 
 def head_grads(
     at_ref, g0_ref, g1_ref, g2_ref, g3_ref, own_hbm, other_ref, qe_hbm, pay_in,
-    pay_ref, hg_ref, mine_ref, theirs_ref, all_ref, own_ref, qe_ref, back_ref, in_sems, out_sem,
+    pay_ref, hg_ref, mine_ref, theirs_ref, all_ref, own_ref, qe_ref, back_ref, in_sems, out_sems,
 ):
     fetch = pltpu.make_async_copy(own_hbm, own_ref, in_sems.at[0])
     fetch_qe = pltpu.make_async_copy(qe_hbm, qe_ref, in_sems.at[1])
@@ -166,13 +170,20 @@
     total = total.astype(BF16)
     hg_ref[...] = total
     fetch_qe.wait()
-    for h in range(qe_ref.shape[0]):
-        back = mm(total[:, h * DV : (h + 1) * DV], qe_ref[h], TN).astype(BF16)
-        for half in range(2):
-            back_ref[2 * h + half] = back[half * HALF : (half + 1) * HALF]
-    put = pltpu.make_async_copy(back_ref, pay_ref.at[:, pl.ds(DK + HALF, HALF)], out_sem)
-    put.start()
-    put.wait()
+    parts = out_sems.shape[0]
+    some = qe_ref.shape[0] // parts
+    puts = []
+    for p in range(parts):
+        for h in range(p * some, (p + 1) * some):
+            back = mm(total[:, h * DV : (h + 1) * DV], qe_ref[h], TN).astype(BF16)
+            for half in range(2):
+                back_ref[2 * h + half] = back[half * HALF : (half + 1) * HALF]
+        at = pl.ds(2 * p * some, 2 * some)
+        out = pay_ref.at[at, pl.ds(DK + HALF, HALF)]
+        puts.append(pltpu.make_async_copy(back_ref.at[at], out, out_sems.at[p]))
+        puts[-1].start()
+    for copy in puts:
+        copy.wait()
 
 
 def chain(maps_ref, first_ref, last_ref, out_ref, kept_ref, sems):
@@ -292,21 +303,23 @@
             out_g = hg_ref[:, cut_v]
             decay_in = decay + x.ident
             scores = pair_q * decay_in
-            fresh = mm_left(x.inverse[h], beta * (value - grow * mm(klow, state, NT))).astype(BF16)
-            fresh_g = mm(scores, out_g, TN) + mm(keep * khat, back, NT)
-            rhs_g = mm(x.inverse[h][0], fresh_g, TN)
-            rhs_low = rhs_g.astype(BF16)
+            inverse = x.inverse[h]
+            known = beta * (value - grow * mm_left(split(khat), state, NT))
+            fresh = split(mm3(inverse, split(known)))
+            fresh_g = mm_left(split(scores), out_g, TN) + mm_left(split(keep * khat), back, NT)
+            rhs_g = mm3(inverse, split(fresh_g), TN)
+            rhs = split(rhs_g)
             read_q = mm(out_g, state)
-            read_k = mm(rhs_low, state)
-            scores_g = mm(out_g, fresh, NT)
-            part_g = jnp.where(strict, -mm(rhs_low, fresh, NT), 0.0) * decay
-            pair_qg = (scores_g * decay_in).astype(BF16)
-            pair_kg = (part_g * beta).astype(BF16)
-            kept_g = mm(fresh, back)
+            read_k = mm_left(rhs, state)
+            scores_g = mm_right(out_g, fresh, NT)
+            part_g = jnp.where(strict, -mm3(rhs, fresh, NT), 0.0) * decay
+            pair_qg, pair_kg = split(scores_g * decay_in), split(part_g * beta)
+            kept_g = mm_left(fresh, back)
             part_k = part_g * pair_k
             gaps = scores_g * scores + part_k * beta
-            low_q = mm(pair_qg, klow).astype(BF16).astype(F32)
-            low_k = mm(pair_qg, qlow, TN) + mm(pair_kg, klow) + mm(pair_kg, klow, TN)
+            low_q = mm_left(pair_qg, klow).astype(BF16).astype(F32)
+            low_k = mm_left(pair_qg, qlow, TN) + mm_left(pair_kg, klow)
+            low_k += mm_left(pair_kg, klow, TN)
             qhat_g += grow * read_q + low_q
             khat_g += keep * kept_g - (beta * grow) * read_k + low_k.astype(BF16).astype(F32)
             dv_ref[0, :, cut_v] = (beta * rhs_g).astype(BF16)
@@ -434,7 +447,7 @@
                 pltpu.VMEM(square, BF16),
                 pltpu.VMEM((blocks, HALF, DK), BF16),
                 dma((2,)),
-                dma(()),
+                dma((2,)),
             ],
             flops=18 * unit,
             input_output_aliases={feats + 4: 0},

time: 128 us -> 125 us (0.977)
  waiting for transfers between devices: 43.4 us -> 40.8 us
  blocking collectives: 24.1 us -> 22 us
  Pallas kernels: 29.5 us -> 31.5 us
    all_to_all x1, waiting for transfers between devices: 21.7 us -> 19 us  [body(): total = lax.all_to_all(spread, 'ctx', 0, 0, tiled=True).reshape(rows, wide)]
    all_to_all x1, blocking collectives: 24.1 us -> 22 us  [body(): partial = lax.all_to_all(partial, 'ctx', 0, 0, tiled=True)]
    pallas_call x9, Pallas kernels: 29.5 us -> 31.5 us  [call(): pl.pallas_call(kernel, grid=grid, out_shape=outs, in_specs=[HELD] * len(a...]
where the time goes in v3:
time: 125 us; the launch traced here: 124 us
  waiting for transfers between devices  40.8 us (33%)
  Pallas kernels  31.5 us (25%)
  starting transfers between devices  28.4 us (23%)
  blocking collectives  22 us (18%)
    pallas_call x9, Pallas kernels, call(): pl.pallas_call(kernel, grid=grid, out_shape=outs, in_specs=[HELD] * len(a...  31.5 us
    all_to_all x1, blocking collectives, body(): partial = lax.all_to_all(partial, 'ctx', 0, 0, tiled=True)  22 us
    all_to_all x1, waiting for transfers between devices, body(): total = lax.all_to_all(spread, 'ctx', 0, 0, tiled=True).reshape(rows, wide)  19 us
    all_to_all x1, waiting for transfers between devices, body(): maps = lax.all_to_all(maps, 'ctx', 0, 0, tiled=True)  14.5 us
    all_to_all x1, starting transfers between devices, body(): maps = lax.all_to_all(maps, 'ctx', 0, 0, tiled=True)  7.91 us
    all_to_all x1, waiting for transfers between devices, body(): states = lax.all_to_all(states, 'ctx', 0, 0, tiled=True)  6.05 us
    ppermute x3, starting transfers between devices, body(): grads.append(lax.ppermute(output_grad, 'tp', pairs))  4.31 us
    ppermute x1, starting transfers between devices, body(): other_low = lax.ppermute(heads_low, 'dp', swap)  4.01 us
  transfers between devices with their start and end apart: 9, of which 4 were waited for; matrix products, arithmetic and copies ran while one was open for 1% of the time, Pallas kernels for 6%

profile of v3, /device:TPU:1, one launch (start us, length us, event | category | flops | bytes accessed | tf_op | source)
XLA Modules:
  0.0 124.5 jit_solution(14636162248491921441)
XLA Ops:
  0.6 0.0 copy-start.2
  0.6 1.5 %collective-permute-start.3 = (bf16[1024,1024]{1,0:T(8,128)(2,1)}, bf16[1024,1024]{1,0:T(8,128)(2,1)S(1)}, u32[]{:S(2)}, u32[]{:S(2)}) collective-permute-start(bf16[1024,1024]{1,0:T(8,128)(2,1)} %own_hbm.1), channel_id=1, source_target_pairs={{0,1},{1,0},{2,3},{3,2},{4,5},{5,4},{6,7},{7,6},{8,9},{9,8},{10,11... | collective-permute-start | bytes 6291464 | tf_op jit(solution)/shard_map/other_rows/ppermute | solution.py:425
  2.1 2.8 %collective-permute-start.1 = (bf16[1,128,512]{2,1,0:T(8,128)(2,1)}, bf16[1,128,512]{2,1,0:T(8,128)(2,1)S(1)}, u32[]{:S(2)}, u32[]{:S(2)}) collective-permute-start(bf16[1,128,512]{2,1,0:T(8,128)(2,1)} %g0_ref.1), channel_id=1, source_target_pairs={{4,0},{6,2},{0,4},{2,6},{5,1},{7,3},{1,5},{3,7},{12,8},{14,10},{8,... | collective-permute-start | bytes 393224 | tf_op jit(solution)/shard_map/gather_grad/ppermute | solution.py:423
  5.0 0.9 collective-permute-start
  5.8 0.6 collective-permute-start.2
  6.5 7.1 %local_maps.1 = (bf16[16,256,128]{2,1,0:T(8,128)(2,1)}, bf16[8,128,128]{2,1,0:T(8,128)(2,1)}, bf16[8,128,128]{2,1,0:T(8,128)(2,1)}) custom-call(bf16[1,128,512]{2,1,0:T(8,128)(2,1)} %refs_0_.3, bf16[1,128,512]{2,1,0:T(8,128)(2,1)} %refs_1_.3, bf16[1,128,1024]{2,1,0:T(8,128)(2,1)} %refs_2_.3, f32[1,8,128]{2,1,0:T(8,128)} %refs_3_.3, f32[1,8,128]{2,1,0:T(8,128)} %refs_4_.3), custom_call_target="tpu_custom_call" | custom-call | flops 1677721600 | bytes 2105344 | tf_op jit(solution)/shard_map/local_maps/pallas_call | solution.py:376
  13.5 0.1 pad_add_fusion.at_ref
  13.6 0.0 collective-permute-done.1.g2_ref
  13.6 0.0 collective-permute-done.g1_ref
  13.6 0.0 collective-permute-done.2.g3_ref
  13.6 0.0 collective-permute-done.3.other_ref
  13.6 0.0 copy-done.2
  13.6 3.6 %head_grads.1 = (bf16[16,256,128]{2,1,0:T(8,128)(2,1)}, bf16[128,1024]{1,0:T(8,128)(2,1)S(1)}, bf16[128,1024]{1,0:T(8,128)(2,1)S(1)}, bf16[128,1024]{1,0:T(8,128)(2,1)S(1)}) custom-call(s32[2]{0:T(128)S(1)} %pad_add_fusion.at_ref, bf16[1,128,512]{2,1,0:T(8,128)(2,1)S(1)} %copy-done.2, ...), custom_call_target="tpu_custom_call", output_to_operand_aliasing={{0}: (8, {})} | custom-call | flops 603979776 | bytes 7864328 | tf_op jit(solution)/shard_map/head_grads/pallas_call | solution.py:376
  17.2 0.0 copy-start
  17.2 0.0 copy-start.1
  17.3 7.9 %all-to-all-start = ((bf16[16,256,128]{2,1,0:T(8,128)(2,1)}), bf16[16,256,128]{2,1,0:T(8,128)(2,1)S(1)}, u32[]{:S(2)}, u32[]{:S(2)}) async-start(bf16[16,256,128]{2,1,0:T(8,128)(2,1)} %get-tuple-element.27), calls=%async_computation | async-start | bytes 2097152 | tf_op jit(solution)/shard_map/send_maps/all_to_all | solution.py:457
  25.2 0.8 dynamic-slice_bitcast_fusion
  26.0 14.5 %all-to-all-done.maps_ref = bf16[16,256,128]{2,1,0:T(8,128)(2,1)S(1)} async-done(((bf16[16,256,128]{2,1,0:T(8,128)(2,1)}), bf16[16,256,128]{2,1,0:T(8,128)(2,1)S(1)}, u32[]{:S(2)}, u32[]{:S(2)}) %all-to-all-start) | async-done | bytes 1048608 | tf_op jit(solution)/shard_map/send_maps/all_to_all | solution.py:457
  40.5 2.9 %chain.1 = bf16[16,128,128]{2,1,0:T(8,128)(2,1)} custom-call(bf16[16,256,128]{2,1,0:T(8,128)(2,1)S(1)} %all-to-all-done.maps_ref, f32[64,128]{1,0:T(8,128)S(1)} %get-tuple-element.43.first_ref, f32[64,128]{1,0:T(8,128)S(1)} %get-tuple-element.42.last_ref), custom_call_target="tpu_custom_call" | custom-call | flops 134217728 | bytes 1638400 | tf_op jit(solution)/shard_map/chain/pallas_call | solution.py:376
  43.3 3.9 %all-to-all-start.1 = ((bf16[16,128,128]{2,1,0:T(8,128)(2,1)}), bf16[16,128,128]{2,1,0:T(8,128)(2,1)S(1)}, u32[]{:S(2)}, u32[]{:S(2)}) async-start(bf16[16,128,128]{2,1,0:T(8,128)(2,1)} %chain.1), calls=%async_computation.1 | async-start | bytes 1048576 | tf_op jit(solution)/shard_map/return_states/all_to_all | solution.py:467
  47.3 3.0 %collective-permute-start.4 = (bf16[128,1024]{1,0:T(8,128)(2,1)S(1)}, bf16[128,1024]{1,0:T(8,128)(2,1)S(1)}, u32[]{:S(2)}, u32[]{:S(2)}) collective-permute-start(bf16[128,1024]{1,0:T(8,128)(2,1)S(1)} %get-tuple-element.29), channel_id=1, source_target_pairs={{0,1},{1,0},{2,3},{3,2},{4,5},{5,4},{6,7},{7,6},{8,9},{9,8},{10,11... | collective-permute-start | bytes 786440 | tf_op jit(solution)/shard_map/head_grads/ppermute | solution.py:455
  50.2 6.0 %all-to-all-done.1.y_ref.refs_6_ = bf16[16,128,128]{2,1,0:T(8,128)(2,1)S(1)} async-done(((bf16[16,128,128]{2,1,0:T(8,128)(2,1)}), bf16[16,128,128]{2,1,0:T(8,128)(2,1)S(1)}, u32[]{:S(2)}, u32[]{:S(2)}) %all-to-all-start.1) | async-done | bytes 524320 | tf_op jit(solution)/shard_map/return_states/all_to_all | solution.py:467
  56.3 0.0 copy-done
  56.3 0.0 copy-done.1
  56.3 0.3 outputs.1.low_ref
  56.6 4.0 %collective-permute-start.5 = (bf16[128,1024]{1,0:T(8,128)(2,1)S(1)}, bf16[128,1024]{1,0:T(8,128)(2,1)S(1)}, u32[]{:S(2)}, u32[]{:S(2)}) collective-permute-start(bf16[128,1024]{1,0:T(8,128)(2,1)S(1)} %outputs.1.low_ref), channel_id=1, source_target_pairs={{0,1},{1,0},{2,3},{3,2},{4,5},{5,4},{6,7},{7,6},{8,9},{9,8},{10,11... | collective-permute-start | bytes 786440 | tf_op jit(solution)/shard_map/outputs/ppermute | solution.py:472
  60.6 0.0 collective-permute-done.4.theirs_ref
  60.6 1.2 collective-permute-done.5.other_ref
  61.8 2.1 %projection.3.refs_7_ = bf16[16,64,1024]{2,1,0:T(8,128)(2,1)} custom-call(bf16[128,1024]{1,0:T(8,128)(2,1)S(1)} %get-tuple-element.28.mine_ref, bf16[128,1024]{1,0:T(8,128)(2,1)S(1)} %collective-permute-done.4.theirs_ref, bf16[128,1024]{1,0:T(8,128)(2,1)S(1)} %outputs.1.low_ref, bf16[128,1024]{1,0:T(8,128)(2,1)S(1)} %collective-permute-done.5.other_ref), custom_call_target="tpu_custom_call" | custom-call | flops 536870912 | bytes 3145728 | tf_op jit(solution)/shard_map/projection/pallas_call | solution.py:376
  63.9 11.4 %gradients.2 = (bf16[1,128,512]{2,1,0:T(8,128)(2,1)}, bf16[1,128,512]{2,1,0:T(8,128)(2,1)}, bf16[1,128,1024]{2,1,0:T(8,128)(2,1)}, f32[1,8,128]{2,1,0:T(8,128)},...) custom-call(s32[1]{0:T(128)} %bitcast.at_ref, ...), custom_call_target="tpu_custom_call", output_to_operand_aliasing={{5}: (8, {})} | custom-call | flops 1174405120 | bytes 6045700 | tf_op jit(solution)/shard_map/gradients/pallas_call | solution.py:376
  75.3 22.0 %all_to_all.20.pieces_ref = bf16[16,64,1024]{2,1,0:T(8,128)(2,1)S(1)} all-to-all(bf16[16,64,1024]{2,1,0:T(8,128)(2,1)} %get-tuple-element.31), channel_id=1, replica_groups=mesh['ctx'=16,'tp'=4,'dp'=2] {'ctx'}, dimensions={0} | all-to-all | bytes 4194304 | tf_op jit(solution)/shard_map/projection/all_to_all | solution.py:490
  97.3 1.7 %projection.4.refs_7_ = bf16[16,64,1024]{2,1,0:T(8,128)(2,1)} custom-call(bf16[16,64,1024]{2,1,0:T(8,128)(2,1)S(1)} %all_to_all.20.pieces_ref), custom_call_target="tpu_custom_call" | custom-call | bytes 4194304 | tf_op jit(solution)/shard_map/projection/pallas_call | solution.py:376
  99.0 3.7 %all-to-all-start.3 = ((bf16[16,64,1024]{2,1,0:T(8,128)(2,1)}), bf16[16,64,1024]{2,1,0:T(8,128)(2,1)S(1)}, u32[]{:S(2)}, u32[]{:S(2)}) async-start(bf16[16,64,1024]{2,1,0:T(8,128)(2,1)} %projection.4.refs_7_), calls=%async_computation.3 | async-start | bytes 4194304 | tf_op jit(solution)/shard_map/projection/all_to_all | solution.py:496
  102.8 0.3 gradients.3
  103.1 19.0 %all-to-all-done.3 = bf16[16,64,1024]{2,1,0:T(8,128)(2,1)S(1)} async-done(((bf16[16,64,1024]{2,1,0:T(8,128)(2,1)}), bf16[16,64,1024]{2,1,0:T(8,128)(2,1)S(1)}, u32[]{:S(2)}, u32[]{:S(2)}) %all-to-all-start.3) | async-done | bytes 2097184 | tf_op jit(solution)/shard_map/projection/all_to_all | solution.py:496
  122.2 2.1 %projection.5 = f32[1024,1024]{1,0:T(8,128)} custom-call(bf16[1024,1024]{1,0:T(8,128)(2,1)S(1)} %bitcast.9), custom_call_target="tpu_custom_call" | custom-call | bytes 6291456 | tf_op jit(solution)/shard_map/projection/pallas_call | solution.py:376
Async XLA Ops:
  0.6 13.0 %copy-start.2 = (bf16[1,128,512]{2,1,0:T(8,128)(2,1)S(1)}, bf16[1,128,512]{2,1,0:T(8,128)(2,1)}, u32[]{:S(2)}) copy-start(bf16[1,128,512]{2,1,0:T(8,128)(2,1)} %g0_ref.1) | copy-start | bytes 393220
  0.6 13.0 %collective-permute-start.3 = (bf16[1024,1024]{1,0:T(8,128)(2,1)}, bf16[1024,1024]{1,0:T(8,128)(2,1)S(1)}, u32[]{:S(2)}, u32[]{:S(2)}) collective-permute-start(bf16[1024,1024]{1,0:T(8,128)(2,1)} %own_hbm.1), channel_id=1, source_target_pairs={{0,1},{1,0},{2,3},{3,2},{4,5},{5,4},{6,7},{7,6},{8,9},{9,8},{10,11... | collective-permute-start | bytes 6291464 | tf_op jit(solution)/shard_map/other_rows/ppermute | solution.py:425
  2.1 11.5 %collective-permute-start.1 = (bf16[1,128,512]{2,1,0:T(8,128)(2,1)}, bf16[1,128,512]{2,1,0:T(8,128)(2,1)S(1)}, u32[]{:S(2)}, u32[]{:S(2)}) collective-permute-start(bf16[1,128,512]{2,1,0:T(8,128)(2,1)} %g0_ref.1), channel_id=1, source_target_pairs={{4,0},{6,2},{0,4},{2,6},{5,1},{7,3},{1,5},{3,7},{12,8},{14,10},{8,... | collective-permute-start | bytes 393224 | tf_op jit(solution)/shard_map/gather_grad/ppermute | solution.py:423
  5.0 8.6 %collective-permute-start = (bf16[1,128,512]{2,1,0:T(8,128)(2,1)}, bf16[1,128,512]{2,1,0:T(8,128)(2,1)S(1)}, u32[]{:S(2)}, u32[]{:S(2)}) collective-permute-start(bf16[1,128,512]{2,1,0:T(8,128)(2,1)} %g0_ref.1), channel_id=1, source_target_pairs={{2,0},{4,2},{6,4},{0,6},{3,1},{5,3},{7,5},{1,7},{10,8},{12,10},{14... | collective-permute-start | bytes 393224 | tf_op jit(solution)/shard_map/gather_grad/ppermute | solution.py:423
  5.8 7.8 %collective-permute-start.2 = (bf16[1,128,512]{2,1,0:T(8,128)(2,1)}, bf16[1,128,512]{2,1,0:T(8,128)(2,1)S(1)}, u32[]{:S(2)}, u32[]{:S(2)}) collective-permute-start(bf16[1,128,512]{2,1,0:T(8,128)(2,1)} %g0_ref.1), channel_id=1, source_target_pairs={{6,0},{0,2},{2,4},{4,6},{7,1},{1,3},{3,5},{5,7},{14,8},{8,10},{10,... | collective-permute-start | bytes 393224 | tf_op jit(solution)/shard_map/gather_grad/ppermute | solution.py:423
  17.2 39.1 %copy-start = (bf16[8,128,128]{2,1,0:T(8,128)(2,1)S(1)}, bf16[8,128,128]{2,1,0:T(8,128)(2,1)}, u32[]{:S(2)}) copy-start(bf16[8,128,128]{2,1,0:T(8,128)(2,1)} %get-tuple-element.24.qe_hbm.qe_ref) | copy-start | bytes 786436
  17.2 39.1 %copy-start.1 = (bf16[8,128,128]{2,1,0:T(8,128)(2,1)S(1)}, bf16[8,128,128]{2,1,0:T(8,128)(2,1)}, u32[]{:S(2)}) copy-start(bf16[8,128,128]{2,1,0:T(8,128)(2,1)} %get-tuple-element.30.o0_ref) | copy-start | bytes 786436
  17.3 23.2 %all-to-all-start = ((bf16[16,256,128]{2,1,0:T(8,128)(2,1)}), bf16[16,256,128]{2,1,0:T(8,128)(2,1)S(1)}, u32[]{:S(2)}, u32[]{:S(2)}) async-start(bf16[16,256,128]{2,1,0:T(8,128)(2,1)} %get-tuple-element.27), calls=%async_computation | async-start | bytes 2097152 | tf_op jit(solution)/shard_map/send_maps/all_to_all | solution.py:457
  43.3 13.0 %all-to-all-start.1 = ((bf16[16,128,128]{2,1,0:T(8,128)(2,1)}), bf16[16,128,128]{2,1,0:T(8,128)(2,1)S(1)}, u32[]{:S(2)}, u32[]{:S(2)}) async-start(bf16[16,128,128]{2,1,0:T(8,128)(2,1)} %chain.1), calls=%async_computation.1 | async-start | bytes 1048576 | tf_op jit(solution)/shard_map/return_states/all_to_all | solution.py:467
  47.3 13.3 %collective-permute-start.4 = (bf16[128,1024]{1,0:T(8,128)(2,1)S(1)}, bf16[128,1024]{1,0:T(8,128)(2,1)S(1)}, u32[]{:S(2)}, u32[]{:S(2)}) collective-permute-start(bf16[128,1024]{1,0:T(8,128)(2,1)S(1)} %get-tuple-element.29), channel_id=1, source_target_pairs={{0,1},{1,0},{2,3},{3,2},{4,5},{5,4},{6,7},{7,6},{8,9},{9,8},{10,11... | collective-permute-start | bytes 786440 | tf_op jit(solution)/shard_map/head_grads/ppermute | solution.py:455
  56.6 5.2 %collective-permute-start.5 = (bf16[128,1024]{1,0:T(8,128)(2,1)S(1)}, bf16[128,1024]{1,0:T(8,128)(2,1)S(1)}, u32[]{:S(2)}, u32[]{:S(2)}) collective-permute-start(bf16[128,1024]{1,0:T(8,128)(2,1)S(1)} %outputs.1.low_ref), channel_id=1, source_target_pairs={{0,1},{1,0},{2,3},{3,2},{4,5},{5,4},{6,7},{7,6},{8,9},{9,8},{10,11... | collective-permute-start | bytes 786440 | tf_op jit(solution)/shard_map/outputs/ppermute | solution.py:472
  99.0 23.1 %all-to-all-start.3 = ((bf16[16,64,1024]{2,1,0:T(8,128)(2,1)}), bf16[16,64,1024]{2,1,0:T(8,128)(2,1)S(1)}, u32[]{:S(2)}, u32[]{:S(2)}) async-start(bf16[16,64,1024]{2,1,0:T(8,128)(2,1)} %projection.4.refs_7_), calls=%async_computation.3 | async-start | bytes 4194304 | tf_op jit(solution)/shard_map/projection/all_to_all | solution.py:496

commit v4 on v3

--- a/solution.py
+++ b/solution.py
@@ -124,8 +124,21 @@
         self.inverse = [split(t) for t in unit_lower_inverses(parts, self.row, self.col)]
 
 
-def local_maps(q_ref, k_ref, v_ref, g_ref, b_ref, pay_ref, qe_ref, o0_ref):
+def local_maps(*refs):
+    far_in, far_out, held, kept, in_sems, out_sems = (
+        refs[:5], refs[5:8], refs[8:13], refs[13:16], *refs[16:]
+    )
+    fetches = [pltpu.make_async_copy(far_in[i], held[i], in_sems.at[i]) for i in range(5)]
+    for copy in fetches:
+        copy.start()
+    for copy in fetches:
+        copy.wait()
+    q_ref, k_ref, v_ref, g_ref, b_ref = held
+    pay_ref, qe_ref, o0_ref = kept
     x = Heads(q_ref, k_ref, g_ref, b_ref)
+    parts = out_sems.shape[0]
+    some = x.count // parts
+    puts = []
     for h in range(x.count):
         j = h // x.copies
         value = v_ref[0, :, h * DV : (h + 1) * DV].astype(F32)
@@ -139,34 +152,45 @@
         o0_ref[h] = mm(scores, u0).astype(BF16)
         for half in range(2):
             pay_ref[2 * h + half, 0:DK] = step
-            pay_ref[2 * h + half, DK : DK + HALF] = write[half * HALF : (half + 1) * HALF]
+            pay_ref[2 * h + half, DK:] = write[half * HALF : (half + 1) * HALF]
+        if (h + 1) % some == 0:
+            p, at = h // some, pl.ds(h + 1 - some, some)
+            both = pl.ds(2 * (h + 1 - some), 2 * some)
+            moves = (
+                (pay_ref.at[both], far_out[0].at[both, pl.ds(0, DK + HALF)]),
+                (qe_ref.at[at], far_out[1].at[at]),
+                (o0_ref.at[at], far_out[2].at[at]),
+            )
+            for i, (a, b) in enumerate(moves):
+                puts.append(pltpu.make_async_copy(a, b, out_sems.at[p, i]))
+                puts[-1].start()
+    for copy in puts:
+        copy.wait()
+
+
+def gathered_into(all_ref, here, refs):
+    for k, ref in enumerate(refs):
+        all_ref[lax.rem(here + k, all_ref.shape[0])] = ref[0]
 
 
 def head_grads(
     at_ref, g0_ref, g1_ref, g2_ref, g3_ref, own_hbm, other_ref, qe_hbm, pay_in,
-    pay_ref, hg_ref, mine_ref, theirs_ref, all_ref, own_ref, qe_ref, back_ref, in_sems, out_sems,
+    pay_ref, hg_ref, all_ref, own_ref, qe_ref, back_ref, in_sems, out_sems,
 ):
     fetch = pltpu.make_async_copy(own_hbm, own_ref, in_sems.at[0])
     fetch_qe = pltpu.make_async_copy(qe_hbm, qe_ref, in_sems.at[1])
     fetch.start()
     fetch_qe.start()
     core, here = at_ref[0], at_ref[1]
+    gathered_into(all_ref, here, (g0_ref, g1_ref, g2_ref, g3_ref))
     feats, wide = all_ref.shape[0], all_ref.shape[2]
-    parts = feats // 2
-    for k, ref in enumerate((g0_ref, g1_ref, g2_ref, g3_ref)):
-        all_ref[lax.rem(here + k, feats)] = ref[0]
+    half = feats // 2
     total = jnp.zeros((BLOCK, own_ref.shape[1]), F32)
-    for i in range(parts):
-        cut = slice(i * wide, (i + 1) * wide)
-        theirs = all_ref[parts * (1 - core) + i]
-        total += mm(theirs, other_ref[cut, :])
-        theirs_ref[:, cut] = theirs
+    for i in range(half):
+        total += mm(all_ref[half * (1 - core) + i], other_ref[i * wide : (i + 1) * wide, :])
     fetch.wait()
-    for i in range(parts):
-        cut = slice(i * wide, (i + 1) * wide)
-        mine = all_ref[parts * core + i]
-        total += mm(mine, own_ref[cut, :])
-        mine_ref[:, cut] = mine
+    for i in range(half):
+        total += mm(all_ref[half * core + i], own_ref[i * wide : (i + 1) * wide, :])
     total = total.astype(BF16)
     hg_ref[...] = total
     fetch_qe.wait()
@@ -176,8 +200,8 @@
     for p in range(parts):
         for h in range(p * some, (p + 1) * some):
             back = mm(total[:, h * DV : (h + 1) * DV], qe_ref[h], TN).astype(BF16)
-            for half in range(2):
-                back_ref[2 * h + half] = back[half * HALF : (half + 1) * HALF]
+            for side in range(2):
+                back_ref[2 * h + side] = back[side * HALF : (side + 1) * HALF]
         at = pl.ds(2 * p * some, 2 * some)
         out = pay_ref.at[at, pl.ds(DK + HALF, HALF)]
         puts.append(pltpu.make_async_copy(back_ref.at[at], out, out_sems.at[p]))
@@ -186,26 +210,40 @@
         copy.wait()
 
 
+def grad_rows(at_ref, g0_ref, g1_ref, g2_ref, g3_ref, mine_ref, theirs_ref, all_ref):
+    core, here = at_ref[0], at_ref[1]
+    gathered_into(all_ref, here, (g0_ref, g1_ref, g2_ref, g3_ref))
+    feats, wide = all_ref.shape[0], all_ref.shape[2]
+    half = feats // 2
+    for i in range(half):
+        cut = slice(i * wide, (i + 1) * wide)
+        mine_ref[cut, :] = all_ref[half * core + i].T
+        theirs_ref[cut, :] = all_ref[half * (1 - core) + i].T
+
+
 def chain(maps_ref, first_ref, last_ref, out_ref, kept_ref, sems):
     blocks = maps_ref.shape[0]
+    some = blocks // sems.shape[0]
     copies = []
 
     def times(state, step, dims):
         out = mm(jnp.concatenate(split(state), axis=0), step, dims)
         return out[:HALF] + out[HALF:]
 
-    def send(value, c, side):
-        rows = pl.ds(side * HALF, HALF)
-        kept_ref[c, rows] = value.astype(BF16)
-        copy = pltpu.make_async_copy(kept_ref.at[c, rows], out_ref.at[c, rows], sems.at[c, side])
-        copy.start()
-        copies.append(copy)
+    def send(first, side):
+        at = (pl.ds(first, some), pl.ds(side * HALF, HALF))
+        group = sems.at[first // some, side]
+        copies.append(pltpu.make_async_copy(kept_ref.at[at], out_ref.at[at], group))
+        copies[-1].start()
 
     state, back = first_ref[...], last_ref[...]
     for c in range(blocks):
         e = blocks - 1 - c
-        send(state, c, 0)
-        send(back, e, 1)
+        kept_ref[c, 0:HALF] = state.astype(BF16)
+        kept_ref[e, HALF:] = back.astype(BF16)
+        if (c + 1) % some == 0:
+            send(c + 1 - some, 0)
+            send(e, 1)
         if c < blocks - 1:
             write = maps_ref[c, DK : DK + HALF].astype(F32)
             read = maps_ref[e, DK + HALF :].astype(F32)
@@ -219,11 +257,12 @@
     blocks, piece = out_ref.shape[0], out_ref.shape[1]
     parts = sems.shape[0]
     some = blocks // parts
+    lows = jnp.concatenate([low_ref[...], other_ref[...]], axis=0)
     copies = []
     for p in range(parts):
         cut = slice(p * some * piece, (p + 1) * some * piece)
-        total = mm(mine_ref[:, cut], low_ref[...], TN) + mm(theirs_ref[:, cut], other_ref[...], TN)
-        total = total.astype(BF16)
+        rows = jnp.concatenate([mine_ref[cut, :], theirs_ref[cut, :]], axis=1)
+        total = mm(rows, lows).astype(BF16)
         for c in range(some):
             kept_ref[p * some + c] = total[c * piece : (c + 1) * piece]
         at = pl.ds(p * some, some)
@@ -429,20 +468,24 @@
         outs = [far((blocks, 2 * DK, DK), BF16)] + [far(square, BF16)] * 2
         maps, qe, o0 = call(
             local_maps, outs, *args,
-            ins=[whole(a) for a in args], out_specs=[whole(o) for o in outs], grid=(1,),
+            ins=[FAR] * 5, out_specs=[FAR] * 3,
+            scratch=[pltpu.VMEM(x.shape, x.dtype) for x in args]
+            + [pltpu.VMEM((blocks, DK + HALF, DK), BF16)]
+            + [pltpu.VMEM(square, BF16)] * 2
+            + [dma((5,)), dma((2, 3))],
             flops=50 * unit,
         )
     with jax.named_scope("head_grads"):
-        maps, head_grad, mine, theirs = call(
+        place = jnp.stack([core, lax.axis_index("tp")])
+        gather = pltpu.VMEM((feats,) + output_grad.shape[1:], BF16)
+        maps, head_grad = call(
             head_grads,
-            [far(maps.shape, BF16), shape((BLOCK, wide), BF16)]
-            + [shape((BLOCK, rows), BF16)] * 2,
-            jnp.stack([core, lax.axis_index("tp")]), *grads,
-            fixed(output_matrix), other_matrix, fixed(qe), fixed(maps),
+            [far(maps.shape, BF16), shape((BLOCK, wide), BF16)],
+            place, *grads, fixed(output_matrix), other_matrix, fixed(qe), fixed(maps),
             ins=[SCALAR] + [HELD] * feats + [FAR, HELD, FAR, FAR],
-            out_specs=[FAR, HELD, HELD, HELD],
+            out_specs=[FAR, HELD],
             scratch=[
-                pltpu.VMEM((feats,) + output_grad.shape[1:], BF16),
+                gather,
                 pltpu.VMEM(output_matrix.shape, BF16),
                 pltpu.VMEM(square, BF16),
                 pltpu.VMEM((blocks, HALF, DK), BF16),
@@ -452,15 +495,20 @@
             flops=18 * unit,
             input_output_aliases={feats + 4: 0},
         )
-        theirs = lax.ppermute(theirs, "dp", swap)
     with jax.named_scope("send_maps"):
         maps = lax.all_to_all(maps, "ctx", 0, 0, tiled=True)
+    with jax.named_scope("grad_rows"):
+        mine, theirs = call(
+            grad_rows, [shape((rows, BLOCK), BF16)] * 2, place, *grads,
+            ins=[SCALAR] + [HELD] * feats, scratch=[gather],
+        )
+        theirs = lax.ppermute(theirs, "dp", swap)
     with jax.named_scope("chain"):
         states, = call(
             chain, [far((blocks, 2 * HALF, DK), BF16)],
             maps, own_half(initial_state), own_half(final_state_grad),
             out_specs=[FAR],
-            scratch=[pltpu.VMEM((blocks, 2 * HALF, DK), BF16), dma((blocks, 2))],
+            scratch=[pltpu.VMEM((blocks, 2 * HALF, DK), BF16), dma((4, 2))],
             flops=4 * unit,
         )
     with jax.named_scope("return_states"):

time: 125 us -> 125 us (level)
    pallas_call x9 -> x10, Pallas kernels: 31.5 us -> 31.5 us  [call(): pl.pallas_call(kernel, grid=grid, out_shape=outs, in_specs=[HELD] * len(a...]
  transfers between devices with their start and end apart: 9 -> 9, of which waited for: 4 -> 4; matrix products, arithmetic and copies ran while one was open for 1% -> 1% of each run, Pallas kernels for 6% -> 7%
where the time goes in v4:
time: 125 us; the launch traced here: 124 us
  waiting for transfers between devices  39.9 us (32%)
  Pallas kernels  31.5 us (25%)
  starting transfers between devices  28.8 us (23%)
  blocking collectives  22 us (18%)
    pallas_call x10, Pallas kernels, call(): pl.pallas_call(kernel, grid=grid, out_shape=outs, in_specs=[HELD] * len(a...  31.5 us
    all_to_all x1, blocking collectives, body(): partial = lax.all_to_all(partial, 'ctx', 0, 0, tiled=True)  22 us
    all_to_all x1, waiting for transfers between devices, body(): total = lax.all_to_all(spread, 'ctx', 0, 0, tiled=True).reshape(rows, wide)  19 us
    all_to_all x1, waiting for transfers between devices, body(): maps = lax.all_to_all(maps, 'ctx', 0, 0, tiled=True)  14.4 us
    all_to_all x1, starting transfers between devices, body(): maps = lax.all_to_all(maps, 'ctx', 0, 0, tiled=True)  7.78 us
    all_to_all x1, waiting for transfers between devices, body(): states = lax.all_to_all(states, 'ctx', 0, 0, tiled=True)  5.26 us
    ppermute x3, starting transfers between devices, body(): grads.append(lax.ppermute(output_grad, 'tp', pairs))  4.91 us
    ppermute x1, starting transfers between devices, body(): other_low = lax.ppermute(heads_low, 'dp', swap)  4.02 us
  transfers between devices with their start and end apart: 9, of which 4 were waited for; matrix products, arithmetic and copies ran while one was open for 1% of the time, Pallas kernels for 7%

profile of v4, /device:TPU:1, one launch (start us, length us, event | category | flops | bytes accessed | tf_op | source)
XLA Modules:
  0.0 124.1 jit_solution(9682586917161755702)
XLA Ops:
  0.6 0.0 copy-start.1
  0.6 1.5 %collective-permute-start.3 = (bf16[1024,1024]{1,0:T(8,128)(2,1)}, bf16[1024,1024]{1,0:T(8,128)(2,1)S(1)}, u32[]{:S(2)}, u32[]{:S(2)}) collective-permute-start(bf16[1024,1024]{1,0:T(8,128)(2,1)} %own_hbm.1), channel_id=1, source_target_pairs={{0,1},{1,0},{2,3},{3,2},{4,5},{5,4},{6,7},{7,6},{8,9},{9,8},{10,11... | collective-permute-start | bytes 6291464 | tf_op jit(solution)/shard_map/other_rows/ppermute | solution.py:464
  2.1 1.3 %collective-permute-start.2 = (bf16[1,128,512]{2,1,0:T(8,128)(2,1)}, bf16[1,128,512]{2,1,0:T(8,128)(2,1)S(1)}, u32[]{:S(2)}, u32[]{:S(2)}) collective-permute-start(bf16[1,128,512]{2,1,0:T(8,128)(2,1)} %g0_ref.3), channel_id=1, source_target_pairs={{6,0},{0,2},{2,4},{4,6},{7,1},{1,3},{3,5},{5,7},{14,8},{8,10},{10,... | collective-permute-start | bytes 393224 | tf_op jit(solution)/shard_map/gather_grad/ppermute | solution.py:462
  3.5 2.5 %collective-permute-start.1 = (bf16[1,128,512]{2,1,0:T(8,128)(2,1)}, bf16[1,128,512]{2,1,0:T(8,128)(2,1)S(1)}, u32[]{:S(2)}, u32[]{:S(2)}) collective-permute-start(bf16[1,128,512]{2,1,0:T(8,128)(2,1)} %g0_ref.3), channel_id=1, source_target_pairs={{4,0},{6,2},{0,4},{2,6},{5,1},{7,3},{1,5},{3,7},{12,8},{14,10},{8,... | collective-permute-start | bytes 393224 | tf_op jit(solution)/shard_map/gather_grad/ppermute | solution.py:462
  5.9 1.2 collective-permute-start
  7.1 6.9 %local_maps.1 = (bf16[16,256,128]{2,1,0:T(8,128)(2,1)}, bf16[8,128,128]{2,1,0:T(8,128)(2,1)}, bf16[8,128,128]{2,1,0:T(8,128)(2,1)}) custom-call(bf16[1,128,512]{2,1,0:T(8,128)(2,1)} %refs_0_.5, bf16[1,128,512]{2,1,0:T(8,128)(2,1)} %refs_1_.5, bf16[1,128,1024]{2,1,0:T(8,128)(2,1)} %refs_2_.5, f32[1,8,128]{2,1,0:T(8,128)} %refs_3_.5, f32[1,8,128]{2,1,0:T(8,128)} %refs_4_.5), custom_call_target="tpu_custom_call" | custom-call | flops 1677721600 | bytes 2105344 | tf_op jit(solution)/shard_map/local_maps/pallas_call | solution.py:415
  14.0 0.1 pad_add_fusion.at_ref
  14.1 0.0 collective-permute-done.2.g3_ref
  14.1 0.0 collective-permute-done.1.g2_ref
  14.1 0.0 collective-permute-done.g1_ref
  14.1 0.0 collective-permute-done.3.other_ref
  14.1 0.0 copy-done.1
  14.1 3.6 %head_grads.1 = (bf16[16,256,128]{2,1,0:T(8,128)(2,1)}, bf16[128,1024]{1,0:T(8,128)(2,1)S(1)}) custom-call(s32[2]{0:T(128)S(1)} %pad_add_fusion.at_ref, bf16[1,128,512]{2,1,0:T(8,128)(2,1)S(1)} %copy-done.1, bf16[1,128,512]{2,1,0:T(8,128)(2,1)S(1)} %collective-permute-done.g1_ref, ...), custom_call_target="tpu_custom_call", output_to_operand_aliasing={{0}: (8, {})} | custom-call | flops 603979776 | bytes 7340040 | tf_op jit(solution)/shard_map/head_grads/pallas_call | solution.py:415
  17.7 7.8 %all-to-all-start = ((bf16[16,256,128]{2,1,0:T(8,128)(2,1)}), bf16[16,256,128]{2,1,0:T(8,128)(2,1)S(1)}, u32[]{:S(2)}, u32[]{:S(2)}) async-start(bf16[16,256,128]{2,1,0:T(8,128)(2,1)} %get-tuple-element.27), calls=%async_computation | async-start | bytes 2097152 | tf_op jit(solution)/shard_map/send_maps/all_to_all | solution.py:499
  25.5 0.0 copy-start
  25.5 0.0 copy-start.2
  25.5 0.8 dynamic-slice_bitcast_fusion
  26.3 14.4 %all-to-all-done.maps_ref = bf16[16,256,128]{2,1,0:T(8,128)(2,1)S(1)} async-done(((bf16[16,256,128]{2,1,0:T(8,128)(2,1)}), bf16[16,256,128]{2,1,0:T(8,128)(2,1)S(1)}, u32[]{:S(2)}, u32[]{:S(2)}) %all-to-all-start) | async-done | bytes 1048608 | tf_op jit(solution)/shard_map/send_maps/all_to_all | solution.py:499
  40.8 2.7 %chain.1 = bf16[16,128,128]{2,1,0:T(8,128)(2,1)} custom-call(bf16[16,256,128]{2,1,0:T(8,128)(2,1)S(1)} %all-to-all-done.maps_ref, f32[64,128]{1,0:T(8,128)S(1)} %get-tuple-element.43.first_ref, f32[64,128]{1,0:T(8,128)S(1)} %get-tuple-element.42.last_ref), custom_call_target="tpu_custom_call" | custom-call | flops 134217728 | bytes 1638400 | tf_op jit(solution)/shard_map/chain/pallas_call | solution.py:415
  43.5 3.9 %all-to-all-start.1 = ((bf16[16,128,128]{2,1,0:T(8,128)(2,1)}), bf16[16,128,128]{2,1,0:T(8,128)(2,1)S(1)}, u32[]{:S(2)}, u32[]{:S(2)}) async-start(bf16[16,128,128]{2,1,0:T(8,128)(2,1)} %chain.1), calls=%async_computation.1 | async-start | bytes 1048576 | tf_op jit(solution)/shard_map/return_states/all_to_all | solution.py:515
  47.4 0.8 grad_rows.1
  48.2 3.0 %collective-permute-start.4 = (bf16[1024,128]{1,0:T(8,128)(2,1)S(1)}, bf16[1024,128]{1,0:T(8,128)(2,1)S(1)}, u32[]{:S(2)}, u32[]{:S(2)}) collective-permute-start(bf16[1024,128]{1,0:T(8,128)(2,1)S(1)} %get-tuple-element.29), channel_id=1, source_target_pairs={{0,1},{1,0},{2,3},{3,2},{4,5},{5,4},{6,7},{7,6},{8,9},{9,8},{10,11... | collective-permute-start | bytes 786440 | tf_op jit(solution)/shard_map/grad_rows/ppermute | solution.py:505
  51.2 5.3 %all-to-all-done.1.y_ref.refs_6_ = bf16[16,128,128]{2,1,0:T(8,128)(2,1)S(1)} async-done(((bf16[16,128,128]{2,1,0:T(8,128)(2,1)}), bf16[16,128,128]{2,1,0:T(8,128)(2,1)S(1)}, u32[]{:S(2)}, u32[]{:S(2)}) %all-to-all-start.1) | async-done | bytes 524320 | tf_op jit(solution)/shard_map/return_states/all_to_all | solution.py:515
  56.4 0.0 copy-done
  56.4 0.0 copy-done.2
  56.4 0.3 outputs.1.low_ref
  56.7 4.0 %collective-permute-start.5 = (bf16[128,1024]{1,0:T(8,128)(2,1)S(1)}, bf16[128,1024]{1,0:T(8,128)(2,1)S(1)}, u32[]{:S(2)}, u32[]{:S(2)}) collective-permute-start(bf16[128,1024]{1,0:T(8,128)(2,1)S(1)} %outputs.1.low_ref), channel_id=1, source_target_pairs={{0,1},{1,0},{2,3},{3,2},{4,5},{5,4},{6,7},{7,6},{8,9},{9,8},{10,11... | collective-permute-start | bytes 786440 | tf_op jit(solution)/shard_map/outputs/ppermute | solution.py:520
  60.7 0.0 collective-permute-done.4.theirs_ref
  60.8 1.2 collective-permute-done.5.other_ref
  61.9 1.7 %projection.3.refs_7_ = bf16[16,64,1024]{2,1,0:T(8,128)(2,1)} custom-call(bf16[1024,128]{1,0:T(8,128)(2,1)S(1)} %get-tuple-element.28.mine_ref, bf16[1024,128]{1,0:T(8,128)(2,1)S(1)} %collective-permute-done.4.theirs_ref, bf16[128,1024]{1,0:T(8,128)(2,1)S(1)} %outputs.1.low_ref, bf16[128,1024]{1,0:T(8,128)(2,1)S(1)} %collective-permute-done.5.other_ref), custom_call_target="tpu_custom_call" | custom-call | flops 536870912 | bytes 3145728 | tf_op jit(solution)/shard_map/projection/pallas_call | solution.py:415
  63.6 11.4 %gradients.2 = (bf16[1,128,512]{2,1,0:T(8,128)(2,1)}, bf16[1,128,512]{2,1,0:T(8,128)(2,1)}, bf16[1,128,1024]{2,1,0:T(8,128)(2,1)}, f32[1,8,128]{2,1,0:T(8,128)},...) custom-call(s32[1]{0:T(128)} %bitcast.at_ref, ...), custom_call_target="tpu_custom_call", output_to_operand_aliasing={{5}: (8, {})} | custom-call | flops 1174405120 | bytes 6045700 | tf_op jit(solution)/shard_map/gradients/pallas_call | solution.py:415
  75.0 22.0 %all_to_all.20.pieces_ref = bf16[16,64,1024]{2,1,0:T(8,128)(2,1)S(1)} all-to-all(bf16[16,64,1024]{2,1,0:T(8,128)(2,1)} %get-tuple-element.31), channel_id=1, replica_groups=mesh['ctx'=16,'tp'=4,'dp'=2] {'ctx'}, dimensions={0} | all-to-all | bytes 4194304 | tf_op jit(solution)/shard_map/projection/all_to_all | solution.py:538
  97.0 1.7 %projection.4.refs_7_ = bf16[16,64,1024]{2,1,0:T(8,128)(2,1)} custom-call(bf16[16,64,1024]{2,1,0:T(8,128)(2,1)S(1)} %all_to_all.20.pieces_ref), custom_call_target="tpu_custom_call" | custom-call | bytes 4194304 | tf_op jit(solution)/shard_map/projection/pallas_call | solution.py:415
  98.7 3.7 %all-to-all-start.3 = ((bf16[16,64,1024]{2,1,0:T(8,128)(2,1)}), bf16[16,64,1024]{2,1,0:T(8,128)(2,1)S(1)}, u32[]{:S(2)}, u32[]{:S(2)}) async-start(bf16[16,64,1024]{2,1,0:T(8,128)(2,1)} %projection.4.refs_7_), calls=%async_computation.3 | async-start | bytes 4194304 | tf_op jit(solution)/shard_map/projection/all_to_all | solution.py:544
  102.5 0.3 gradients.3
  102.8 19.0 %all-to-all-done.3 = bf16[16,64,1024]{2,1,0:T(8,128)(2,1)S(1)} async-done(((bf16[16,64,1024]{2,1,0:T(8,128)(2,1)}), bf16[16,64,1024]{2,1,0:T(8,128)(2,1)S(1)}, u32[]{:S(2)}, u32[]{:S(2)}) %all-to-all-start.3) | async-done | bytes 2097184 | tf_op jit(solution)/shard_map/projection/all_to_all | solution.py:544
  121.8 2.1 %projection.5 = f32[1024,1024]{1,0:T(8,128)} custom-call(bf16[1024,1024]{1,0:T(8,128)(2,1)S(1)} %bitcast.9), custom_call_target="tpu_custom_call" | custom-call | bytes 6291456 | tf_op jit(solution)/shard_map/projection/pallas_call | solution.py:415
Async XLA Ops:
  0.6 13.5 %copy-start.1 = (bf16[1,128,512]{2,1,0:T(8,128)(2,1)S(1)}, bf16[1,128,512]{2,1,0:T(8,128)(2,1)}, u32[]{:S(2)}) copy-start(bf16[1,128,512]{2,1,0:T(8,128)(2,1)} %g0_ref.3) | copy-start | bytes 393220
  0.6 13.4 %collective-permute-start.3 = (bf16[1024,1024]{1,0:T(8,128)(2,1)}, bf16[1024,1024]{1,0:T(8,128)(2,1)S(1)}, u32[]{:S(2)}, u32[]{:S(2)}) collective-permute-start(bf16[1024,1024]{1,0:T(8,128)(2,1)} %own_hbm.1), channel_id=1, source_target_pairs={{0,1},{1,0},{2,3},{3,2},{4,5},{5,4},{6,7},{7,6},{8,9},{9,8},{10,11... | collective-permute-start | bytes 6291464 | tf_op jit(solution)/shard_map/other_rows/ppermute | solution.py:464
  2.1 11.9 %collective-permute-start.2 = (bf16[1,128,512]{2,1,0:T(8,128)(2,1)}, bf16[1,128,512]{2,1,0:T(8,128)(2,1)S(1)}, u32[]{:S(2)}, u32[]{:S(2)}) collective-permute-start(bf16[1,128,512]{2,1,0:T(8,128)(2,1)} %g0_ref.3), channel_id=1, source_target_pairs={{6,0},{0,2},{2,4},{4,6},{7,1},{1,3},{3,5},{5,7},{14,8},{8,10},{10,... | collective-permute-start | bytes 393224 | tf_op jit(solution)/shard_map/gather_grad/ppermute | solution.py:462
  3.5 10.6 %collective-permute-start.1 = (bf16[1,128,512]{2,1,0:T(8,128)(2,1)}, bf16[1,128,512]{2,1,0:T(8,128)(2,1)S(1)}, u32[]{:S(2)}, u32[]{:S(2)}) collective-permute-start(bf16[1,128,512]{2,1,0:T(8,128)(2,1)} %g0_ref.3), channel_id=1, source_target_pairs={{4,0},{6,2},{0,4},{2,6},{5,1},{7,3},{1,5},{3,7},{12,8},{14,10},{8,... | collective-permute-start | bytes 393224 | tf_op jit(solution)/shard_map/gather_grad/ppermute | solution.py:462
  5.9 8.2 %collective-permute-start = (bf16[1,128,512]{2,1,0:T(8,128)(2,1)}, bf16[1,128,512]{2,1,0:T(8,128)(2,1)S(1)}, u32[]{:S(2)}, u32[]{:S(2)}) collective-permute-start(bf16[1,128,512]{2,1,0:T(8,128)(2,1)} %g0_ref.3), channel_id=1, source_target_pairs={{2,0},{4,2},{6,4},{0,6},{3,1},{5,3},{7,5},{1,7},{10,8},{12,10},{14... | collective-permute-start | bytes 393224 | tf_op jit(solution)/shard_map/gather_grad/ppermute | solution.py:462
  17.7 23.1 %all-to-all-start = ((bf16[16,256,128]{2,1,0:T(8,128)(2,1)}), bf16[16,256,128]{2,1,0:T(8,128)(2,1)S(1)}, u32[]{:S(2)}, u32[]{:S(2)}) async-start(bf16[16,256,128]{2,1,0:T(8,128)(2,1)} %get-tuple-element.27), calls=%async_computation | async-start | bytes 2097152 | tf_op jit(solution)/shard_map/send_maps/all_to_all | solution.py:499
  25.5 30.9 %copy-start = (bf16[8,128,128]{2,1,0:T(8,128)(2,1)S(1)}, bf16[8,128,128]{2,1,0:T(8,128)(2,1)}, u32[]{:S(2)}) copy-start(bf16[8,128,128]{2,1,0:T(8,128)(2,1)} %get-tuple-element.24.qe_hbm.qe_ref) | copy-start | bytes 786436
  25.5 30.9 %copy-start.2 = (bf16[8,128,128]{2,1,0:T(8,128)(2,1)S(1)}, bf16[8,128,128]{2,1,0:T(8,128)(2,1)}, u32[]{:S(2)}) copy-start(bf16[8,128,128]{2,1,0:T(8,128)(2,1)} %get-tuple-element.30.o0_ref) | copy-start | bytes 786436
  43.5 12.9 %all-to-all-start.1 = ((bf16[16,128,128]{2,1,0:T(8,128)(2,1)}), bf16[16,128,128]{2,1,0:T(8,128)(2,1)S(1)}, u32[]{:S(2)}, u32[]{:S(2)}) async-start(bf16[16,128,128]{2,1,0:T(8,128)(2,1)} %chain.1), calls=%async_computation.1 | async-start | bytes 1048576 | tf_op jit(solution)/shard_map/return_states/all_to_all | solution.py:515
  48.2 12.6 %collective-permute-start.4 = (bf16[1024,128]{1,0:T(8,128)(2,1)S(1)}, bf16[1024,128]{1,0:T(8,128)(2,1)S(1)}, u32[]{:S(2)}, u32[]{:S(2)}) collective-permute-start(bf16[1024,128]{1,0:T(8,128)(2,1)S(1)} %get-tuple-element.29), channel_id=1, source_target_pairs={{0,1},{1,0},{2,3},{3,2},{4,5},{5,4},{6,7},{7,6},{8,9},{9,8},{10,11... | collective-permute-start | bytes 786440 | tf_op jit(solution)/shard_map/grad_rows/ppermute | solution.py:505
  56.7 5.2 %collective-permute-start.5 = (bf16[128,1024]{1,0:T(8,128)(2,1)S(1)}, bf16[128,1024]{1,0:T(8,128)(2,1)S(1)}, u32[]{:S(2)}, u32[]{:S(2)}) collective-permute-start(bf16[128,1024]{1,0:T(8,128)(2,1)S(1)} %outputs.1.low_ref), channel_id=1, source_target_pairs={{0,1},{1,0},{2,3},{3,2},{4,5},{5,4},{6,7},{7,6},{8,9},{9,8},{10,11... | collective-permute-start | bytes 786440 | tf_op jit(solution)/shard_map/outputs/ppermute | solution.py:520
  98.7 23.1 %all-to-all-start.3 = ((bf16[16,64,1024]{2,1,0:T(8,128)(2,1)}), bf16[16,64,1024]{2,1,0:T(8,128)(2,1)S(1)}, u32[]{:S(2)}, u32[]{:S(2)}) async-start(bf16[16,64,1024]{2,1,0:T(8,128)(2,1)} %projection.4.refs_7_), calls=%async_computation.3 | async-start | bytes 4194304 | tf_op jit(solution)/shard_map/projection/all_to_all | solution.py:544

commit v5 on v4

--- a/solution.py
+++ b/solution.py
@@ -73,7 +73,7 @@
     return jnp.where(strict, jnp.exp(jnp.where(strict, gap, 0.0)), 0.0)
 
 
-def unit_lower_inverses(parts, row, col):
+def unit_lower_inverses(parts, row, col, finer):
     ident = (row == col).astype(F32)
     found = None
     size = 1
@@ -89,11 +89,15 @@
         size *= 2
     lows = [t.astype(BF16) for t in found]
     rest = [ident - (t.astype(F32) + mm_left(split(a), t)) for t, a in zip(lows, parts)]
-    return [t.astype(F32) + mm(t, r) for t, r in zip(lows, rest)]
+    found = [t.astype(F32) + mm(t, r) for t, r in zip(lows, rest)]
+    if finer:
+        rest = [ident - (t + mm3(split(a), split(t))) for t, a in zip(found, parts)]
+        found = [t + mm3(split(t), split(r)) for t, r in zip(found, rest)]
+    return found
 
 
 class Heads:
-    def __init__(self, q_ref, k_ref, g_ref, b_ref):
+    def __init__(self, q_ref, k_ref, g_ref, b_ref, inverse=None, finer=False):
         self.count = g_ref.shape[1]
         self.copies = self.count * DK // q_ref.shape[2]
         self.row, self.col = iotas()
@@ -118,10 +122,18 @@
             self.k_scale.append(k_scale)
             self.pair_k.append(mm(khat, khat, NT))
             self.pair_q.append(mm(qn * QSCALE, khat, NT))
-        parts = [
-            self.beta[h] * self.pair_k[h // self.copies] * self.decay[h] for h in range(self.count)
-        ]
-        self.inverse = [split(t) for t in unit_lower_inverses(parts, self.row, self.col)]
+        self.inverse = inverse
+        if inverse is None:
+            parts = [
+                self.beta[h] * self.pair_k[h // self.copies] * self.decay[h]
+                for h in range(self.count)
+            ]
+            found = unit_lower_inverses(parts, self.row, self.col, finer)
+            self.inverse = [split(t) for t in found]
+
+    def fresh(self, h, value, state):
+        read = mm_left(split(self.khat[h // self.copies]), state, NT)
+        return split(mm3(self.inverse[h], split(self.beta[h] * (value - self.grow[h] * read))))
 
 
 def local_maps(*refs):
@@ -157,7 +169,7 @@
             p, at = h // some, pl.ds(h + 1 - some, some)
             both = pl.ds(2 * (h + 1 - some), 2 * some)
             moves = (
-                (pay_ref.at[both], far_out[0].at[both, pl.ds(0, DK + HALF)]),
+                (pay_ref.at[both], far_out[0].at[both]),
                 (qe_ref.at[at], far_out[1].at[at]),
                 (o0_ref.at[at], far_out[2].at[at]),
             )
@@ -174,8 +186,8 @@
 
 
 def head_grads(
-    at_ref, g0_ref, g1_ref, g2_ref, g3_ref, own_hbm, other_ref, qe_hbm, pay_in,
-    pay_ref, hg_ref, all_ref, own_ref, qe_ref, back_ref, in_sems, out_sems,
+    at_ref, g0_ref, g1_ref, g2_ref, g3_ref, own_hbm, other_ref, qe_hbm,
+    back_out, hg_ref, all_ref, own_ref, qe_ref, back_ref, in_sems, out_sems,
 ):
     fetch = pltpu.make_async_copy(own_hbm, own_ref, in_sems.at[0])
     fetch_qe = pltpu.make_async_copy(qe_hbm, qe_ref, in_sems.at[1])
@@ -203,8 +215,7 @@
             for side in range(2):
                 back_ref[2 * h + side] = back[side * HALF : (side + 1) * HALF]
         at = pl.ds(2 * p * some, 2 * some)
-        out = pay_ref.at[at, pl.ds(DK + HALF, HALF)]
-        puts.append(pltpu.make_async_copy(back_ref.at[at], out, out_sems.at[p]))
+        puts.append(pltpu.make_async_copy(back_ref.at[at], back_out.at[at], out_sems.at[p]))
         puts[-1].start()
     for copy in puts:
         copy.wait()
@@ -221,40 +232,84 @@
         theirs_ref[cut, :] = all_ref[half * (1 - core) + i].T
 
 
-def chain(maps_ref, first_ref, last_ref, out_ref, kept_ref, sems):
-    blocks = maps_ref.shape[0]
-    some = blocks // sems.shape[0]
+def times(state, step, dims):
+    out = mm(jnp.concatenate(split(state), axis=0), step, dims)
+    return out[:HALF] + out[HALF:]
+
+
+def forward_chain(
+    at_ref, maps_hbm, back_hbm, first_hbm, out_ref,
+    maps_ref, kept_ref, first_ref, back_sems, in_sems, sems,
+):
+    blocks, parts = maps_ref.shape[0], sems.shape[0]
+    some = blocks // parts
+    groups = [pl.ds(p * some, some) for p in range(parts)]
+    fetches = [
+        pltpu.make_async_copy(maps_hbm.at[at], maps_ref.at[at], in_sems.at[p])
+        for p, at in enumerate(groups)
+    ]
+    fetch_first = pltpu.make_async_copy(first_hbm.at[at_ref[0]], first_ref, back_sems.at[1])
+    fetch_first.start()
+    fetches[0].start()
+    fetch_back = pltpu.make_async_copy(back_hbm, kept_ref.at[:, pl.ds(HALF, HALF)], back_sems.at[0])
+    fetch_back.start()
+    for copy in fetches[1:]:
+        copy.start()
     copies = []
-
-    def times(state, step, dims):
-        out = mm(jnp.concatenate(split(state), axis=0), step, dims)
-        return out[:HALF] + out[HALF:]
-
-    def send(first, side):
-        at = (pl.ds(first, some), pl.ds(side * HALF, HALF))
-        group = sems.at[first // some, side]
-        copies.append(pltpu.make_async_copy(kept_ref.at[at], out_ref.at[at], group))
-        copies[-1].start()
-
-    state, back = first_ref[...], last_ref[...]
+    fetch_first.wait()
+    state = first_ref[...]
     for c in range(blocks):
-        e = blocks - 1 - c
         kept_ref[c, 0:HALF] = state.astype(BF16)
-        kept_ref[e, HALF:] = back.astype(BF16)
+        if c % some == 0:
+            fetches[c // some].wait()
         if (c + 1) % some == 0:
-            send(c + 1 - some, 0)
-            send(e, 1)
+            p = c // some
+            if p == 0:
+                fetch_back.wait()
+            at = groups[p]
+            copies.append(pltpu.make_async_copy(kept_ref.at[at], out_ref.at[at], sems.at[p]))
+            copies[-1].start()
         if c < blocks - 1:
-            write = maps_ref[c, DK : DK + HALF].astype(F32)
-            read = maps_ref[e, DK + HALF :].astype(F32)
-            state = times(state, maps_ref[c, 0:DK], NN) + write
-            back = times(back, maps_ref[e, 0:DK], NT) + read
+            state = times(state, maps_ref[c, 0:DK], NN) + maps_ref[c, DK:].astype(F32)
     for copy in copies:
         copy.wait()
 
 
-def projection(mine_ref, theirs_ref, low_ref, other_ref, out_ref, kept_ref, sems):
-    blocks, piece = out_ref.shape[0], out_ref.shape[1]
+def backward_chain(
+    at_ref, maps_hbm, in_ref, last_hbm, out_ref, maps_ref, kept_ref, last_ref, last_sem, in_sems, sems
+):
+    blocks, parts = maps_ref.shape[0], sems.shape[0]
+    some = blocks // parts
+    wide = out_ref.shape[2] - DK
+    groups = [pl.ds(p * some, some) for p in range(parts)]
+    fetches = [
+        pltpu.make_async_copy(maps_hbm.at[at, pl.ds(0, DK)], maps_ref.at[at], in_sems.at[p])
+        for p, at in enumerate(groups)
+    ]
+    fetch_last = pltpu.make_async_copy(last_hbm.at[at_ref[0]], last_ref, last_sem)
+    fetch_last.start()
+    for copy in reversed(fetches):
+        copy.start()
+    copies = []
+    fetch_last.wait()
+    back = last_ref[...]
+    for c in range(blocks - 1, -1, -1):
+        kept_ref[c] = back.astype(BF16)
+        p = c // some
+        if c % some == some - 1:
+            fetches[p].wait()
+        if c % some == 0:
+            out = out_ref.at[groups[p], :, pl.ds(wide, DK)]
+            copies.append(pltpu.make_async_copy(kept_ref.at[groups[p]], out, sems.at[p]))
+            copies[-1].start()
+        if c > 0:
+            back = times(back, maps_ref[c], NT) + in_ref[c, HALF:].astype(F32)
+    for copy in copies:
+        copy.wait()
+
+
+def projection(mine_ref, theirs_ref, low_ref, other_ref, in_ref, out_ref, kept_ref, sems):
+    blocks, piece, wide = kept_ref.shape
     parts = sems.shape[0]
     some = blocks // parts
     lows = jnp.concatenate([low_ref[...], other_ref[...]], axis=0)
@@ -266,26 +321,30 @@
         for c in range(some):
             kept_ref[p * some + c] = total[c * piece : (c + 1) * piece]
         at = pl.ds(p * some, some)
-        copies.append(pltpu.make_async_copy(kept_ref.at[at], out_ref.at[at], sems.at[p]))
+        out = out_ref.at[at, :, pl.ds(0, wide)]
+        copies.append(pltpu.make_async_copy(kept_ref.at[at], out, sems.at[p]))
         copies[-1].start()
     for copy in copies:
         copy.wait()
 
 
-def reduce_spread(scale, pieces_ref, out_ref, sum_ref, sems):
-    blocks, rows = out_ref.shape[:2]
+def reduce_spread(scale, pieces_ref, out_ref, back_ref, sum_ref, back_sem, sems):
+    blocks, rows, wide = out_ref.shape
     parts = sems.shape[1]
     copies = []
     for p in range(parts):
         at = pl.ds(p * (rows // parts), rows // parts)
-        total = pieces_ref[0, at].astype(F32)
+        total = pieces_ref[0, at, 0:wide].astype(F32)
         for c in range(1, blocks):
-            total += pieces_ref[c, at].astype(F32)
+            total += pieces_ref[c, at, 0:wide].astype(F32)
         sum_ref[at] = (total * scale).astype(BF16)
         for c in range(blocks):
             copy = pltpu.make_async_copy(sum_ref.at[at], out_ref.at[c, at], sems.at[c, p])
             copy.start()
             copies.append(copy)
+    back = pieces_ref.at[:, :, pl.ds(wide, DK)]
+    copies.append(pltpu.make_async_copy(back, back_ref, back_sem))
+    copies[-1].start()
     for copy in copies:
         copy.wait()
 
@@ -314,11 +373,57 @@
         o_ref[:, h * DV : (h + 1) * DV] = out.astype(BF16)
 
 
+def query_gradients(
+    q_ref, k_ref, v_ref, g_ref, b_ref, hg_ref, y_ref, dq_ref, dk_ref, dg_ref, rhs_ref,
+    *kept_refs,
+):
+    x = Heads(q_ref, k_ref, g_ref, b_ref, finer=True)
+    lane = lax.broadcasted_iota(jnp.int32, (BLOCK, x.count), 1)
+    level = lax.broadcasted_iota(jnp.int32, (x.count, BLOCK), 0)
+    cumul_g = jnp.zeros((BLOCK, x.count), F32)
+    across = jnp.zeros((x.count, BLOCK), F32)
+    for j in range(x.count // x.copies):
+        cut = slice(j * DK, (j + 1) * DK)
+        qn, klow = x.qn[j], x.khat[j].astype(BF16)
+        qhat = qn * QSCALE
+        qlow = qhat.astype(BF16)
+        qhat_g = jnp.zeros((BLOCK, DK), F32)
+        khat_g = jnp.zeros((BLOCK, DK), F32)
+        for h in range(j * x.copies, (j + 1) * x.copies):
+            cut_v = slice(h * DV, (h + 1) * DV)
+            value = v_ref[0, :, cut_v].astype(F32)
+            state, out_g = halves_of(y_ref, h, 0), hg_ref[:, cut_v]
+            decay_in = x.decay[h] + x.ident
+            fresh = x.fresh(h, value, state)
+            for ref, part in zip(kept_refs, (*x.inverse[h], *fresh)):
+                ref[h] = part
+            pair_g = mm_right(out_g, fresh, NT) * decay_in
+            gaps = pair_g * x.pair_q[j]
+            pair_g = split(pair_g)
+            scores = x.pair_q[j] * decay_in
+            fresh_g = mm_left(split(scores), out_g, TN)
+            rhs_ref[h] = mm3(x.inverse[h], split(fresh_g), TN)
+            read_q = mm(out_g, state)
+            low_q, low_k = mm_left(pair_g, klow), mm_left(pair_g, qlow, TN)
+            qhat_g += x.grow[h] * read_q + low_q.astype(BF16).astype(F32)
+            khat_g += low_k.astype(BF16).astype(F32)
+            grow_g = jnp.sum(read_q * qhat, axis=1, keepdims=True)
+            cumul_col = grow_g * x.grow[h] + jnp.sum(gaps, axis=1, keepdims=True)
+            cumul_g = jnp.where(lane == h, cumul_col, cumul_g)
+            across = jnp.where(level == h, jnp.sum(gaps, axis=0, keepdims=True), across)
+        q_along = jnp.sum(qn * qhat_g, axis=1, keepdims=True)
+        dq_ref[0, :, cut] = ((x.q_scale[j] * QSCALE) * (qhat_g - qn * q_along)).astype(BF16)
+        dk_ref[0, :, cut] = khat_g
+    dg_ref[0] = cumul_g.T - across
+
+
 def gradients(
-    q_ref, k_ref, v_ref, g_ref, b_ref, hg_ref, y_ref,
-    dq_ref, dk_ref, dv_ref, dg_ref, db_ref,
+    q_ref, k_ref, v_ref, g_ref, b_ref, hg_ref, y_ref, back_ref, part_dk_ref, part_dg_ref,
+    part_rhs_ref, t_high_ref, t_low_ref, fresh_high_ref, fresh_low_ref,
+    dk_ref, dv_ref, dg_ref, db_ref,
 ):
-    x = Heads(q_ref, k_ref, g_ref, b_ref)
+    inverse = [(t_high_ref[h], t_low_ref[h]) for h in range(g_ref.shape[1])]
+    x = Heads(q_ref, k_ref, g_ref, b_ref, inverse)
     row, col = x.row, x.col
     strict = row > col
     lane = lax.broadcasted_iota(jnp.int32, (BLOCK, x.count), 1)
@@ -328,77 +433,69 @@
     across = jnp.zeros((x.count, BLOCK), F32)
     for j in range(x.count // x.copies):
         cut = slice(j * DK, (j + 1) * DK)
-        qn, khat = x.qn[j], x.khat[j]
-        qhat = qn * QSCALE
-        qlow, klow = qhat.astype(BF16), khat.astype(BF16)
-        pair_k, pair_q = x.pair_k[j], x.pair_q[j]
-        qhat_g = jnp.zeros((BLOCK, DK), F32)
-        khat_g = jnp.zeros((BLOCK, DK), F32)
+        khat = x.khat[j]
+        klow = khat.astype(BF16)
+        pair_k = x.pair_k[j]
+        khat_g = part_dk_ref[0, :, cut]
         for h in range(j * x.copies, (j + 1) * x.copies):
             cut_v = slice(h * DV, (h + 1) * DV)
             decay, grow, keep, beta = x.decay[h], x.grow[h], x.keep[h], x.beta[h]
             value = v_ref[0, :, cut_v].astype(F32)
-            state, back = halves_of(y_ref, h, 0), halves_of(y_ref, h, HALF)
-            out_g = hg_ref[:, cut_v]
-            decay_in = decay + x.ident
-            scores = pair_q * decay_in
-            inverse = x.inverse[h]
-            known = beta * (value - grow * mm_left(split(khat), state, NT))
-            fresh = split(mm3(inverse, split(known)))
-            fresh_g = mm_left(split(scores), out_g, TN) + mm_left(split(keep * khat), back, NT)
-            rhs_g = mm3(inverse, split(fresh_g), TN)
+            state, back = halves_of(y_ref, h, 0), halves_of(back_ref, h, 0)
+            fresh = fresh_high_ref[h], fresh_low_ref[h]
+            fresh_g = mm_left(split(keep * khat), back, NT)
+            rhs_g = part_rhs_ref[h] + mm3(x.inverse[h], split(fresh_g), TN)
             rhs = split(rhs_g)
-            read_q = mm(out_g, state)
             read_k = mm_left(rhs, state)
-            scores_g = mm_right(out_g, fresh, NT)
             part_g = jnp.where(strict, -mm3(rhs, fresh, NT), 0.0) * decay
-            pair_qg, pair_kg = split(scores_g * decay_in), split(part_g * beta)
+            pair_kg = split(part_g * beta)
             kept_g = mm_left(fresh, back)
             part_k = part_g * pair_k
-            gaps = scores_g * scores + part_k * beta
-            low_q = mm_left(pair_qg, klow).astype(BF16).astype(F32)
-            low_k = mm_left(pair_qg, qlow, TN) + mm_left(pair_kg, klow)
-            low_k += mm_left(pair_kg, klow, TN)
-            qhat_g += grow * read_q + low_q
+            gaps = part_k * beta
+            low_k = mm_left(pair_kg, klow) + mm_left(pair_kg, klow, TN)
             khat_g += keep * kept_g - (beta * grow) * read_k + low_k.astype(BF16).astype(F32)
             dv_ref[0, :, cut_v] = (beta * rhs_g).astype(BF16)
             read_sum = jnp.sum(read_k * khat, axis=1, keepdims=True)
             beta_col = jnp.sum(rhs_g * value + part_k, axis=1, keepdims=True) - grow * read_sum
             kept_sum = jnp.sum(kept_g * khat, axis=1, keepdims=True) * keep
-            grow_g = jnp.sum(read_q * qhat, axis=1, keepdims=True) - beta * read_sum
-            cumul_col = grow_g * grow + jnp.sum(gaps, axis=1, keepdims=True) - kept_sum
+            cumul_col = -(beta * grow) * read_sum + jnp.sum(gaps, axis=1, keepdims=True) - kept_sum
             whole = jnp.sum(back.astype(F32) * state.astype(F32)) * x.end[h]
             at_end = jnp.sum(kept_sum, axis=0, keepdims=True) + whole
             cumul_col += jnp.where(row[:, 0:1] == BLOCK - 1, at_end, 0.0)
             cumul_g = jnp.where(lane == h, cumul_col, cumul_g)
             beta_g = jnp.where(lane == h, beta_col, beta_g)
             across = jnp.where(level == h, jnp.sum(gaps, axis=0, keepdims=True), across)
-        q_along = jnp.sum(qn * qhat_g, axis=1, keepdims=True)
         k_along = jnp.sum(khat * khat_g, axis=1, keepdims=True)
-        dq_ref[0, :, cut] = ((x.q_scale[j] * QSCALE) * (qhat_g - qn * q_along)).astype(BF16)
         dk_ref[0, :, cut] = (x.k_scale[j] * (khat_g - khat * k_along)).astype(BF16)
     db_ref[0] = beta_g.T
-    dg_ref[0] = exact(cumul_g.T - across, (row >= col).astype(F32))
-
-
-def gradients_on(turn, at_ref, *refs):
-    *held, sems = refs[-13:]
-    far_in = refs[:7]
-    far_out = refs[7 + (1 if turn else 6) :][:5]
+    dg_ref[0] = exact(part_dg_ref[0] + cumul_g.T - across, (row >= col).astype(F32))
+
+
+def fetched(kernel, count, refs, scratch):
+    *held, sems = scratch
+    fetches = [pltpu.make_async_copy(refs[i], held[i], sems.at[i]) for i in range(count)]
+    for copy in fetches:
+        copy.start()
+    for copy in fetches:
+        copy.wait()
+    kernel(*held)
+    puts = [pltpu.make_async_copy(held[i], refs[i], sems.at[i]) for i in range(count, len(refs))]
+    for copy in puts:
+        copy.start()
+    for copy in puts:
+        copy.wait()
+
+
+def query_gradients_on(turn, at_ref, *refs):
+    outs = refs[8:16] if turn else refs[16:24]
 
     @pl.when(at_ref[0] == turn)
     def _():
-        fetches = [pltpu.make_async_copy(far_in[i], held[i], sems.at[i]) for i in range(7)]
-        for copy in fetches:
-            copy.start()
-        for copy in fetches:
-            copy.wait()
-        gradients(*held)
-        puts = [pltpu.make_async_copy(held[7 + i], far_out[i], sems.at[7 + i]) for i in range(5)]
-        for copy in puts:
-            copy.start()
-        for copy in puts:
-            copy.wait()
+        fetched(query_gradients, 7, (*refs[:7], *outs), refs[-16:])
+
+
+def all_gradients(*refs):
+    fetched(gradients, 15, refs[:19], refs[19:])
 
 
 def whole(x):
@@ -451,9 +548,8 @@
     square = (heads, BLOCK, DK)
     unit = 2 * BLOCK**3 * heads
 
-    def own_half(states):
-        parts = states.reshape(blocks, HALF, DK)
-        return lax.dynamic_index_in_dim(parts, here, 0, keepdims=False)
+    def halves(states):
+        return fixed(states.reshape(blocks, HALF, DK))
 
     with jax.named_scope("gather_grad"):
         grads = [output_grad]
@@ -465,7 +561,7 @@
     dma = pltpu.SemaphoreType.DMA
     with jax.named_scope("local_maps"):
         args = tuple(map(fixed, (queries, key_rows, value_rows, log_decay, write_rate)))
-        outs = [far((blocks, 2 * DK, DK), BF16)] + [far(square, BF16)] * 2
+        outs = [far((blocks, DK + HALF, DK), BF16)] + [far(square, BF16)] * 2
         maps, qe, o0 = call(
             local_maps, outs, *args,
             ins=[FAR] * 5, out_specs=[FAR] * 3,
@@ -475,14 +571,16 @@
             + [dma((5,)), dma((2, 3))],
             flops=50 * unit,
         )
+    with jax.named_scope("send_maps"):
+        maps = lax.all_to_all(maps, "ctx", 0, 0, tiled=True)
     with jax.named_scope("head_grads"):
         place = jnp.stack([core, lax.axis_index("tp")])
         gather = pltpu.VMEM((feats,) + output_grad.shape[1:], BF16)
-        maps, head_grad = call(
+        backs, head_grad = call(
             head_grads,
-            [far(maps.shape, BF16), shape((BLOCK, wide), BF16)],
-            place, *grads, fixed(output_matrix), other_matrix, fixed(qe), fixed(maps),
-            ins=[SCALAR] + [HELD] * feats + [FAR, HELD, FAR, FAR],
+            [far((blocks, HALF, DK), BF16), shape((BLOCK, wide), BF16)],
+            place, *grads, fixed(output_matrix), other_matrix, fixed(qe),
+            ins=[SCALAR] + [HELD] * feats + [FAR, HELD, FAR],
             out_specs=[FAR, HELD],
             scratch=[
                 gather,
@@ -493,23 +591,30 @@
                 dma((2,)),
             ],
             flops=18 * unit,
-            input_output_aliases={feats + 4: 0},
-        )
-    with jax.named_scope("send_maps"):
-        maps = lax.all_to_all(maps, "ctx", 0, 0, tiled=True)
+        )
     with jax.named_scope("grad_rows"):
         mine, theirs = call(
             grad_rows, [shape((rows, BLOCK), BF16)] * 2, place, *grads,
             ins=[SCALAR] + [HELD] * feats, scratch=[gather],
         )
         theirs = lax.ppermute(theirs, "dp", swap)
-    with jax.named_scope("chain"):
+    pieces = (blocks, piece, wide)
+    buffer = far((blocks, piece, wide + DK), BF16)
+    with jax.named_scope("forward_chain"):
+        maps = fixed(maps)
         states, = call(
-            chain, [far((blocks, 2 * HALF, DK), BF16)],
-            maps, own_half(initial_state), own_half(final_state_grad),
-            out_specs=[FAR],
-            scratch=[pltpu.VMEM((blocks, 2 * HALF, DK), BF16), dma((4, 2))],
-            flops=4 * unit,
+            forward_chain, [far((blocks, 2 * HALF, DK), BF16)],
+            here.reshape(1), maps, fixed(backs), halves(initial_state),
+            ins=[SCALAR] + [FAR] * 3, out_specs=[FAR],
+            scratch=[
+                pltpu.VMEM(maps.shape, BF16),
+                pltpu.VMEM((blocks, 2 * HALF, DK), BF16),
+                pltpu.VMEM((HALF, DK), F32),
+                dma((2,)),
+                dma((4,)),
+                dma((4,)),
+            ],
+            flops=2 * unit,
         )
     with jax.named_scope("return_states"):
         states = lax.all_to_all(states, "ctx", 0, 0, tiled=True)
@@ -518,28 +623,50 @@
             outputs, [shape((BLOCK, wide), BF16)], qe, o0, states, flops=unit
         )
         other_low = lax.ppermute(heads_low, "dp", swap)
+    with jax.named_scope("backward_chain"):
+        partial, = call(
+            backward_chain, [buffer], here.reshape(1), maps, states, halves(final_state_grad),
+            ins=[SCALAR, FAR, HELD, FAR], out_specs=[FAR],
+            scratch=[
+                pltpu.VMEM((blocks, DK, DK), BF16),
+                pltpu.VMEM((blocks, HALF, DK), BF16),
+                pltpu.VMEM((HALF, DK), F32),
+                dma(()),
+                dma((4,)),
+                dma((4,)),
+            ],
+            flops=2 * unit,
+        )
     with jax.named_scope("projection"):
-        pieces = (blocks, piece, wide)
         partial, = call(
-            projection, [far(pieces, BF16)], mine, theirs, heads_low, other_low,
-            out_specs=[FAR], scratch=[pltpu.VMEM(pieces, BF16), dma((4,))], flops=16 * unit,
-        )
+            projection, [buffer], mine, theirs, heads_low, other_low, fixed(partial),
+            ins=[HELD] * 4 + [FAR], out_specs=[FAR],
+            scratch=[pltpu.VMEM(pieces, BF16), dma((4,))], flops=16 * unit,
+            input_output_aliases={4: 0},
+        )
+
+    def holding(*arrays):
+        return [pltpu.VMEM(x.shape, x.dtype) for x in arrays] + [dma((len(arrays),))]
+
     with jax.named_scope("gradients"):
         args += (head_grad, states)
-        outs = [far(x.shape, x.dtype) for x in args[:5]]
-        held = [pltpu.VMEM(x.shape, x.dtype) for x in args + args[:5]] + [dma((12,))]
-        *found, partial = call(
-            functools.partial(gradients_on, 1), outs + [far(pieces, BF16)],
+        results = [
+            far(queries.shape, BF16), far(key_rows.shape, F32), far(log_decay.shape, F32),
+            far(square, F32), *[far(square, BF16)] * 4,
+        ]
+        held = holding(*args, *results)
+        *results, partial = call(
+            functools.partial(query_gradients_on, 1), results + [buffer],
             core.reshape(1), *args, fixed(partial),
-            ins=[SCALAR] + [FAR] * 8, out_specs=[FAR] * 6, scratch=held, flops=35 * unit,
-            input_output_aliases={8: 5},
+            ins=[SCALAR] + [FAR] * 8, out_specs=[FAR] * 9, scratch=held,
+            flops=35 * unit, input_output_aliases={8: 8},
         )
     with jax.named_scope("projection"):
         partial = lax.all_to_all(partial, "ctx", 0, 0, tiled=True)
-        spread, = call(
+        spread, backs = call(
             functools.partial(reduce_spread, float(BLOCK * blocks * lax.axis_size("dp")) ** (-0.5)),
-            [far(pieces, BF16)], partial,
-            out_specs=[FAR], scratch=[pltpu.VMEM((piece, wide), BF16), dma((blocks, 2))],
+            [far(pieces, BF16), far((blocks, HALF, DK), BF16)], partial, out_specs=[FAR] * 2,
+            scratch=[pltpu.VMEM((piece, wide), BF16), dma(()), dma((blocks, 2))],
         )
         total = lax.all_to_all(spread, "ctx", 0, 0, tiled=True).reshape(rows, wide)
         weight_grad, = call(
@@ -547,11 +674,19 @@
             out_specs=[FAR], scratch=[pltpu.VMEM((rows, wide), F32), dma((8,))],
         )
     with jax.named_scope("gradients"):
-        query_g, key_g, value_g, decay_g, rate_g = call(
-            functools.partial(gradients_on, 0), outs,
-            core.reshape(1), *args, fixed(spread), *map(fixed, found),
-            ins=[SCALAR] + [FAR] * 13, out_specs=[FAR] * 5, scratch=held, flops=35 * unit,
-            input_output_aliases={9 + i: i for i in range(5)},
+        results = call(
+            functools.partial(query_gradients_on, 0), [far(x.shape, x.dtype) for x in results],
+            core.reshape(1), *args, fixed(spread), *map(fixed, results),
+            ins=[SCALAR] + [FAR] * 16, out_specs=[FAR] * 8, scratch=held,
+            flops=35 * unit, input_output_aliases={9 + i: i for i in range(8)},
+        )
+        query_g, *shares = results
+        outs = [far(x.shape, x.dtype) for x in args[1:5]]
+        args += (fixed(backs), *map(fixed, shares))
+        key_g, value_g, decay_g, rate_g = call(
+            all_gradients, outs, *args,
+            ins=[FAR] * 15, out_specs=[FAR] * 4, scratch=holding(*args, *outs),
+            flops=35 * unit,
         )
     return (query_g, key_g, value_g, decay_g, rate_g, weight_grad)
 

time: 125 us -> 123 us (0.984)
  waiting for transfers between devices: 39.9 us -> 24 us
  Pallas kernels: 31.5 us -> 43.3 us
  blocking collectives: 22 us -> 25.1 us
    all_to_all x1, waiting for transfers between devices: 14.4 us -> 0.01 us  [body(): maps = lax.all_to_all(maps, 'ctx', 0, 0, tiled=True)]
    pallas_call x10 -> x12, Pallas kernels: 31.5 us -> 43.3 us  [call(): pl.pallas_call(kernel, grid=grid, out_shape=outs, in_specs=[HELD] * len(a...]
    all_to_all x1, waiting for transfers between devices: 19 us -> 12.4 us  [body(): total = lax.all_to_all(spread, 'ctx', 0, 0, tiled=True).reshape(rows, wide)]
    ppermute x3, waiting for transfers between devices: 0.01 us -> 5.01 us  [body(): grads.append(lax.ppermute(output_grad, 'tp', pairs))]
    all_to_all x1, blocking collectives: 22 us -> 25.1 us  [body(): partial = lax.all_to_all(partial, 'ctx', 0, 0, tiled=True)]
    all_to_all x1, starting transfers between devices: 3.93 us -> 6.2 us  [body(): states = lax.all_to_all(states, 'ctx', 0, 0, tiled=True)]
    all_to_all x1, waiting for transfers between devices: 5.26 us -> 6.56 us  [body(): states = lax.all_to_all(states, 'ctx', 0, 0, tiled=True)]
  transfers between devices with their start and end apart: 9 -> 9, of which waited for: 4 -> 4; matrix products, arithmetic and copies ran while one was open for 1% -> 0% of each run, Pallas kernels for 7% -> 19%
where the time goes in v5:
time: 123 us
  Pallas kernels  43.3 us (35%)
  starting transfers between devices  29.4 us (24%)
  blocking collectives  25.1 us (20%)
  waiting for transfers between devices  24 us (20%)
    pallas_call x12, Pallas kernels, call(): pl.pallas_call(kernel, grid=grid, out_shape=outs, in_specs=[HELD] * len(a...  43.3 us
    all_to_all x1, blocking collectives, body(): partial = lax.all_to_all(partial, 'ctx', 0, 0, tiled=True)  25.1 us
    all_to_all x1, waiting for transfers between devices, body(): total = lax.all_to_all(spread, 'ctx', 0, 0, tiled=True).reshape(rows, wide)  12.4 us
    all_to_all x1, starting transfers between devices, body(): maps = lax.all_to_all(maps, 'ctx', 0, 0, tiled=True)  7.9 us
    all_to_all x1, waiting for transfers between devices, body(): states = lax.all_to_all(states, 'ctx', 0, 0, tiled=True)  6.56 us
    all_to_all x1, starting transfers between devices, body(): states = lax.all_to_all(states, 'ctx', 0, 0, tiled=True)  6.2 us
    ppermute x3, waiting for transfers between devices, body(): grads.append(lax.ppermute(output_grad, 'tp', pairs))  5.01 us
    ppermute x3, starting transfers between devices, body(): grads.append(lax.ppermute(output_grad, 'tp', pairs))  4.88 us
  transfers between devices with their start and end apart: 9, of which 4 were waited for; matrix products, arithmetic and copies ran while one was open for 0% of the time, Pallas kernels for 19%

profile of v5, /device:TPU:1, one launch (start us, length us, event | category | flops | bytes accessed | tf_op | source)
XLA Modules:
  0.0 122.8 jit_solution(17419046501770110739)
XLA Ops:
  0.6 0.0 copy-start.1
  0.6 1.5 %collective-permute-start.3 = (bf16[1024,1024]{1,0:T(8,128)(2,1)}, bf16[1024,1024]{1,0:T(8,128)(2,1)S(1)}, u32[]{:S(2)}, u32[]{:S(2)}) collective-permute-start(bf16[1024,1024]{1,0:T(8,128)(2,1)} %own_hbm.1), channel_id=1, source_target_pairs={{0,1},{1,0},{2,3},{3,2},{4,5},{5,4},{6,7},{7,6},{8,9},{9,8},{10,11... | collective-permute-start | bytes 6291464 | tf_op jit(solution)/shard_map/other_rows/ppermute | solution.py:560
  2.1 6.9 %local_maps.1 = (bf16[16,192,128]{2,1,0:T(8,128)(2,1)}, bf16[8,128,128]{2,1,0:T(8,128)(2,1)}, bf16[8,128,128]{2,1,0:T(8,128)(2,1)}) custom-call(bf16[1,128,512]{2,1,0:T(8,128)(2,1)} %refs_0_.7, bf16[1,128,512]{2,1,0:T(8,128)(2,1)} %refs_1_.7, bf16[1,128,1024]{2,1,0:T(8,128)(2,1)} %refs_2_.7, f32[1,8,128]{2,1,0:T(8,128)} %refs_3_.7, f32[1,8,128]{2,1,0:T(8,128)} %refs_4_.7), custom_call_target="tpu_custom_call" | custom-call | flops 1677721600 | bytes 1843200 | tf_op jit(solution)/shard_map/local_maps/pallas_call | solution.py:512
  9.0 7.9 %all-to-all-start = ((bf16[16,192,128]{2,1,0:T(8,128)(2,1)}), bf16[16,192,128]{2,1,0:T(8,128)(2,1)}, u32[]{:S(2)}, u32[]{:S(2)}) async-start(bf16[16,192,128]{2,1,0:T(8,128)(2,1)} %get-tuple-element.38), calls=%async_computation | async-start | bytes 1572864 | tf_op jit(solution)/shard_map/send_maps/all_to_all | solution.py:575
  17.0 0.0 copy-done.1
  17.0 1.3 %collective-permute-start.2 = (bf16[1,128,512]{2,1,0:T(8,128)(2,1)S(1)}, bf16[1,128,512]{2,1,0:T(8,128)(2,1)S(1)}, u32[]{:S(2)}, u32[]{:S(2)}) collective-permute-start(bf16[1,128,512]{2,1,0:T(8,128)(2,1)S(1)} %copy-done.1), channel_id=1, source_target_pairs={{6,0},{0,2},{2,4},{4,6},{7,1},{1,3},{3,5},{5,7},{14,8},{8,10},{10,... | collective-permute-start | bytes 393224 | tf_op jit(solution)/shard_map/gather_grad/ppermute | solution.py:558
  18.2 2.5 %collective-permute-start.1 = (bf16[1,128,512]{2,1,0:T(8,128)(2,1)S(1)}, bf16[1,128,512]{2,1,0:T(8,128)(2,1)S(1)}, u32[]{:S(2)}, u32[]{:S(2)}) collective-permute-start(bf16[1,128,512]{2,1,0:T(8,128)(2,1)S(1)} %copy-done.1), channel_id=1, source_target_pairs={{4,0},{6,2},{0,4},{2,6},{5,1},{7,3},{1,5},{3,7},{12,8},{14,10},{8,... | collective-permute-start | bytes 393224 | tf_op jit(solution)/shard_map/gather_grad/ppermute | solution.py:558
  20.7 1.1 collective-permute-start
  21.8 0.1 pad_add_fusion.at_ref
  21.9 1.2 collective-permute-done.2.g3_ref
  23.1 3.8 %collective-permute-done.1.g2_ref = bf16[1,128,512]{2,1,0:T(8,128)(2,1)S(1)} collective-permute-done((bf16[1,128,512]{2,1,0:T(8,128)(2,1)S(1)}, bf16[1,128,512]{2,1,0:T(8,128)(2,1)S(1)}, u32[]{:S(2)}, u32[]{:S(2)}) %collective-permute-start.1) | collective-permute-done | bytes 131104 | tf_op jit(solution)/shard_map/gather_grad/ppermute | solution.py:558
  26.9 0.0 collective-permute-done.g1_ref
  26.9 0.0 collective-permute-done.3.other_ref
  26.9 3.6 %head_grads.1 = (bf16[16,64,128]{2,1,0:T(8,128)(2,1)}, bf16[128,1024]{1,0:T(8,128)(2,1)S(1)}) custom-call(s32[2]{0:T(128)S(1)} %pad_add_fusion.at_ref, bf16[1,128,512]{2,1,0:T(8,128)(2,1)S(1)} %copy-done.1, bf16[1,128,512]{2,1,0:T(8,128)(2,1)S(1)} %collective-permute-done.g1_ref, bf16[1,128,512]{2,1,0:T(8,128)(2,1)S(1)} %collective-permute-done.1.g2_ref, ...), custom_call_target="tpu_custom_call" | custom-call | flops 603979776 | bytes 5505032 | tf_op jit(solution)/shard_map/head_grads/pallas_call | solution.py:512
  30.5 0.0 copy-start
  30.5 0.0 copy-start.2
  30.5 0.0 all-to-all-done.maps_hbm
  30.6 3.8 %forward_chain.1 = bf16[16,128,128]{2,1,0:T(8,128)(2,1)} custom-call(s32[1]{0:T(128)} %bitcast.2.at_ref, bf16[16,192,128]{2,1,0:T(8,128)(2,1)} %all-to-all-done.maps_hbm, bf16[16,64,128]{2,1,0:T(8,128)(2,1)} %get-tuple-element.39.back_hbm, f32[16,64,128]{2,1,0:T(8,128)} %bitcast.7), custom_call_target="tpu_custom_call" | custom-call | flops 67108864 | bytes 2097156 | tf_op jit(solution)/shard_map/forward_chain/pallas_call | solution.py:512
  34.3 6.2 %all-to-all-start.1 = ((bf16[16,128,128]{2,1,0:T(8,128)(2,1)}), bf16[16,128,128]{2,1,0:T(8,128)(2,1)S(1)}, u32[]{:S(2)}, u32[]{:S(2)}) async-start(bf16[16,128,128]{2,1,0:T(8,128)(2,1)} %forward_chain.1), calls=%async_computation.1 | async-start | bytes 1048576 | tf_op jit(solution)/shard_map/return_states/all_to_all | solution.py:620
  40.5 0.8 grad_rows.1
  41.3 1.8 %collective-permute-start.4 = (bf16[1024,128]{1,0:T(8,128)(2,1)S(1)}, bf16[1024,128]{1,0:T(8,128)(2,1)S(1)}, u32[]{:S(2)}, u32[]{:S(2)}) collective-permute-start(bf16[1024,128]{1,0:T(8,128)(2,1)S(1)} %get-tuple-element.41), channel_id=1, source_target_pairs={{0,1},{1,0},{2,3},{3,2},{4,5},{5,4},{6,7},{7,6},{8,9},{9,8},{10,11... | collective-permute-start | bytes 786440 | tf_op jit(solution)/shard_map/grad_rows/ppermute | solution.py:600
  43.1 6.6 %all-to-all-done.1.y_ref.in_ref.refs_6_ = bf16[16,128,128]{2,1,0:T(8,128)(2,1)S(1)} async-done(((bf16[16,128,128]{2,1,0:T(8,128)(2,1)}), bf16[16,128,128]{2,1,0:T(8,128)(2,1)S(1)}, u32[]{:S(2)}, u32[]{:S(2)}) %all-to-all-start.1) | async-done | bytes 524320 | tf_op jit(solution)/shard_map/return_states/all_to_all | solution.py:620
  49.7 0.0 copy-done
  49.7 0.0 copy-done.2
  49.7 0.3 outputs.1.low_ref
  50.0 3.4 %collective-permute-start.5 = (bf16[128,1024]{1,0:T(8,128)(2,1)S(1)}, bf16[128,1024]{1,0:T(8,128)(2,1)S(1)}, u32[]{:S(2)}, u32[]{:S(2)}) collective-permute-start(bf16[128,1024]{1,0:T(8,128)(2,1)S(1)} %outputs.1.low_ref), channel_id=1, source_target_pairs={{0,1},{1,0},{2,3},{3,2},{4,5},{5,4},{6,7},{7,6},{8,9},{9,8},{10,11... | collective-permute-start | bytes 786440 | tf_op jit(solution)/shard_map/outputs/ppermute | solution.py:625
  53.4 3.7 %backward_chain.1.in_ref = bf16[16,64,1152]{2,1,0:T(8,128)(2,1)} custom-call(s32[1]{0:T(128)} %bitcast.2.at_ref, bf16[16,192,128]{2,1,0:T(8,128)(2,1)} %all-to-all-done.maps_hbm, bf16[16,128,128]{2,1,0:T(8,128)(2,1)S(1)} %all-to-all-done.1.y_ref.in_ref.refs_6_, f32[16,64,128]{2,1,0:T(8,128)} %bitcast.8), custom_call_target="tpu_custom_call" | custom-call | flops 67108864 | bytes 4194308 | tf_op jit(solution)/shard_map/backward_chain/pallas_call | solution.py:512
  57.1 0.0 collective-permute-done.4.theirs_ref
  57.1 0.0 collective-permute-done.5.other_ref
  57.1 1.7 %projection.3.refs_7_ = bf16[16,64,1152]{2,1,0:T(8,128)(2,1)} custom-call(bf16[1024,128]{1,0:T(8,128)(2,1)S(1)} %get-tuple-element.40.mine_ref, bf16[1024,128]{1,0:T(8,128)(2,1)S(1)} %collective-permute-done.4.theirs_ref, bf16[128,1024]{1,0:T(8,128)(2,1)S(1)} %outputs.1.low_ref, ...), custom_call_target="tpu_custom_call", output_to_operand_aliasing={{}: (4, {})} | custom-call | flops 536870912 | bytes 5767168 | tf_op jit(solution)/shard_map/projection/pallas_call | solution.py:512
  58.8 10.7 %gradients.3 = (bf16[1,128,512]{2,1,0:T(8,128)(2,1)}, f32[1,128,512]{2,1,0:T(8,128)}, f32[1,8,128]{2,1,0:T(8,128)}, f32[8,128,128]{2,1,0:T(8,128)}, bf16[8,128,1...) custom-call(s32[1]{0:T(128)} %bitcast.at_ref, ...), custom_call_target="tpu_custom_call", output_to_operand_aliasing={{8}: (8, {})} | custom-call | flops 1174405120 | bytes 8007684 | tf_op jit(solution)/shard_map/gradients/pallas_call | solution.py:512
  69.4 25.1 %all_to_all.20.pieces_ref = bf16[16,64,1152]{2,1,0:T(8,128)(2,1)S(1)} all-to-all(bf16[16,64,1152]{2,1,0:T(8,128)(2,1)} %get-tuple-element.43), channel_id=1, replica_groups=mesh['ctx'=16,'tp'=4,'dp'=2] {'ctx'}, dimensions={0} | all-to-all | bytes 4718592 | tf_op jit(solution)/shard_map/projection/all_to_all | solution.py:665
  94.5 1.8 %projection.4 = (bf16[16,64,1024]{2,1,0:T(8,128)(2,1)}, bf16[16,64,128]{2,1,0:T(8,128)(2,1)}) custom-call(bf16[16,64,1152]{2,1,0:T(8,128)(2,1)S(1)} %all_to_all.20.pieces_ref), custom_call_target="tpu_custom_call" | custom-call | bytes 4718592 | tf_op jit(solution)/shard_map/projection/pallas_call | solution.py:512
  96.3 3.7 %all-to-all-start.3 = ((bf16[16,64,1024]{2,1,0:T(8,128)(2,1)}), bf16[16,64,1024]{2,1,0:T(8,128)(2,1)S(1)}, u32[]{:S(2)}, u32[]{:S(2)}) async-start(bf16[16,64,1024]{2,1,0:T(8,128)(2,1)} %get-tuple-element.44.refs_7_), calls=%async_computation.3 | async-start | bytes 4194304 | tf_op jit(solution)/shard_map/projection/all_to_all | solution.py:671
  100.1 0.4 gradients.4
  100.4 7.7 %gradients.5 = (bf16[1,128,512]{2,1,0:T(8,128)(2,1)}, bf16[1,128,1024]{2,1,0:T(8,128)(2,1)}, f32[1,8,128]{2,1,0:T(8,128)}, f32[1,8,128]{2,1,0:T(8,128)}) custom-call(bf16[1,128,512]{2,1,0:T(8,128)(2,1)} %refs_0_.7, bf16[1,128,512]{2,1,0:T(8,128)(2,1)} %refs_1_.7, bf16[1,128,1024]{2,1,0:T(8,128)(2,1)} %refs_2_.7, f32[1,8,128]{2,1,0:T(8,128)} %refs_3_.7, ...), custom_call_target="tpu_custom_call" | custom-call | flops 1174405120 | bytes 3821568 | tf_op jit(solution)/shard_map/gradients/pallas_call | solution.py:512
  108.2 12.4 %all-to-all-done.3 = bf16[16,64,1024]{2,1,0:T(8,128)(2,1)S(1)} async-done(((bf16[16,64,1024]{2,1,0:T(8,128)(2,1)}), bf16[16,64,1024]{2,1,0:T(8,128)(2,1)S(1)}, u32[]{:S(2)}, u32[]{:S(2)}) %all-to-all-start.3) | async-done | bytes 2097184 | tf_op jit(solution)/shard_map/projection/all_to_all | solution.py:671
  120.5 2.1 %projection.5 = f32[1024,1024]{1,0:T(8,128)} custom-call(bf16[1024,1024]{1,0:T(8,128)(2,1)S(1)} %bitcast.6), custom_call_target="tpu_custom_call" | custom-call | bytes 6291456 | tf_op jit(solution)/shard_map/projection/pallas_call | solution.py:512
Async XLA Ops:
  0.6 16.3 %copy-start.1 = (bf16[1,128,512]{2,1,0:T(8,128)(2,1)S(1)}, bf16[1,128,512]{2,1,0:T(8,128)(2,1)}, u32[]{:S(2)}) copy-start(bf16[1,128,512]{2,1,0:T(8,128)(2,1)} %g0_ref.3) | copy-start | bytes 393220
  0.6 26.3 %collective-permute-start.3 = (bf16[1024,1024]{1,0:T(8,128)(2,1)}, bf16[1024,1024]{1,0:T(8,128)(2,1)S(1)}, u32[]{:S(2)}, u32[]{:S(2)}) collective-permute-start(bf16[1024,1024]{1,0:T(8,128)(2,1)} %own_hbm.1), channel_id=1, source_target_pairs={{0,1},{1,0},{2,3},{3,2},{4,5},{5,4},{6,7},{7,6},{8,9},{9,8},{10,11... | collective-permute-start | bytes 6291464 | tf_op jit(solution)/shard_map/other_rows/ppermute | solution.py:560
  9.0 21.5 %all-to-all-start = ((bf16[16,192,128]{2,1,0:T(8,128)(2,1)}), bf16[16,192,128]{2,1,0:T(8,128)(2,1)}, u32[]{:S(2)}, u32[]{:S(2)}) async-start(bf16[16,192,128]{2,1,0:T(8,128)(2,1)} %get-tuple-element.38), calls=%async_computation | async-start | bytes 1572864 | tf_op jit(solution)/shard_map/send_maps/all_to_all | solution.py:575
  17.0 6.2 %collective-permute-start.2 = (bf16[1,128,512]{2,1,0:T(8,128)(2,1)S(1)}, bf16[1,128,512]{2,1,0:T(8,128)(2,1)S(1)}, u32[]{:S(2)}, u32[]{:S(2)}) collective-permute-start(bf16[1,128,512]{2,1,0:T(8,128)(2,1)S(1)} %copy-done.1), channel_id=1, source_target_pairs={{6,0},{0,2},{2,4},{4,6},{7,1},{1,3},{3,5},{5,7},{14,8},{8,10},{10,... | collective-permute-start | bytes 393224 | tf_op jit(solution)/shard_map/gather_grad/ppermute | solution.py:558
  18.2 8.7 %collective-permute-start.1 = (bf16[1,128,512]{2,1,0:T(8,128)(2,1)S(1)}, bf16[1,128,512]{2,1,0:T(8,128)(2,1)S(1)}, u32[]{:S(2)}, u32[]{:S(2)}) collective-permute-start(bf16[1,128,512]{2,1,0:T(8,128)(2,1)S(1)} %copy-done.1), channel_id=1, source_target_pairs={{4,0},{6,2},{0,4},{2,6},{5,1},{7,3},{1,5},{3,7},{12,8},{14,10},{8,... | collective-permute-start | bytes 393224 | tf_op jit(solution)/shard_map/gather_grad/ppermute | solution.py:558
  20.7 6.2 %collective-permute-start = (bf16[1,128,512]{2,1,0:T(8,128)(2,1)S(1)}, bf16[1,128,512]{2,1,0:T(8,128)(2,1)S(1)}, u32[]{:S(2)}, u32[]{:S(2)}) collective-permute-start(bf16[1,128,512]{2,1,0:T(8,128)(2,1)S(1)} %copy-done.1), channel_id=1, source_target_pairs={{2,0},{4,2},{6,4},{0,6},{3,1},{5,3},{7,5},{1,7},{10,8},{12,10},{14... | collective-permute-start | bytes 393224 | tf_op jit(solution)/shard_map/gather_grad/ppermute | solution.py:558
  30.5 19.2 %copy-start = (bf16[8,128,128]{2,1,0:T(8,128)(2,1)S(1)}, bf16[8,128,128]{2,1,0:T(8,128)(2,1)}, u32[]{:S(2)}) copy-start(bf16[8,128,128]{2,1,0:T(8,128)(2,1)} %get-tuple-element.36.qe_hbm.qe_ref) | copy-start | bytes 786436
  30.5 19.1 %copy-start.2 = (bf16[8,128,128]{2,1,0:T(8,128)(2,1)S(1)}, bf16[8,128,128]{2,1,0:T(8,128)(2,1)}, u32[]{:S(2)}) copy-start(bf16[8,128,128]{2,1,0:T(8,128)(2,1)} %get-tuple-element.42.o0_ref) | copy-start | bytes 786436
  34.3 15.4 %all-to-all-start.1 = ((bf16[16,128,128]{2,1,0:T(8,128)(2,1)}), bf16[16,128,128]{2,1,0:T(8,128)(2,1)S(1)}, u32[]{:S(2)}, u32[]{:S(2)}) async-start(bf16[16,128,128]{2,1,0:T(8,128)(2,1)} %forward_chain.1), calls=%async_computation.1 | async-start | bytes 1048576 | tf_op jit(solution)/shard_map/return_states/all_to_all | solution.py:620
  41.3 15.8 %collective-permute-start.4 = (bf16[1024,128]{1,0:T(8,128)(2,1)S(1)}, bf16[1024,128]{1,0:T(8,128)(2,1)S(1)}, u32[]{:S(2)}, u32[]{:S(2)}) collective-permute-start(bf16[1024,128]{1,0:T(8,128)(2,1)S(1)} %get-tuple-element.41), channel_id=1, source_target_pairs={{0,1},{1,0},{2,3},{3,2},{4,5},{5,4},{6,7},{7,6},{8,9},{9,8},{10,11... | collective-permute-start | bytes 786440 | tf_op jit(solution)/shard_map/grad_rows/ppermute | solution.py:600
  50.0 7.1 %collective-permute-start.5 = (bf16[128,1024]{1,0:T(8,128)(2,1)S(1)}, bf16[128,1024]{1,0:T(8,128)(2,1)S(1)}, u32[]{:S(2)}, u32[]{:S(2)}) collective-permute-start(bf16[128,1024]{1,0:T(8,128)(2,1)S(1)} %outputs.1.low_ref), channel_id=1, source_target_pairs={{0,1},{1,0},{2,3},{3,2},{4,5},{5,4},{6,7},{7,6},{8,9},{9,8},{10,11... | collective-permute-start | bytes 786440 | tf_op jit(solution)/shard_map/outputs/ppermute | solution.py:625
  96.3 24.2 %all-to-all-start.3 = ((bf16[16,64,1024]{2,1,0:T(8,128)(2,1)}), bf16[16,64,1024]{2,1,0:T(8,128)(2,1)S(1)}, u32[]{:S(2)}, u32[]{:S(2)}) async-start(bf16[16,64,1024]{2,1,0:T(8,128)(2,1)} %get-tuple-element.44.refs_7_), calls=%async_computation.3 | async-start | bytes 4194304 | tf_op jit(solution)/shard_map/projection/all_to_all | solution.py:671

commit v6 on v5

--- a/solution.py
+++ b/solution.py
@@ -641,7 +641,7 @@
         partial, = call(
             projection, [buffer], mine, theirs, heads_low, other_low, fixed(partial),
             ins=[HELD] * 4 + [FAR], out_specs=[FAR],
-            scratch=[pltpu.VMEM(pieces, BF16), dma((4,))], flops=16 * unit,
+            scratch=[pltpu.VMEM(pieces, BF16), dma((8,))], flops=16 * unit,
             input_output_aliases={4: 0},
         )
 

time: 123 us -> 123 us (level)
  no operation moved by 1% of the time
where the time goes in v6:
time: 123 us
  Pallas kernels  43.3 us (35%)
  starting transfers between devices  29.4 us (24%)
  blocking collectives  25.1 us (20%)
  waiting for transfers between devices  23.9 us (19%)
    pallas_call x12, Pallas kernels, call(): pl.pallas_call(kernel, grid=grid, out_shape=outs, in_specs=[HELD] * len(a...  43.3 us
    all_to_all x1, blocking collectives, body(): partial = lax.all_to_all(partial, 'ctx', 0, 0, tiled=True)  25.1 us
    all_to_all x1, waiting for transfers between devices, body(): total = lax.all_to_all(spread, 'ctx', 0, 0, tiled=True).reshape(rows, wide)  12.4 us
    all_to_all x1, starting transfers between devices, body(): maps = lax.all_to_all(maps, 'ctx', 0, 0, tiled=True)  7.9 us
    all_to_all x1, waiting for transfers between devices, body(): states = lax.all_to_all(states, 'ctx', 0, 0, tiled=True)  6.56 us
    all_to_all x1, starting transfers between devices, body(): states = lax.all_to_all(states, 'ctx', 0, 0, tiled=True)  6.2 us
    ppermute x3, waiting for transfers between devices, body(): grads.append(lax.ppermute(output_grad, 'tp', pairs))  5.01 us
    ppermute x3, starting transfers between devices, body(): grads.append(lax.ppermute(output_grad, 'tp', pairs))  4.88 us
  transfers between devices with their start and end apart: 9, of which 4 were waited for; matrix products, arithmetic and copies ran while one was open for 0% of the time, Pallas kernels for 19%

profile of v6, /device:TPU:1, one launch (start us, length us, event | category | flops | bytes accessed | tf_op | source)
XLA Modules:
  0.0 122.8 jit_solution(7877435450282808033)
XLA Ops:
  0.6 0.0 copy-start.1
  0.6 1.5 %collective-permute-start.3 = (bf16[1024,1024]{1,0:T(8,128)(2,1)}, bf16[1024,1024]{1,0:T(8,128)(2,1)S(1)}, u32[]{:S(2)}, u32[]{:S(2)}) collective-permute-start(bf16[1024,1024]{1,0:T(8,128)(2,1)} %own_hbm.1), channel_id=1, source_target_pairs={{0,1},{1,0},{2,3},{3,2},{4,5},{5,4},{6,7},{7,6},{8,9},{9,8},{10,11... | collective-permute-start | bytes 6291464 | tf_op jit(solution)/shard_map/other_rows/ppermute | solution.py:560
  2.1 6.9 %local_maps.1 = (bf16[16,192,128]{2,1,0:T(8,128)(2,1)}, bf16[8,128,128]{2,1,0:T(8,128)(2,1)}, bf16[8,128,128]{2,1,0:T(8,128)(2,1)}) custom-call(bf16[1,128,512]{2,1,0:T(8,128)(2,1)} %refs_0_.7, bf16[1,128,512]{2,1,0:T(8,128)(2,1)} %refs_1_.7, bf16[1,128,1024]{2,1,0:T(8,128)(2,1)} %refs_2_.7, f32[1,8,128]{2,1,0:T(8,128)} %refs_3_.7, f32[1,8,128]{2,1,0:T(8,128)} %refs_4_.7), custom_call_target="tpu_custom_call" | custom-call | flops 1677721600 | bytes 1843200 | tf_op jit(solution)/shard_map/local_maps/pallas_call | solution.py:512
  9.0 7.9 %all-to-all-start = ((bf16[16,192,128]{2,1,0:T(8,128)(2,1)}), bf16[16,192,128]{2,1,0:T(8,128)(2,1)}, u32[]{:S(2)}, u32[]{:S(2)}) async-start(bf16[16,192,128]{2,1,0:T(8,128)(2,1)} %get-tuple-element.38), calls=%async_computation | async-start | bytes 1572864 | tf_op jit(solution)/shard_map/send_maps/all_to_all | solution.py:575
  17.0 0.0 copy-done.1
  17.0 1.3 %collective-permute-start.2 = (bf16[1,128,512]{2,1,0:T(8,128)(2,1)S(1)}, bf16[1,128,512]{2,1,0:T(8,128)(2,1)S(1)}, u32[]{:S(2)}, u32[]{:S(2)}) collective-permute-start(bf16[1,128,512]{2,1,0:T(8,128)(2,1)S(1)} %copy-done.1), channel_id=1, source_target_pairs={{6,0},{0,2},{2,4},{4,6},{7,1},{1,3},{3,5},{5,7},{14,8},{8,10},{10,... | collective-permute-start | bytes 393224 | tf_op jit(solution)/shard_map/gather_grad/ppermute | solution.py:558
  18.2 2.5 %collective-permute-start.1 = (bf16[1,128,512]{2,1,0:T(8,128)(2,1)S(1)}, bf16[1,128,512]{2,1,0:T(8,128)(2,1)S(1)}, u32[]{:S(2)}, u32[]{:S(2)}) collective-permute-start(bf16[1,128,512]{2,1,0:T(8,128)(2,1)S(1)} %copy-done.1), channel_id=1, source_target_pairs={{4,0},{6,2},{0,4},{2,6},{5,1},{7,3},{1,5},{3,7},{12,8},{14,10},{8,... | collective-permute-start | bytes 393224 | tf_op jit(solution)/shard_map/gather_grad/ppermute | solution.py:558
  20.7 1.1 collective-permute-start
  21.8 0.1 pad_add_fusion.at_ref
  21.9 1.2 collective-permute-done.2.g3_ref
  23.1 3.8 %collective-permute-done.1.g2_ref = bf16[1,128,512]{2,1,0:T(8,128)(2,1)S(1)} collective-permute-done((bf16[1,128,512]{2,1,0:T(8,128)(2,1)S(1)}, bf16[1,128,512]{2,1,0:T(8,128)(2,1)S(1)}, u32[]{:S(2)}, u32[]{:S(2)}) %collective-permute-start.1) | collective-permute-done | bytes 131104 | tf_op jit(solution)/shard_map/gather_grad/ppermute | solution.py:558
  26.9 0.0 collective-permute-done.g1_ref
  26.9 0.0 collective-permute-done.3.other_ref
  26.9 3.6 %head_grads.1 = (bf16[16,64,128]{2,1,0:T(8,128)(2,1)}, bf16[128,1024]{1,0:T(8,128)(2,1)S(1)}) custom-call(s32[2]{0:T(128)S(1)} %pad_add_fusion.at_ref, bf16[1,128,512]{2,1,0:T(8,128)(2,1)S(1)} %copy-done.1, bf16[1,128,512]{2,1,0:T(8,128)(2,1)S(1)} %collective-permute-done.g1_ref, bf16[1,128,512]{2,1,0:T(8,128)(2,1)S(1)} %collective-permute-done.1.g2_ref, ...), custom_call_target="tpu_custom_call" | custom-call | flops 603979776 | bytes 5505032 | tf_op jit(solution)/shard_map/head_grads/pallas_call | solution.py:512
  30.5 0.0 copy-start
  30.5 0.0 copy-start.2
  30.5 0.0 all-to-all-done.maps_hbm
  30.6 3.8 %forward_chain.1 = bf16[16,128,128]{2,1,0:T(8,128)(2,1)} custom-call(s32[1]{0:T(128)} %bitcast.2.at_ref, bf16[16,192,128]{2,1,0:T(8,128)(2,1)} %all-to-all-done.maps_hbm, bf16[16,64,128]{2,1,0:T(8,128)(2,1)} %get-tuple-element.39.back_hbm, f32[16,64,128]{2,1,0:T(8,128)} %bitcast.7), custom_call_target="tpu_custom_call" | custom-call | flops 67108864 | bytes 2097156 | tf_op jit(solution)/shard_map/forward_chain/pallas_call | solution.py:512
  34.3 6.2 %all-to-all-start.1 = ((bf16[16,128,128]{2,1,0:T(8,128)(2,1)}), bf16[16,128,128]{2,1,0:T(8,128)(2,1)S(1)}, u32[]{:S(2)}, u32[]{:S(2)}) async-start(bf16[16,128,128]{2,1,0:T(8,128)(2,1)} %forward_chain.1), calls=%async_computation.1 | async-start | bytes 1048576 | tf_op jit(solution)/shard_map/return_states/all_to_all | solution.py:620
  40.5 0.8 grad_rows.1
  41.3 1.8 %collective-permute-start.4 = (bf16[1024,128]{1,0:T(8,128)(2,1)S(1)}, bf16[1024,128]{1,0:T(8,128)(2,1)S(1)}, u32[]{:S(2)}, u32[]{:S(2)}) collective-permute-start(bf16[1024,128]{1,0:T(8,128)(2,1)S(1)} %get-tuple-element.41), channel_id=1, source_target_pairs={{0,1},{1,0},{2,3},{3,2},{4,5},{5,4},{6,7},{7,6},{8,9},{9,8},{10,11... | collective-permute-start | bytes 786440 | tf_op jit(solution)/shard_map/grad_rows/ppermute | solution.py:600
  43.1 6.6 %all-to-all-done.1.y_ref.in_ref.refs_6_ = bf16[16,128,128]{2,1,0:T(8,128)(2,1)S(1)} async-done(((bf16[16,128,128]{2,1,0:T(8,128)(2,1)}), bf16[16,128,128]{2,1,0:T(8,128)(2,1)S(1)}, u32[]{:S(2)}, u32[]{:S(2)}) %all-to-all-start.1) | async-done | bytes 524320 | tf_op jit(solution)/shard_map/return_states/all_to_all | solution.py:620
  49.7 0.0 copy-done
  49.7 0.0 copy-done.2
  49.7 0.3 outputs.1.low_ref
  50.0 3.4 %collective-permute-start.5 = (bf16[128,1024]{1,0:T(8,128)(2,1)S(1)}, bf16[128,1024]{1,0:T(8,128)(2,1)S(1)}, u32[]{:S(2)}, u32[]{:S(2)}) collective-permute-start(bf16[128,1024]{1,0:T(8,128)(2,1)S(1)} %outputs.1.low_ref), channel_id=1, source_target_pairs={{0,1},{1,0},{2,3},{3,2},{4,5},{5,4},{6,7},{7,6},{8,9},{9,8},{10,11... | collective-permute-start | bytes 786440 | tf_op jit(solution)/shard_map/outputs/ppermute | solution.py:625
  53.4 3.7 %backward_chain.1.in_ref = bf16[16,64,1152]{2,1,0:T(8,128)(2,1)} custom-call(s32[1]{0:T(128)} %bitcast.2.at_ref, bf16[16,192,128]{2,1,0:T(8,128)(2,1)} %all-to-all-done.maps_hbm, bf16[16,128,128]{2,1,0:T(8,128)(2,1)S(1)} %all-to-all-done.1.y_ref.in_ref.refs_6_, f32[16,64,128]{2,1,0:T(8,128)} %bitcast.8), custom_call_target="tpu_custom_call" | custom-call | flops 67108864 | bytes 4194308 | tf_op jit(solution)/shard_map/backward_chain/pallas_call | solution.py:512
  57.1 0.0 collective-permute-done.4.theirs_ref
  57.1 0.0 collective-permute-done.5.other_ref
  57.1 1.6 %projection.3.refs_7_ = bf16[16,64,1152]{2,1,0:T(8,128)(2,1)} custom-call(bf16[1024,128]{1,0:T(8,128)(2,1)S(1)} %get-tuple-element.40.mine_ref, bf16[1024,128]{1,0:T(8,128)(2,1)S(1)} %collective-permute-done.4.theirs_ref, bf16[128,1024]{1,0:T(8,128)(2,1)S(1)} %outputs.1.low_ref, ...), custom_call_target="tpu_custom_call", output_to_operand_aliasing={{}: (4, {})} | custom-call | flops 536870912 | bytes 5767168 | tf_op jit(solution)/shard_map/projection/pallas_call | solution.py:512
  58.7 10.7 %gradients.3 = (bf16[1,128,512]{2,1,0:T(8,128)(2,1)}, f32[1,128,512]{2,1,0:T(8,128)}, f32[1,8,128]{2,1,0:T(8,128)}, f32[8,128,128]{2,1,0:T(8,128)}, bf16[8,128,1...) custom-call(s32[1]{0:T(128)} %bitcast.at_ref, ...), custom_call_target="tpu_custom_call", output_to_operand_aliasing={{8}: (8, {})} | custom-call | flops 1174405120 | bytes 8007684 | tf_op jit(solution)/shard_map/gradients/pallas_call | solution.py:512
  69.4 25.1 %all_to_all.20.pieces_ref = bf16[16,64,1152]{2,1,0:T(8,128)(2,1)S(1)} all-to-all(bf16[16,64,1152]{2,1,0:T(8,128)(2,1)} %get-tuple-element.43), channel_id=1, replica_groups=mesh['ctx'=16,'tp'=4,'dp'=2] {'ctx'}, dimensions={0} | all-to-all | bytes 4718592 | tf_op jit(solution)/shard_map/projection/all_to_all | solution.py:665
  94.5 1.8 %projection.4 = (bf16[16,64,1024]{2,1,0:T(8,128)(2,1)}, bf16[16,64,128]{2,1,0:T(8,128)(2,1)}) custom-call(bf16[16,64,1152]{2,1,0:T(8,128)(2,1)S(1)} %all_to_all.20.pieces_ref), custom_call_target="tpu_custom_call" | custom-call | bytes 4718592 | tf_op jit(solution)/shard_map/projection/pallas_call | solution.py:512
  96.3 3.7 %all-to-all-start.3 = ((bf16[16,64,1024]{2,1,0:T(8,128)(2,1)}), bf16[16,64,1024]{2,1,0:T(8,128)(2,1)S(1)}, u32[]{:S(2)}, u32[]{:S(2)}) async-start(bf16[16,64,1024]{2,1,0:T(8,128)(2,1)} %get-tuple-element.44.refs_7_), calls=%async_computation.3 | async-start | bytes 4194304 | tf_op jit(solution)/shard_map/projection/all_to_all | solution.py:671
  100.0 0.4 gradients.4
  100.4 7.7 %gradients.5 = (bf16[1,128,512]{2,1,0:T(8,128)(2,1)}, bf16[1,128,1024]{2,1,0:T(8,128)(2,1)}, f32[1,8,128]{2,1,0:T(8,128)}, f32[1,8,128]{2,1,0:T(8,128)}) custom-call(bf16[1,128,512]{2,1,0:T(8,128)(2,1)} %refs_0_.7, bf16[1,128,512]{2,1,0:T(8,128)(2,1)} %refs_1_.7, bf16[1,128,1024]{2,1,0:T(8,128)(2,1)} %refs_2_.7, f32[1,8,128]{2,1,0:T(8,128)} %refs_3_.7, ...), custom_call_target="tpu_custom_call" | custom-call | flops 1174405120 | bytes 3821568 | tf_op jit(solution)/shard_map/gradients/pallas_call | solution.py:512
  108.1 12.4 %all-to-all-done.3 = bf16[16,64,1024]{2,1,0:T(8,128)(2,1)S(1)} async-done(((bf16[16,64,1024]{2,1,0:T(8,128)(2,1)}), bf16[16,64,1024]{2,1,0:T(8,128)(2,1)S(1)}, u32[]{:S(2)}, u32[]{:S(2)}) %all-to-all-start.3) | async-done | bytes 2097184 | tf_op jit(solution)/shard_map/projection/all_to_all | solution.py:671
  120.5 2.1 %projection.5 = f32[1024,1024]{1,0:T(8,128)} custom-call(bf16[1024,1024]{1,0:T(8,128)(2,1)S(1)} %bitcast.6), custom_call_target="tpu_custom_call" | custom-call | bytes 6291456 | tf_op jit(solution)/shard_map/projection/pallas_call | solution.py:512
Async XLA Ops:
  0.6 16.3 %copy-start.1 = (bf16[1,128,512]{2,1,0:T(8,128)(2,1)S(1)}, bf16[1,128,512]{2,1,0:T(8,128)(2,1)}, u32[]{:S(2)}) copy-start(bf16[1,128,512]{2,1,0:T(8,128)(2,1)} %g0_ref.3) | copy-start | bytes 393220
  0.6 26.3 %collective-permute-start.3 = (bf16[1024,1024]{1,0:T(8,128)(2,1)}, bf16[1024,1024]{1,0:T(8,128)(2,1)S(1)}, u32[]{:S(2)}, u32[]{:S(2)}) collective-permute-start(bf16[1024,1024]{1,0:T(8,128)(2,1)} %own_hbm.1), channel_id=1, source_target_pairs={{0,1},{1,0},{2,3},{3,2},{4,5},{5,4},{6,7},{7,6},{8,9},{9,8},{10,11... | collective-permute-start | bytes 6291464 | tf_op jit(solution)/shard_map/other_rows/ppermute | solution.py:560
  9.0 21.5 %all-to-all-start = ((bf16[16,192,128]{2,1,0:T(8,128)(2,1)}), bf16[16,192,128]{2,1,0:T(8,128)(2,1)}, u32[]{:S(2)}, u32[]{:S(2)}) async-start(bf16[16,192,128]{2,1,0:T(8,128)(2,1)} %get-tuple-element.38), calls=%async_computation | async-start | bytes 1572864 | tf_op jit(solution)/shard_map/send_maps/all_to_all | solution.py:575
  17.0 6.2 %collective-permute-start.2 = (bf16[1,128,512]{2,1,0:T(8,128)(2,1)S(1)}, bf16[1,128,512]{2,1,0:T(8,128)(2,1)S(1)}, u32[]{:S(2)}, u32[]{:S(2)}) collective-permute-start(bf16[1,128,512]{2,1,0:T(8,128)(2,1)S(1)} %copy-done.1), channel_id=1, source_target_pairs={{6,0},{0,2},{2,4},{4,6},{7,1},{1,3},{3,5},{5,7},{14,8},{8,10},{10,... | collective-permute-start | bytes 393224 | tf_op jit(solution)/shard_map/gather_grad/ppermute | solution.py:558
  18.2 8.7 %collective-permute-start.1 = (bf16[1,128,512]{2,1,0:T(8,128)(2,1)S(1)}, bf16[1,128,512]{2,1,0:T(8,128)(2,1)S(1)}, u32[]{:S(2)}, u32[]{:S(2)}) collective-permute-start(bf16[1,128,512]{2,1,0:T(8,128)(2,1)S(1)} %copy-done.1), channel_id=1, source_target_pairs={{4,0},{6,2},{0,4},{2,6},{5,1},{7,3},{1,5},{3,7},{12,8},{14,10},{8,... | collective-permute-start | bytes 393224 | tf_op jit(solution)/shard_map/gather_grad/ppermute | solution.py:558
  20.7 6.2 %collective-permute-start = (bf16[1,128,512]{2,1,0:T(8,128)(2,1)S(1)}, bf16[1,128,512]{2,1,0:T(8,128)(2,1)S(1)}, u32[]{:S(2)}, u32[]{:S(2)}) collective-permute-start(bf16[1,128,512]{2,1,0:T(8,128)(2,1)S(1)} %copy-done.1), channel_id=1, source_target_pairs={{2,0},{4,2},{6,4},{0,6},{3,1},{5,3},{7,5},{1,7},{10,8},{12,10},{14... | collective-permute-start | bytes 393224 | tf_op jit(solution)/shard_map/gather_grad/ppermute | solution.py:558
  30.5 19.2 %copy-start = (bf16[8,128,128]{2,1,0:T(8,128)(2,1)S(1)}, bf16[8,128,128]{2,1,0:T(8,128)(2,1)}, u32[]{:S(2)}) copy-start(bf16[8,128,128]{2,1,0:T(8,128)(2,1)} %get-tuple-element.36.qe_hbm.qe_ref) | copy-start | bytes 786436
  30.5 19.1 %copy-start.2 = (bf16[8,128,128]{2,1,0:T(8,128)(2,1)S(1)}, bf16[8,128,128]{2,1,0:T(8,128)(2,1)}, u32[]{:S(2)}) copy-start(bf16[8,128,128]{2,1,0:T(8,128)(2,1)} %get-tuple-element.42.o0_ref) | copy-start | bytes 786436
  34.3 15.4 %all-to-all-start.1 = ((bf16[16,128,128]{2,1,0:T(8,128)(2,1)}), bf16[16,128,128]{2,1,0:T(8,128)(2,1)S(1)}, u32[]{:S(2)}, u32[]{:S(2)}) async-start(bf16[16,128,128]{2,1,0:T(8,128)(2,1)} %forward_chain.1), calls=%async_computation.1 | async-start | bytes 1048576 | tf_op jit(solution)/shard_map/return_states/all_to_all | solution.py:620
  41.3 15.8 %collective-permute-start.4 = (bf16[1024,128]{1,0:T(8,128)(2,1)S(1)}, bf16[1024,128]{1,0:T(8,128)(2,1)S(1)}, u32[]{:S(2)}, u32[]{:S(2)}) collective-permute-start(bf16[1024,128]{1,0:T(8,128)(2,1)S(1)} %get-tuple-element.41), channel_id=1, source_target_pairs={{0,1},{1,0},{2,3},{3,2},{4,5},{5,4},{6,7},{7,6},{8,9},{9,8},{10,11... | collective-permute-start | bytes 786440 | tf_op jit(solution)/shard_map/grad_rows/ppermute | solution.py:600
  50.0 7.1 %collective-permute-start.5 = (bf16[128,1024]{1,0:T(8,128)(2,1)S(1)}, bf16[128,1024]{1,0:T(8,128)(2,1)S(1)}, u32[]{:S(2)}, u32[]{:S(2)}) collective-permute-start(bf16[128,1024]{1,0:T(8,128)(2,1)S(1)} %outputs.1.low_ref), channel_id=1, source_target_pairs={{0,1},{1,0},{2,3},{3,2},{4,5},{5,4},{6,7},{7,6},{8,9},{9,8},{10,11... | collective-permute-start | bytes 786440 | tf_op jit(solution)/shard_map/outputs/ppermute | solution.py:625
  96.3 24.2 %all-to-all-start.3 = ((bf16[16,64,1024]{2,1,0:T(8,128)(2,1)}), bf16[16,64,1024]{2,1,0:T(8,128)(2,1)S(1)}, u32[]{:S(2)}, u32[]{:S(2)}) async-start(bf16[16,64,1024]{2,1,0:T(8,128)(2,1)} %get-tuple-element.44.refs_7_), calls=%async_computation.3 | async-start | bytes 4194304 | tf_op jit(solution)/shard_map/projection/all_to_all | solution.py:671
